TPU v7x, 32 devices: a whole 2x2x4 slice. The times are simulated.
32 devices in a mesh: grp: 4 (over y, x), seq: 8 (over z, core).
Axes of the slice: x: 2, y: 2, z: 4, core: 2. Of those that a mesh axis runs over, the one named last changes fastest.
Arguments:
- frames: bfloat16 [8, 1536, 1024], P('grp', 'seq'), may hold values from -6 to 6
- shortcut: bfloat16 [8, 1536, 1024], P('grp', 'seq'), may hold values from -6 to 6
- time_embed: float32 [8, 2, 1024], P('grp'), may hold values from -6 to 6
- lengths: int32 [8, 2], P('grp'), may hold values from 1 to 1024, 1536 in all within a row
- kept_mask: int32 [8, 1536], P('grp', 'seq'), may hold values from 0 to 1, as said below
- target: bfloat16 [8, 1536, 1024], P('grp', 'seq'), may hold values from -6 to 6
- combine: bfloat16 [2048, 1024], P('seq'), may hold values from -0.125 to 0.125
- modulation: bfloat16 [1024, 6144], P('seq'), may hold values from -0.1875 to 0.1875
- projection: bfloat16 [1024, 3072], P('seq'), may hold values from -0.1875 to 0.1875
- readout: bfloat16 [1024, 1024], P('seq'), may hold values from -2.5 to 2.5
- expand: bfloat16 [1024, 4096], P('seq'), may hold values from -0.1875 to 0.1875
- contract: bfloat16 [4096, 1024], P('seq'), may hold values from -0.09375 to 0.09375
Outputs:
- result: bfloat16 [8, 1536, 1024], P('grp', 'seq')
- frames_grad: float32 [8, 1536, 1024], P('grp', 'seq')
- shortcut_grad: float32 [8, 1536, 1024], P('grp', 'seq')
- time_grad: float32 [8, 2, 1024], P('grp')
- combine_grad: float32 [2048, 1024], P('seq')
- modulation_grad: float32 [1024, 6144], P('seq')
- projection_grad: float32 [1024, 3072], P('seq')
- readout_grad: float32 [1024, 1024], P('seq')
- expand_grad: float32 [1024, 4096], P('seq')
- contract_grad: float32 [4096, 1024], P('seq')
Inputs may be any that keep to these rules, and one draw needn't show every extreme that they name: Each group's 2 utterance lengths sum to 1536; utterances lie end to end in the order given. `kept_mask`: the last frame of every group is kept.
All inputs are finite; a program needn't handle non-finite values.
Results may differ from a plain program's by a relative error of at most 0.018.
The roundings to bfloat16 on the way count: a program that leaves them out, or rounds other values in their place, can miss the bound.
Values may be sent and summed in bfloat16 or wider, within the bound.
A program may use at most 320 MiB of HBM per device.

v0:
```python
import jax
import jax.numpy as jnp
from jax import lax
from jax.sharding import PartitionSpec as P

HEADS = 16
HEAD_DIM = 64


precise = lax.Precision.HIGHEST
epsilon = 1e-06
rope_base = 10000.0


def product(first_op, second_op):
    return jnp.dot(first_op, second_op, preferred_element_type=jnp.float32)


def product_left(first_op, second_op):
    return lax.dot_general(
        first_op, second_op, (((0,), (0,)), ((), ())), preferred_element_type=jnp.float32
    )


def product_right(first_op, second_op):
    return lax.dot_general(
        first_op, second_op, (((1,), (1,)), ((), ())), preferred_element_type=jnp.float32
    )


def gelu_tanh(values):
    return jax.nn.gelu(values, approximate=True)


def modulate(hidden, shift_part, scale_part):
    center = hidden - jnp.mean(hidden, axis=-1, keepdims=True)
    variance = jnp.mean(center * center, axis=-1, keepdims=True)
    return center * lax.rsqrt(variance + epsilon) * (1.0 + scale_part) + shift_part


def segment_info(lengths, frame_index):
    utter_count = lengths.shape[0]
    utter_ends = jnp.cumsum(lengths)
    starts = utter_ends - lengths
    segment = jnp.sum((frame_index[:, None] >= utter_ends[None, :]).astype(jnp.int32), axis=1)
    member = segment[:, None] == jnp.arange(utter_count, dtype=jnp.int32)[None, :]
    offset = jnp.sum(jnp.where(member, starts[None, :], 0), axis=1)
    return (segment, member, frame_index - offset)


def rotary_tables(position):
    half_dim = HEAD_DIM // 2
    ladder = jnp.arange(half_dim, dtype=jnp.float32) / half_dim
    inverse = jnp.exp(-jnp.log(rope_base) * ladder)
    angles = position.astype(jnp.float32)[:, None] * inverse[None, :]
    return (jnp.cos(angles)[:, None, :], jnp.sin(angles)[:, None, :])


def rotate(vectors, cos_table, sin_table):
    half_dim = vectors.shape[-1] // 2
    front_half = vectors[..., :half_dim]
    back_half = vectors[..., half_dim:]
    return jnp.concatenate(
        [
            front_half * cos_table - back_half * sin_table,
            back_half * cos_table + front_half * sin_table,
        ],
        axis=-1,
    )


def masked_scores(query_block, key_all, segment_block, segment_all):
    raw_scores = jnp.einsum(
        "qhd,khd->hqk", query_block, key_all, preferred_element_type=jnp.float32
    )
    same_utter = segment_block[:, None] == segment_all[None, :]
    return jnp.where(same_utter[None, :, :], raw_scores * HEAD_DIM ** (-0.5), -1e30)


def attend_forward(query_heads, key_heads, value_heads, segment_all):
    total_rows = query_heads.shape[0]
    local_width = query_heads.shape[1]
    local_heads = local_width // HEAD_DIM
    head_shape = (total_rows, local_heads, HEAD_DIM)
    queries = query_heads.reshape(head_shape)
    key_all = key_heads.reshape(head_shape)
    value_all = value_heads.reshape(head_shape)
    block_rows = min(512, total_rows)
    blocks = total_rows // block_rows

    def one_block(block_index):
        first_row = block_index * block_rows
        query_block = lax.dynamic_slice_in_dim(queries, first_row, block_rows, 0)
        segment_block = lax.dynamic_slice_in_dim(segment_all, first_row, block_rows, 0)
        scores = masked_scores(query_block, key_all, segment_block, segment_all)
        row_peak = jnp.max(scores, axis=-1, keepdims=True)
        lifted = jnp.exp(scores - row_peak)
        row_total = jnp.sum(lifted, axis=-1, keepdims=True)
        attn_weight = (lifted / row_total).astype(jnp.bfloat16)
        mixture = jnp.einsum(
            "hqk,khd->qhd", attn_weight, value_all, preferred_element_type=jnp.float32
        )
        log_block = (row_peak + jnp.log(row_total))[..., 0]
        return (mixture.astype(jnp.bfloat16).reshape(block_rows, local_width), log_block)

    mixture, log_total = lax.map(one_block, jnp.arange(blocks, dtype=jnp.int32))
    return (mixture.reshape(total_rows, local_width), log_total)


def attend_backward(query_heads, key_heads, value_heads, mixture_grad, log_total, segment_all):
    total_rows = query_heads.shape[0]
    local_width = query_heads.shape[1]
    local_heads = local_width // HEAD_DIM
    head_shape = (total_rows, local_heads, HEAD_DIM)
    queries = query_heads.reshape(head_shape)
    key_all = key_heads.reshape(head_shape)
    value_all = value_heads.reshape(head_shape)
    grad_all = mixture_grad.reshape(head_shape)
    block_rows = min(512, total_rows)
    blocks = total_rows // block_rows

    def one_block(running, block_items):
        block_index, log_block = block_items
        key_sum, value_sum = running
        first_row = block_index * block_rows
        query_block = lax.dynamic_slice_in_dim(queries, first_row, block_rows, 0)
        grad_block = lax.dynamic_slice_in_dim(grad_all, first_row, block_rows, 0)
        segment_block = lax.dynamic_slice_in_dim(segment_all, first_row, block_rows, 0)
        scores = masked_scores(query_block, key_all, segment_block, segment_all)
        attn_prob = jnp.exp(scores - log_block[..., None])
        weight_grad = jnp.einsum(
            "qhd,khd->hqk", grad_block, value_all, preferred_element_type=jnp.float32
        )
        row_dot = jnp.sum(attn_prob * weight_grad, axis=-1, keepdims=True)
        score_grad = (HEAD_DIM ** (-0.5) * attn_prob * (weight_grad - row_dot)).astype(jnp.bfloat16)
        query_grad = jnp.einsum(
            "hqk,khd->qhd", score_grad, key_all, preferred_element_type=jnp.float32
        )
        key_sum = key_sum + jnp.einsum(
            "hqk,qhd->khd", score_grad, query_block, preferred_element_type=jnp.float32
        )
        value_sum = value_sum + jnp.einsum(
            "hqk,qhd->khd",
            attn_prob.astype(jnp.bfloat16),
            grad_block,
            preferred_element_type=jnp.float32,
        )
        return ((key_sum, value_sum), query_grad.astype(jnp.bfloat16))

    zero_start = jnp.zeros(head_shape, jnp.float32)
    sums, query_grad = lax.scan(
        one_block, (zero_start, zero_start), (jnp.arange(blocks, dtype=jnp.int32), log_total)
    )
    return (
        query_grad.reshape(total_rows, local_width),
        sums[0].astype(jnp.bfloat16).reshape(total_rows, local_width),
        sums[1].astype(jnp.bfloat16).reshape(total_rows, local_width),
    )


def shards(
    frames,
    shortcut,
    time_embed,
    lengths,
    kept_mask,
    target,
    combine,
    modulation,
    projection,
    readout,
    expand,
    contract,
):
    gathered = (
        lax.all_gather(combine, "seq", axis=0, tiled=True),
        lax.all_gather(modulation, "seq", axis=0, tiled=True),
        lax.all_gather(projection, "seq", axis=0, tiled=True),
        lax.all_gather(readout, "seq", axis=0, tiled=True),
        lax.all_gather(expand, "seq", axis=0, tiled=True),
        lax.all_gather(contract, "seq", axis=0, tiled=True),
    )
    combine_full, modulation_full, projection_full, readout_full, expand_full, contract_full = (
        gathered
    )
    group_count = frames.shape[0]
    local_rows = frames.shape[1]
    width = HEADS * HEAD_DIM
    row_count = group_count * local_rows
    seq_count = lax.axis_size("seq")
    group_frames = local_rows * seq_count
    all_frames = group_frames * lax.axis_size("grp") * group_count
    utter_count = time_embed.shape[1]
    kept_float = kept_mask.astype(jnp.float32).reshape(row_count)
    kept_total = lax.psum(jnp.sum(kept_float), ("grp", "seq"))
    local_index = lax.axis_index("seq") * local_rows + jnp.arange(local_rows, dtype=jnp.int32)
    frame_order = jnp.arange(group_frames, dtype=jnp.int32)

    def local_info(length_row):
        return segment_info(length_row, local_index)

    def whole_segment(length_row):
        return segment_info(length_row, frame_order)[0]

    member_info = jax.vmap(local_info)(lengths)
    member_float = member_info[1].astype(jnp.float32)
    position = member_info[2]
    segment_all = jax.vmap(whole_segment)(lengths)
    cos_table, sin_table = rotary_tables(position.reshape(row_count))
    joined = jnp.concatenate([frames, shortcut], axis=2).reshape(row_count, 2 * width)
    hidden = product(joined, combine_full)
    silu_value, silu_pull = jax.vjp(jax.nn.silu, time_embed)
    condition = silu_value.astype(jnp.bfloat16)
    modulation_utter = product(
        condition.reshape(group_count * utter_count, width), modulation_full
    ).reshape(group_count, utter_count, 6 * width)
    modulation_frame = jnp.einsum(
        "gtu,gue->gte",
        member_float,
        modulation_utter,
        precision=precise,
        preferred_element_type=jnp.float32,
    ).reshape(row_count, 6 * width)
    shift_first, scale_first, gate_first, shift_second, scale_second, gate_second = jnp.split(
        modulation_frame, 6, axis=1
    )
    normed_value, first_pull = jax.vjp(modulate, hidden, shift_first, scale_first)
    normed = normed_value.astype(jnp.bfloat16)
    packed = product(normed, projection_full)
    query_raw, key_raw, value_raw = jnp.split(packed, 3, axis=1)
    head_shape = (row_count, HEADS, HEAD_DIM)
    split_shape = (group_count, local_rows, width)

    def rotate_local(vectors):
        return rotate(vectors, cos_table, sin_table)

    query_turned, query_pull = jax.vjp(rotate_local, query_raw.reshape(head_shape))
    key_turned, key_pull = jax.vjp(rotate_local, key_raw.reshape(head_shape))
    query_low = query_turned.reshape(split_shape).astype(jnp.bfloat16)
    key_low = key_turned.reshape(split_shape).astype(jnp.bfloat16)
    value_low = value_raw.reshape(split_shape).astype(jnp.bfloat16)
    query_heads, key_heads, value_heads = (
        lax.all_to_all(query_low, "seq", split_axis=2, concat_axis=1, tiled=True),
        lax.all_to_all(key_low, "seq", split_axis=2, concat_axis=1, tiled=True),
        lax.all_to_all(value_low, "seq", split_axis=2, concat_axis=1, tiled=True),
    )
    mixture_list = []
    log_list = []
    for group_slot in range(group_count):
        mixture_one, log_one = attend_forward(
            query_heads[group_slot],
            key_heads[group_slot],
            value_heads[group_slot],
            segment_all[group_slot],
        )
        mixture_list.append(mixture_one)
        log_list.append(log_one)
    mixture_heads = jnp.stack(mixture_list)
    mixture = lax.all_to_all(mixture_heads, "seq", split_axis=1, concat_axis=2, tiled=True).reshape(
        row_count, width
    )
    branch = product(mixture, readout_full)
    middle = hidden + gate_first * branch
    second_value, second_pull = jax.vjp(modulate, middle, shift_second, scale_second)
    normed_second = second_value.astype(jnp.bfloat16)
    expanded = product(normed_second, expand_full)
    active_value, gelu_pull = jax.vjp(gelu_tanh, expanded)
    active = active_value.astype(jnp.bfloat16)
    contracted = product(active, contract_full)
    output = middle + gate_second * contracted
    loss_scale = all_frames / kept_total
    output_grad = (
        loss_scale
        * kept_float[:, None]
        * (output - target.reshape(row_count, width).astype(jnp.float32))
    )
    combine_back, modulation_back, projection_back, readout_back, expand_back, contract_back = (
        gathered
    )
    gate_second_grad = output_grad * contracted
    contracted_grad = (gate_second * output_grad).astype(jnp.bfloat16)
    contract_part = product_left(active, contracted_grad)
    active_grad = product_right(contracted_grad, contract_back)
    expanded_grad = gelu_pull(active_grad)[0].astype(jnp.bfloat16)
    expand_part = product_left(normed_second, expanded_grad)
    normed_second_grad = product_right(expanded_grad, expand_back)
    middle_extra, shift_second_grad, scale_second_grad = second_pull(normed_second_grad)
    middle_grad = output_grad + middle_extra
    gate_first_grad = middle_grad * branch
    branch_grad = (gate_first * middle_grad).astype(jnp.bfloat16)
    readout_part = product_left(mixture, branch_grad)
    mixture_grad = product_right(branch_grad, readout_back).astype(jnp.bfloat16)
    mixture_grad_heads = lax.all_to_all(
        mixture_grad.reshape(split_shape), "seq", split_axis=2, concat_axis=1, tiled=True
    )
    query_list = []
    key_list = []
    value_list = []
    for group_slot in range(group_count):
        query_one, key_one, value_one = attend_backward(
            query_heads[group_slot],
            key_heads[group_slot],
            value_heads[group_slot],
            mixture_grad_heads[group_slot],
            log_list[group_slot],
            segment_all[group_slot],
        )
        query_list.append(query_one)
        key_list.append(key_one)
        value_list.append(value_one)
    query_back, key_back, value_back = (
        lax.all_to_all(jnp.stack(query_list), "seq", split_axis=1, concat_axis=2, tiled=True),
        lax.all_to_all(jnp.stack(key_list), "seq", split_axis=1, concat_axis=2, tiled=True),
        lax.all_to_all(jnp.stack(value_list), "seq", split_axis=1, concat_axis=2, tiled=True),
    )
    query_unturned = query_pull(query_back.reshape(head_shape).astype(jnp.float32))[0].reshape(
        row_count, width
    )
    key_unturned = key_pull(key_back.reshape(head_shape).astype(jnp.float32))[0].reshape(
        row_count, width
    )
    packed_grad = jnp.concatenate(
        [
            query_unturned.astype(jnp.bfloat16),
            key_unturned.astype(jnp.bfloat16),
            value_back.reshape(row_count, width),
        ],
        axis=1,
    )
    projection_part = product_left(normed, packed_grad)
    normed_grad = product_right(packed_grad, projection_back)
    hidden_extra, shift_first_grad, scale_first_grad = first_pull(normed_grad)
    hidden_grad = (middle_grad + hidden_extra).astype(jnp.bfloat16)
    combine_part = product_left(joined, hidden_grad)
    joined_grad = product_right(hidden_grad, combine_back)
    frames_grad = joined_grad[:, :width].reshape(split_shape)
    shortcut_grad = joined_grad[:, width:].reshape(split_shape)
    modulation_frame_grad = jnp.concatenate(
        [
            shift_first_grad,
            scale_first_grad,
            gate_first_grad,
            shift_second_grad,
            scale_second_grad,
            gate_second_grad,
        ],
        axis=1,
    )
    utter_part = jnp.einsum(
        "gtu,gte->gue",
        member_float,
        modulation_frame_grad.reshape(group_count, local_rows, 6 * width),
        precision=precise,
        preferred_element_type=jnp.float32,
    )
    utter_grad = lax.psum(utter_part.astype(jnp.bfloat16), "seq")
    utter_rows = utter_grad.reshape(group_count * utter_count, 6 * width)
    condition_grad = product_right(utter_rows, modulation_back).reshape(
        group_count, utter_count, width
    )
    time_grad = silu_pull(condition_grad)[0]
    shard_rows = modulation.shape[0]
    condition_part = lax.dynamic_slice_in_dim(
        condition, lax.axis_index("seq") * shard_rows, shard_rows, 2
    ).reshape(group_count * utter_count, shard_rows)
    modulation_part = product_left(condition_part, utter_rows)
    scattered = (
        lax.psum_scatter(
            combine_part.astype(jnp.bfloat16), "seq", scatter_dimension=0, tiled=True
        ).astype(jnp.float32),
        lax.psum_scatter(
            projection_part.astype(jnp.bfloat16), "seq", scatter_dimension=0, tiled=True
        ).astype(jnp.float32),
        lax.psum_scatter(
            readout_part.astype(jnp.bfloat16), "seq", scatter_dimension=0, tiled=True
        ).astype(jnp.float32),
        lax.psum_scatter(
            expand_part.astype(jnp.bfloat16), "seq", scatter_dimension=0, tiled=True
        ).astype(jnp.float32),
        lax.psum_scatter(
            contract_part.astype(jnp.bfloat16), "seq", scatter_dimension=0, tiled=True
        ).astype(jnp.float32),
    )
    summed = (
        lax.psum(scattered[0].astype(jnp.bfloat16), "grp").astype(jnp.float32),
        lax.psum(modulation_part.astype(jnp.bfloat16), "grp").astype(jnp.float32),
        lax.psum(scattered[1].astype(jnp.bfloat16), "grp").astype(jnp.float32),
        lax.psum(scattered[2].astype(jnp.bfloat16), "grp").astype(jnp.float32),
        lax.psum(scattered[3].astype(jnp.bfloat16), "grp").astype(jnp.float32),
        lax.psum(scattered[4].astype(jnp.bfloat16), "grp").astype(jnp.float32),
    )
    return (
        output.astype(jnp.bfloat16).reshape(split_shape),
        frames_grad,
        shortcut_grad,
        time_grad,
        summed[0],
        summed[1],
        summed[2],
        summed[3],
        summed[4],
        summed[5],
    )


def solution(mesh):
    return jax.shard_map(
        shards,
        mesh=mesh,
        in_specs=(
            P("grp", "seq", None),
            P("grp", "seq", None),
            P("grp", None, None),
            P("grp", None),
            P("grp", "seq"),
            P("grp", "seq", None),
            P("seq", None),
            P("seq", None),
            P("seq", None),
            P("seq", None),
            P("seq", None),
            P("seq", None),
        ),
        out_specs=(
            P("grp", "seq", None),
            P("grp", "seq", None),
            P("grp", "seq", None),
            P("grp", None, None),
            P("seq", None),
            P("seq", None),
            P("seq", None),
            P("seq", None),
            P("seq", None),
            P("seq", None),
        ),
        check_vma=False,
    )
```

profile of v0, /device:TPU:0, one launch (start us, length us, event | category | flops | bytes accessed | tf_op | source)
XLA Modules:
  0.0 1312.1 jit_solution(11178994237697151347)
XLA Ops:
  12.2 47.4 %all-gather.7.cloned.1.call-done = bf16[2048,1024]{1,0:T(8,128)(2,1)} async-done(((bf16[256,1024]{1,0:T(8,128)(2,1)}), bf16[2048,1024]{1,0:T(8,128)(2,1)}) %all-gather.7.cloned.1.call-update) | async-done | bytes 4194320 | tf_op jit(solution)/shard_map/all_gather | solution.py:176
  59.6 4.1 fusion.108
  64.0 112.7 %all-gather.9.cloned.1.call-done = bf16[1024,6144]{1,0:T(8,128)(2,1)} async-done(((bf16[128,6144]{1,0:T(8,128)(2,1)}), bf16[1024,6144]{1,0:T(8,128)(2,1)}) %all-gather.9.cloned.1.call-update) | async-done | bytes 12582928 | tf_op jit(solution)/shard_map/all_gather | solution.py:177
  176.7 6.4 fusion.60
  183.1 4.0 fusion.87
  187.1 3.6 copy-done.4
  191.1 50.3 %all-gather.11.cloned.1.call-done = bf16[1024,3072]{1,0:T(8,128)(2,1)} async-done(((bf16[128,3072]{1,0:T(8,128)(2,1)}), bf16[1024,3072]{1,0:T(8,128)(2,1)}) %all-gather.11.cloned.1.call-update) | async-done | bytes 6291472 | tf_op jit(solution)/shard_map/all_gather | solution.py:178
  241.4 4.7 fusion.109
  254.8 4.0 all-to-all-start.1
  260.5 31.6 %all-to-all-done.1 = bf16[2,192,1024]{1,0,2:T(2,128)(2,1)S(1)} async-done(((bf16[2,192,1024]{1,0,2:T(2,128)(2,1)}), bf16[2,192,1024]{1,0,2:T(2,128)(2,1)S(1)}, u32[]{:S(2)}, u32[]{:S(2)}) %all-to-all-start.1) | async-done | bytes 786464 | tf_op jit(solution)/shard_map/all_to_all | solution.py:244
  292.1 3.6 all-to-all-start
  299.2 51.4 %all-to-all-done = bf16[2,192,1024]{1,0,2:T(2,128)(2,1)S(1)} async-done(((bf16[2,192,1024]{1,0,2:T(2,128)(2,1)}), bf16[2,192,1024]{1,0,2:T(2,128)(2,1)S(1)}, u32[]{:S(2)}, u32[]{:S(2)}) %all-to-all-start) | async-done | bytes 786464 | tf_op jit(solution)/shard_map/all_to_all | solution.py:243
  350.6 3.6 all-to-all-start.2
  363.8 37.4 %all-to-all-done.2 = bf16[2,192,1024]{1,0,2:T(2,128)(2,1)S(1)} async-done(((bf16[2,192,1024]{1,0,2:T(2,128)(2,1)}), bf16[2,192,1024]{1,0,2:T(2,128)(2,1)S(1)}, u32[]{:S(2)}, u32[]{:S(2)}) %all-to-all-start.2) | async-done | bytes 786464 | tf_op jit(solution)/shard_map/all_to_all | solution.py:245
  404.7 25.0 %while.54 = (s32[]{:T(128)}, bf16[3,512,128]{2,1,0:T(8,128)(2,1)S(1)}, f32[3,2,512]{2,1,0:T(2,128)S(1)}, s32[3]{0:T(128)S(1)}, s32[1536]{0:T(1024)}, /*index=5*/...) while((s32[]{:T(128)}, ...), condition=%wide.region_9.10_spmd, body=%wide.region_6.9_spmd.sunk | while | flops 422378496 | bytes 23650508 | solution.py:106
  433.3 24.8 %while.55 = (s32[]{:T(128)}, bf16[3,512,128]{2,1,0:T(8,128)(2,1)S(1)}, f32[3,2,512]{2,1,0:T(2,128)S(1)}, s32[3]{0:T(128)S(1)}, s32[1536]{0:T(1024)}, /*index=5*/...) while((s32[]{:T(128)}, ...), condition=%wide.region_13.14_spmd, body=%wide.region_10.13_spmd.sunk | while | flops 422378496 | bytes 23650508 | solution.py:106
  460.2 7.3 copy.117
  467.5 4.2 all-to-all-start.3
  472.3 53.3 %psum.56 = f32[]{:T(128)} all-reduce(f32[]{:T(128)} %convert_reduce_fusion), channel_id=1, replica_groups=mesh['grp'=4,'seq'=8] {'grp','seq'}, use_global_device_ids=true, to_apply=%region_17.18 | all-reduce | flops 1 | bytes 8 | tf_op jit(solution)/shard_map/psum | solution.py:195
  529.5 4.4 fusion.101
  536.8 8.9 fusion.110
  545.8 11.5 multiply_convert_fusion.4
  558.1 10.3 fusion.69
  568.5 7.6 multiply_reduce_fusion.3
  582.4 3.6 all-to-all-start.4
  586.1 26.6 %all-to-all-done.4 = bf16[2,192,1024]{1,0,2:T(2,128)(2,1)S(1)} async-done(((bf16[2,192,1024]{1,0,2:T(2,128)(2,1)}), bf16[2,192,1024]{1,0,2:T(2,128)(2,1)S(1)}, u32[]{:S(2)}, u32[]{:S(2)}) %all-to-all-start.4) | async-done | bytes 786464 | tf_op jit(solution)/shard_map/all_to_all | solution.py:293
  616.8 67.2 %while.56 = (s32[]{:T(128)}, f32[1536,2,64]{0,2,1:T(8,128)}, f32[1536,2,64]{0,2,1:T(8,128)}, bf16[3,512,2,64]{1,3,2,0:T(8,128)(2,1)}, s32[3]{0:T(128)S(1)}, /*in...) while((s32[]{:T(128)}, f32[1536,2,64]{0,2,1:T(8,128)}, ...), condition=%wide.region_22.23_spmd.clone, body=%wide.region_20.22_spmd.clone.sunk | while | flops 1023998976 | bytes 127710296 | solution.py:151
  618.0 3.7 fusion.210
  623.7 4.7 multiply_reduce_fusion.8
  640.1 3.7 fusion.210
  645.7 4.7 multiply_reduce_fusion.8
  662.7 3.7 fusion.210
  668.3 4.7 multiply_reduce_fusion.8
  688.7 67.4 %while.57 = (s32[]{:T(128)}, f32[1536,2,64]{0,2,1:T(8,128)}, f32[1536,2,64]{0,2,1:T(8,128)}, bf16[3,512,2,64]{1,3,2,0:T(8,128)(2,1)}, s32[3]{0:T(128)S(1)}, /*in...) while((s32[]{:T(128)}, f32[1536,2,64]{0,2,1:T(8,128)}, ...), condition=%wide.region_25.26_spmd.clone, body=%wide.region_23.25_spmd.clone.sunk | while | flops 1023998976 | bytes 127710136 | solution.py:151
  690.2 3.7 fusion.223
  695.9 4.7 multiply_reduce_fusion.9
  712.2 3.7 fusion.223
  717.9 4.7 multiply_reduce_fusion.9
  734.8 3.7 fusion.223
  740.5 4.7 multiply_reduce_fusion.9
  760.2 3.5 all-to-all-start.6
  767.5 17.2 %all-to-all-done.6 = bf16[2,1536,128]{2,0,1:T(2,128)(2,1)S(1)} async-done(((bf16[2,1536,128]{2,0,1:T(2,128)(2,1)}), bf16[2,1536,128]{2,0,1:T(2,128)(2,1)S(1)}, u32[]{:S(2)}, u32[]{:S(2)}) %all-to-all-start.6) | async-done | bytes 786464 | tf_op jit(solution)/shard_map/all_to_all | solution.py:313
  784.7 3.5 all-to-all-start.5
  794.7 14.5 %all-to-all-done.5 = bf16[2,1536,128]{2,0,1:T(2,128)(2,1)S(1)} async-done(((bf16[2,1536,128]{2,0,1:T(2,128)(2,1)}), bf16[2,1536,128]{2,0,1:T(2,128)(2,1)S(1)}, u32[]{:S(2)}, u32[]{:S(2)}) %all-to-all-start.5) | async-done | bytes 786464 | tf_op jit(solution)/shard_map/all_to_all | solution.py:312
  809.1 4.2 all-to-all-start.7
  813.4 3.7 convolution_convert_fusion.7
  831.3 8.3 all-to-all-done.7
  841.7 3.6 copy.139
  845.4 3.7 reshape.435
  851.2 7.3 constant_dynamic-update-slice_fusion.3
  858.6 3.4 fusion.98
  864.3 4.4 convolution_convert_fusion.6
  869.9 8.3 convolution_convert_fusion.5
  879.3 10.9 convolution_convert_fusion.2
  891.4 8.7 convolution_convert_fusion.3
  906.7 6.9 convolution_convert_fusion.4
  913.6 27.7 %psum.57 = bf16[2,2,6144]{2,1,0:T(2,128)(2,1)S(1)} all-reduce(bf16[2,2,6144]{2,1,0:T(2,128)(2,1)S(1)} %convolution_convert_fusion.4), channel_id=1, replica_groups=mesh['grp'=4,'seq'=8] {'seq'}, use_global_device_ids=true, to_apply=%region_28.29 | all-reduce | flops 24576 | bytes 98304 | tf_op jit(solution)/shard_map/psum | solution.py:356
  943.8 45.0 %reduce-scatter.8.cloned.1.call-done = bf16[128,3072]{1,0:T(8,128)(2,1)} async-done(((bf16[1024,3072]{1,0:T(8,128)(2,1)}), bf16[128,3072]{1,0:T(8,128)(2,1)}) %reduce-scatter.8.cloned.1.call-update) | async-done | bytes 786448 | tf_op jit(solution)/shard_map/reduce_scatter | solution.py:371
  988.8 89.8 %reduce-scatter.14.cloned.1.call-done = bf16[512,1024]{1,0:T(8,128)(2,1)} async-done(((bf16[4096,1024]{1,0:T(8,128)(2,1)}), bf16[512,1024]{1,0:T(8,128)(2,1)}) %reduce-scatter.14.cloned.1.call-update) | async-done | bytes 1048592 | tf_op jit(solution)/shard_map/reduce_scatter | solution.py:380
  1078.6 90.3 %reduce-scatter.12.cloned.1.call-done = bf16[128,4096]{1,0:T(8,128)(2,1)} async-done(((bf16[1024,4096]{1,0:T(8,128)(2,1)}), bf16[128,4096]{1,0:T(8,128)(2,1)}) %reduce-scatter.12.cloned.1.call-update) | async-done | bytes 1048592 | tf_op jit(solution)/shard_map/reduce_scatter | solution.py:377
  1168.9 4.0 fusion.111
  1174.9 9.5 fusion.83
  1184.4 110.9 %all-reduce.7.cloned.1.call-done = (bf16[256,1024]{1,0:T(8,128)(2,1)}, bf16[128,6144]{1,0:T(8,128)(2,1)}, bf16[128,3072]{1,0:T(8,128)(2,1)}, bf16[128,1024]{1,0:...) async-done(((bf16[256,1024]{1,0:T(8,128)(2,1)}, bf16[128,6144]{1,0:T(8,128)(2,1)}, bf16[128,3072]{1,0:T(8,128)(2,1)}, bf16[128,1024]{1,0:T(8,128)(2,1)}, ...) | async-done | bytes 5242896 | tf_op jit(solution)/shard_map/psum | solution.py:385
  1295.2 3.5 convert_element_type.247
  (530 shorter events, 241.8 us)
Async XLA Ops:
  7.2 52.4 %all-gather.7.cloned.1.call-start = ((), (), s32[]{:S(2)}) async-start(), calls=%async_computation.13 | async-start | bytes 4718592 | tf_op jit(solution)/shard_map/all_gather | solution.py:176
  8.0 168.7 %all-gather.9.cloned.1.call-start = ((), (), s32[]{:S(2)}) async-start(), calls=%async_computation.14 | async-start | bytes 14155776 | tf_op jit(solution)/shard_map/all_gather | solution.py:177
  8.7 232.7 %all-gather.11.cloned.1.call-start = ((), (), s32[]{:S(2)}) async-start(), calls=%async_computation.15 | async-start | bytes 7077888 | tf_op jit(solution)/shard_map/all_gather | solution.py:178
  9.4 520.1 %all-gather.13.cloned.1.call-start = ((), (), s32[]{:S(2)}) async-start(), calls=%async_computation.16 | async-start | bytes 2359296 | tf_op jit(solution)/shard_map/all_gather | solution.py:179
  10.0 526.8 %all-gather.15.cloned.1.call-start = ((), (), s32[]{:S(2)}) async-start(), calls=%async_computation.17 | async-start | bytes 9437184 | tf_op jit(solution)/shard_map/all_gather | solution.py:180
  10.9 172.2 %copy-start.70 = (s32[2,192]{1,0:T(2,128)}, s32[2,192]{1,0:T(2,128)S(1)}, u32[]{:S(2)}) copy-start(s32[2,192]{1,0:T(2,128)S(1)} %fusion.86) | copy-start | bytes 4612
  11.1 165.6 %copy-start.72 = (bf16[2,2,1024]{2,1,0:T(2,128)(2,1)}, bf16[2,2,1024]{2,1,0:T(2,128)(2,1)S(1)}, u32[]{:S(2)}) copy-start(bf16[2,2,1024]{2,1,0:T(2,128)(2,1)S(1)} %multiply_convert_fusion.5) | copy-start | bytes 24580
  12.2 51.4 %copy-start.35 = (bf16[2,192,2048]{2,1,0:T(8,128)(2,1)}, bf16[2,192,2048]{2,1,0:T(8,128)(2,1)S(1)}, u32[]{:S(2)}) copy-start(bf16[2,192,2048]{2,1,0:T(8,128)(2,1)S(1)} %pad_maximum_fusion.1) | copy-start | bytes 4718596
  63.6 123.5 %copy-start.9 = (f32[384,1024]{1,0:T(8,128)}, f32[384,1024]{1,0:T(8,128)S(1)}, u32[]{:S(2)}) copy-start(f32[384,1024]{1,0:T(8,128)S(1)} %get-tuple-element.467) | copy-start | bytes 4718596
  63.7 123.5 %copy-start.73 = (f32[384]{0:T(512)}, f32[384]{0:T(512)S(1)}, u32[]{:S(2)}) copy-start(f32[384]{0:T(512)S(1)} %broadcast_multiply_fusion.1) | copy-start | bytes 4612
  64.0 119.1 %copy-start.80 = (f32[384]{0:T(512)}, f32[384]{0:T(512)S(1)}, u32[]{:S(2)}) copy-start(f32[384]{0:T(512)S(1)} %multiply_reduce_fusion.5) | copy-start | bytes 4612
  64.0 123.1 %copy-start.78 = (f32[384]{0:T(512)}, f32[384]{0:T(512)S(1)}, u32[]{:S(2)}) copy-start(f32[384]{0:T(512)S(1)} %fusion.90) | copy-start | bytes 4612
  191.1 50.3 %copy-start.48 = (bf16[384,1024]{1,0:T(8,128)(2,1)}, bf16[384,1024]{1,0:T(8,128)(2,1)S(1)}, u32[]{:S(2)}) copy-start(bf16[384,1024]{1,0:T(8,128)(2,1)S(1)} %fusion.71) | copy-start | bytes 2359300
  254.8 37.3 %all-to-all-start.1 = ((bf16[2,192,1024]{1,0,2:T(2,128)(2,1)}), bf16[2,192,1024]{1,0,2:T(2,128)(2,1)S(1)}, u32[]{:S(2)}, u32[]{:S(2)}) async-start(bf16[2,192,1024]{1,0,2:T(2,128)(2,1)} %convert_element_type.214), calls=%async_computation.1 | async-start | bytes 2097152 | tf_op jit(solution)/shard_map/all_to_all | solution.py:244
  292.1 58.5 %all-to-all-start = ((bf16[2,192,1024]{1,0,2:T(2,128)(2,1)}), bf16[2,192,1024]{1,0,2:T(2,128)(2,1)S(1)}, u32[]{:S(2)}, u32[]{:S(2)}) async-start(bf16[2,192,1024]{1,0,2:T(2,128)(2,1)} %convert_element_type.213), calls=%async_computation | async-start | bytes 2097152 | tf_op jit(solution)/shard_map/all_to_all | solution.py:243
  350.6 50.6 %all-to-all-start.2 = ((bf16[2,192,1024]{1,0,2:T(2,128)(2,1)}), bf16[2,192,1024]{1,0,2:T(2,128)(2,1)S(1)}, u32[]{:S(2)}, u32[]{:S(2)}) async-start(bf16[2,192,1024]{1,0,2:T(2,128)(2,1)} %copy.109), calls=%async_computation.2 | async-start | bytes 2097152 | tf_op jit(solution)/shard_map/all_to_all | solution.py:245
  354.2 191.5 %all-gather.17.cloned.1.call-start = ((), (), s32[]{:S(2)}) async-start(), calls=%async_computation.18 | async-start | bytes 9437184 | tf_op jit(solution)/shard_map/all_gather | solution.py:181
  404.7 25.8 %copy-start.37 = (bf16[1,8,192,128]{3,1,2,0:T(8,128)(2,1)S(1)}, bf16[1,8,192,128]{3,1,2,0:T(8,128)(2,1)}, u32[]{:S(2)}) copy-start(bf16[1,8,192,128]{3,1,2,0:T(8,128)(2,1)} %get-tuple-element.455) | copy-start | bytes 1179652
  404.7 26.7 %copy-start.38 = (bf16[1,8,192,128]{3,1,2,0:T(8,128)(2,1)S(1)}, bf16[1,8,192,128]{3,1,2,0:T(8,128)(2,1)}, u32[]{:S(2)}) copy-start(bf16[1,8,192,128]{3,1,2,0:T(8,128)(2,1)} %get-tuple-element.457) | copy-start | bytes 1179652
  458.2 71.3 %copy-start.5 = (bf16[1536,2,64]{0,2,1:T(8,128)(2,1)}, bf16[1536,2,64]{0,2,1:T(8,128)(2,1)S(1)}, u32[]{:S(2)}) copy-start(bf16[1536,2,64]{0,2,1:T(8,128)(2,1)S(1)} %get-tuple-element.946) | copy-start | bytes 1179652
  458.2 71.3 %copy-start.14 = (bf16[1536,2,64]{0,2,1:T(8,128)(2,1)}, bf16[1536,2,64]{0,2,1:T(8,128)(2,1)S(1)}, u32[]{:S(2)}) copy-start(bf16[1536,2,64]{0,2,1:T(8,128)(2,1)S(1)} %get-tuple-element.947) | copy-start | bytes 1179652
  458.2 71.3 %copy-start.24 = (bf16[1536,2,64]{0,2,1:T(8,128)(2,1)}, bf16[1536,2,64]{0,2,1:T(8,128)(2,1)S(1)}, u32[]{:S(2)}) copy-start(bf16[1536,2,64]{0,2,1:T(8,128)(2,1)S(1)} %get-tuple-element.987) | copy-start | bytes 1179652
  458.2 13.5 %copy-start.84 = (s32[2,192]{1,0:T(2,128)S(1)}, s32[2,192]{1,0:T(2,128)}, u32[]{:S(2)}) copy-start(s32[2,192]{1,0:T(2,128)} %param.24) | copy-start | bytes 4612
  458.9 70.6 %copy-start.10 = (f32[384,1024]{1,0:T(8,128)S(1)}, f32[384,1024]{1,0:T(8,128)}, u32[]{:S(2)}) copy-start(f32[384,1024]{1,0:T(8,128)} %copy-done.9) | copy-start | bytes 4718596
  467.5 59.5 %all-to-all-start.3 = ((bf16[2,1536,128]{2,0,1:T(2,128)(2,1)}), bf16[2,1536,128]{2,0,1:T(2,128)(2,1)}, u32[]{:S(2)}, u32[]{:S(2)}) async-start(bf16[2,1536,128]{2,0,1:T(2,128)(2,1)} %copy.117), calls=%async_computation.3 | async-start | bytes 1572864 | tf_op jit(solution)/shard_map/all_to_all | solution.py:259
  533.9 42.1 %copy-start.7 = (f32[384,1024]{1,0:T(8,128)}, f32[384,1024]{1,0:T(8,128)S(1)}, u32[]{:S(2)}) copy-start(f32[384,1024]{1,0:T(8,128)S(1)} %get-tuple-element.423) | copy-start | bytes 4718596
  534.2 11.4 copy-start.82
  534.3 11.4 copy-start.75
  536.8 8.9 copy-start.50
  536.8 9.0 copy-start.86
  545.7 12.4 copy-start.89
  545.7 22.7 %slice-start.4 = ((s8[9437184]{0:T(1024)(128)(4,1)}), s8[4194304]{0:T(1024)(128)(4,1)S(1)}, s32[]{:S(2)}) async-start(s8[9437184]{0:T(1024)(128)(4,1)} %bitcast.268), calls=%async_computation.29 | async-start | bytes 8388608
  557.2 20.0 %copy-start.29 = (f32[384,1024]{1,0:T(8,128)}, f32[384,1024]{1,0:T(8,128)S(1)}, u32[]{:S(2)}) copy-start(f32[384,1024]{1,0:T(8,128)S(1)} %get-tuple-element.421) | copy-start | bytes 4718596
  558.1 10.3 slice-start.5
  558.1 10.3 slice-start.6
  558.1 10.3 copy-start.68
  568.4 7.6 copy-start.83
  568.4 7.6 copy-start.76
  582.4 30.2 %all-to-all-start.4 = ((bf16[2,192,1024]{1,0,2:T(2,128)(2,1)}), bf16[2,192,1024]{1,0,2:T(2,128)(2,1)S(1)}, u32[]{:S(2)}, u32[]{:S(2)}) async-start(bf16[2,192,1024]{1,0,2:T(2,128)(2,1)} %copy.119), calls=%async_computation.4 | async-start | bytes 2097152 | tf_op jit(solution)/shard_map/all_to_all | solution.py:293
  586.0 30.7 %copy-start.18 = (bf16[1536,2,64]{0,2,1:T(8,128)(2,1)S(1)}, bf16[1536,2,64]{0,2,1:T(8,128)(2,1)}, u32[]{:S(2)}) copy-start(bf16[1536,2,64]{0,2,1:T(8,128)(2,1)} %copy-done.17) | copy-start | bytes 1179652
  623.7 7.3 slice-start.1
  645.7 7.3 slice-start.1
  695.9 7.3 slice-start.2
  695.9 7.3 slice-start.3
  717.9 7.3 slice-start.3
  756.1 7.7 copy-start.42
  757.3 7.4 copy-start.41
  760.2 24.5 %all-to-all-start.6 = ((bf16[2,1536,128]{2,0,1:T(2,128)(2,1)}), bf16[2,1536,128]{2,0,1:T(2,128)(2,1)S(1)}, u32[]{:S(2)}, u32[]{:S(2)}) async-start(bf16[2,1536,128]{2,0,1:T(2,128)(2,1)} %copy.128), calls=%async_computation.6 | async-start | bytes 1572864 | tf_op jit(solution)/shard_map/all_to_all | solution.py:313
  784.7 24.5 %all-to-all-start.5 = ((bf16[2,1536,128]{2,0,1:T(2,128)(2,1)}), bf16[2,1536,128]{2,0,1:T(2,128)(2,1)S(1)}, u32[]{:S(2)}, u32[]{:S(2)}) async-start(bf16[2,1536,128]{2,0,1:T(2,128)(2,1)} %copy.125), calls=%async_computation.5 | async-start | bytes 1572864 | tf_op jit(solution)/shard_map/all_to_all | solution.py:312
  789.4 24.0 %copy-start.33 = (bf16[2,8,192,128]{3,1,2,0:T(8,128)(2,1)S(1)}, bf16[2,8,192,128]{3,1,2,0:T(8,128)(2,1)}, u32[]{:S(2)}) copy-start(bf16[2,8,192,128]{3,1,2,0:T(8,128)(2,1)} %copy.118) | copy-start | bytes 2359300
  809.1 30.5 %all-to-all-start.7 = ((bf16[2,1536,128]{2,0,1:T(2,128)(2,1)}), bf16[2,1536,128]{2,0,1:T(2,128)(2,1)}, u32[]{:S(2)}, u32[]{:S(2)}) async-start(bf16[2,1536,128]{2,0,1:T(2,128)(2,1)} %copy.131), calls=%async_computation.7 | async-start | bytes 1572864 | tf_op jit(solution)/shard_map/all_to_all | solution.py:314
  813.4 130.4 %reduce-scatter.10.cloned.1.call-start = ((), (), s32[]{:S(2)}) async-start(), calls=%async_computation.21 | async-start | bytes 2359296 | tf_op jit(solution)/shard_map/reduce_scatter | solution.py:374
  817.2 126.6 %reduce-scatter.6.cloned.1.call-start = ((), (), s32[]{:S(2)}) async-start(), calls=%async_computation.19 | async-start | bytes 4718592 | tf_op jit(solution)/shard_map/reduce_scatter | solution.py:368
  831.3 17.8 %copy-start.26 = (f32[384,16,64]{0,2,1:T(8,128)S(1)}, f32[384,16,64]{0,2,1:T(8,128)}, u32[]{:S(2)}) copy-start(f32[384,16,64]{0,2,1:T(8,128)} %reshape.430) | copy-start | bytes 4718596
  831.3 17.8 %copy-start.27 = (f32[384,16,64]{0,2,1:T(8,128)S(1)}, f32[384,16,64]{0,2,1:T(8,128)}, u32[]{:S(2)}) copy-start(f32[384,16,64]{0,2,1:T(8,128)} %reshape.429) | copy-start | bytes 4718596
  831.3 17.8 %copy-start.60 = (f32[384,32]{0,1:T(8,128)S(1)}, f32[384,32]{0,1:T(8,128)}, u32[]{:S(2)}) copy-start(f32[384,32]{0,1:T(8,128)} %get-tuple-element.464) | copy-start | bytes 147460
  831.3 17.8 %copy-start.61 = (f32[384,32]{0,1:T(8,128)S(1)}, f32[384,32]{0,1:T(8,128)}, u32[]{:S(2)}) copy-start(f32[384,32]{0,1:T(8,128)} %get-tuple-element.465) | copy-start | bytes 147460
  851.2 7.3 copy-start.81
  851.2 7.3 copy-start.79
  868.8 120.0 %reduce-scatter.8.cloned.1.call-start = ((), (), s32[]{:S(2)}) async-start(), calls=%async_computation.20 | async-start | bytes 7077888 | tf_op jit(solution)/shard_map/reduce_scatter | solution.py:371
  878.2 200.4 %reduce-scatter.14.cloned.1.call-start = ((), (), s32[]{:S(2)}) async-start(), calls=%async_computation.23 | async-start | bytes 9437184 | tf_op jit(solution)/shard_map/reduce_scatter | solution.py:380
  890.3 278.6 %reduce-scatter.12.cloned.1.call-start = ((), (), s32[]{:S(2)}) async-start(), calls=%async_computation.22 | async-start | bytes 9437184 | tf_op jit(solution)/shard_map/reduce_scatter | solution.py:377
  900.1 395.1 %all-reduce.7.cloned.1.call-start = ((), (), s32[]{:S(2)}) async-start(), calls=%async_computation.24 | async-start | bytes 10485760 | tf_op jit(solution)/shard_map/psum | solution.py:385
  941.3 227.7 %copy-start.58 = (bf16[384,1024]{1,0:T(8,128)(2,1)S(1)}, bf16[384,1024]{1,0:T(8,128)(2,1)}, u32[]{:S(2)}) copy-start(bf16[384,1024]{1,0:T(8,128)(2,1)} %copy-done.57) | copy-start | bytes 2359300
  (87 other events, 299.1 us)
Sparse Core Ops, SparseCore 0:
  9.7 49.8 all-gather.6
  61.2 115.4 all-gather.8
  178.3 62.9 all-gather.10
  242.8 34.8 all-gather.12
  279.1 128.9 all-gather.14
  409.5 96.2 all-gather.16
  817.3 39.7 reduce-scatter.9
  868.9 48.8 reduce-scatter.5
  920.1 68.6 reduce-scatter.7
  990.9 87.6 reduce-scatter.13
  1080.9 87.9 reduce-scatter.11
  1173.8 121.3 all-reduce.6
where the time goes:
time: 1320 us; the launch traced here: 1310 us
  waiting for transfers between devices  737 us (56%)
  matrix products  245 us (19%)
  local copies, waits for them, and re-layouts  131 us (10%)
  blocking collectives  81 us (6%)
  other arithmetic  62.6 us (5%)
  starting transfers between devices  30.7 us (2%)
  between operations  16.4 us (1%)
    all_gather x1, waiting for transfers between devices, shards(): lax.all_gather(modulation, 'seq', axis=0, tiled=True)  113 us
    psum x1, waiting for transfers between devices, shards(): lax.psum(scattered[0].astype(jnp.bfloat16), 'grp').astype(jnp.float32)  111 us
    reduce_scatter x1, waiting for transfers between devices, shards(): lax.psum_scatter(expand_part.astype(jnp.bfloat16), 'seq', scatter_dimensi...  90.3 us
    reduce_scatter x1, waiting for transfers between devices, shards(): lax.psum_scatter(contract_part.astype(jnp.bfloat16), 'seq', scatter_dimen...  89.8 us
    psum x1, blocking collectives, shards(): kept_total = lax.psum(jnp.sum(kept_float), ('grp', 'seq'))  53.3 us
    all_to_all x1, waiting for transfers between devices, shards(): lax.all_to_all(query_low, 'seq', split_axis=2, concat_axis=1, tiled=True)  51.4 us
    all_gather x1, waiting for transfers between devices, shards(): lax.all_gather(projection, 'seq', axis=0, tiled=True)  50.3 us
    all_gather x1, waiting for transfers between devices, shards(): lax.all_gather(combine, 'seq', axis=0, tiled=True)  47.4 us
  transfers between devices with their start and end apart: 20, of which 14 were waited for; matrix products, arithmetic and copies ran while one was open for 18% of the time, Pallas kernels for 0%

commit v1 on v0

v1 whole, which is shorter than its diff:
```python
import functools

import jax
import jax.numpy as jnp
from jax import lax
from jax.experimental import pallas as pl
from jax.experimental.pallas import tpu as pltpu
from jax.sharding import PartitionSpec as P

HEADS = 16
HEAD_DIM = 64


precise = lax.Precision.HIGHEST
epsilon = 1e-06
rope_base = 10000.0


def product(first_op, second_op):
    return jnp.dot(first_op, second_op, preferred_element_type=jnp.float32)


def product_left(first_op, second_op):
    return lax.dot_general(
        first_op, second_op, (((0,), (0,)), ((), ())), preferred_element_type=jnp.float32
    )


def product_right(first_op, second_op):
    return lax.dot_general(
        first_op, second_op, (((1,), (1,)), ((), ())), preferred_element_type=jnp.float32
    )


def gelu_tanh(values):
    return jax.nn.gelu(values, approximate=True)


def modulate(hidden, shift_part, scale_part):
    center = hidden - jnp.mean(hidden, axis=-1, keepdims=True)
    variance = jnp.mean(center * center, axis=-1, keepdims=True)
    return center * lax.rsqrt(variance + epsilon) * (1.0 + scale_part) + shift_part


def segment_info(lengths, frame_index):
    utter_count = lengths.shape[0]
    utter_ends = jnp.cumsum(lengths)
    starts = utter_ends - lengths
    segment = jnp.sum((frame_index[:, None] >= utter_ends[None, :]).astype(jnp.int32), axis=1)
    member = segment[:, None] == jnp.arange(utter_count, dtype=jnp.int32)[None, :]
    offset = jnp.sum(jnp.where(member, starts[None, :], 0), axis=1)
    return (segment, member, frame_index - offset)


def rotary_tables(position):
    half_dim = HEAD_DIM // 2
    ladder = jnp.arange(half_dim, dtype=jnp.float32) / half_dim
    inverse = jnp.exp(-jnp.log(rope_base) * ladder)
    angles = position.astype(jnp.float32)[:, None] * inverse[None, :]
    return (jnp.cos(angles)[:, None, :], jnp.sin(angles)[:, None, :])


def rotate(vectors, cos_table, sin_table):
    half_dim = vectors.shape[-1] // 2
    front_half = vectors[..., :half_dim]
    back_half = vectors[..., half_dim:]
    return jnp.concatenate(
        [
            front_half * cos_table - back_half * sin_table,
            back_half * cos_table + front_half * sin_table,
        ],
        axis=-1,
    )


MESH = pl.DeviceIdType.MESH
NEG = -1e30


def utter_features(boundary, total_rows, for_keys):
    row = lax.broadcasted_iota(jnp.int32, (total_rows, 128), 0)
    lane = lax.broadcasted_iota(jnp.int32, (total_rows, 128), 1)
    second = (row >= boundary).astype(jnp.float32)
    ahead = (lane == 0).astype(jnp.float32)
    after = (lane == 1).astype(jnp.float32)
    if for_keys:
        return (NEG * (second * ahead + (1.0 - second) * after)).astype(jnp.bfloat16)
    return (second * after + (1.0 - second) * ahead).astype(jnp.bfloat16)


def head_lanes(values, head):
    lane = lax.broadcasted_iota(jnp.int32, values.shape, 1)
    own = (lane >= head * HEAD_DIM) & (lane < (head + 1) * HEAD_DIM)
    return jnp.where(own, values.astype(jnp.float32), 0.0).astype(jnp.bfloat16)


def dot_nn(first_op, second_op):
    return jnp.dot(first_op, second_op, preferred_element_type=jnp.float32)


def dot_nt(first_op, second_op):
    return lax.dot_general(
        first_op, second_op, (((1,), (1,)), ((), ())), preferred_element_type=jnp.float32
    )


def fold_rows(values, combine):
    return combine(values.reshape(values.shape[0] // 8, 8, values.shape[1]), axis=0)


def enter(partners):
    barrier = pltpu.get_barrier_semaphore()
    for partner in partners:
        pl.semaphore_signal(barrier, inc=1, device_id=partner, device_id_type=MESH)
    pl.semaphore_wait(barrier, len(partners))


def key_span(third, total_rows):
    size = total_rows // 3
    return (max(third - 1, 0) * size, min(third + 2, 3) * size)


def forward_kernel(
    seq_count, bound_ref, qkv_ref, kept_ref, mixture_ref, log_ref,
    key_scr, query_scr, value_t_scr, score_scr, mix_t_scr, mix_scr,
    send_sem, recv_sem, back_send_sem, back_recv_sem, local_sem,
):
    group_count, local_rows, local_width = qkv_ref.shape[1], qkv_ref.shape[3], qkv_ref.shape[4]
    total_rows = seq_count * local_rows
    heads = local_width // HEAD_DIM
    me = lax.axis_index("seq")
    grp = lax.axis_index("grp")
    others = [lax.rem(me + step, seq_count) for step in range(1, seq_count)]
    origins = [lax.rem(me + seq_count - step, seq_count) for step in range(1, seq_count)]
    block = min(256, total_rows // 3)
    enter([(grp, other) for other in others])
    copies = []
    for group in range(group_count):
        own = pltpu.make_async_copy(qkv_ref.at[me, group], kept_ref.at[me, group], local_sem.at[group])
        own.start()
        row = [own]
        for step, other in enumerate(others):
            copy = pltpu.make_async_remote_copy(
                qkv_ref.at[other, group], kept_ref.at[me, group],
                send_sem.at[group, step], recv_sem.at[group, step],
                device_id=(grp, other), device_id_type=MESH,
            )
            copy.start()
            row.append(copy)
        copies.append(row)
    back = []
    for group in range(group_count):
        for copy in copies[group]:
            copy.wait()
        boundary = bound_ref[group]
        keys = kept_ref[:, group, 1].reshape(total_rows, local_width)
        values = kept_ref[:, group, 2].reshape(total_rows, local_width)
        key_scr[:, :local_width] = keys
        key_scr[:, local_width:] = utter_features(boundary, total_rows, True)
        query_scr[:, local_width:] = utter_features(boundary, total_rows, False)
        value_t_scr[...] = values.astype(jnp.float32).T.astype(jnp.bfloat16)

        def one_head(head, carry):
            queries = kept_ref[:, group, 0].reshape(total_rows, local_width)
            query_scr[:, :local_width] = head_lanes(queries, head) * jnp.bfloat16(HEAD_DIM ** (-0.5))
            for third in range(3):
                first_key, last_key = key_span(third, total_rows)
                chunks = range(first_key, last_key, block)

                def one_block(index, carry):
                    first_row = pl.multiple_of(third * (total_rows // 3) + index * block, block)
                    query_block = query_scr[pl.ds(first_row, block), :]
                    peak = jnp.full((8, block), -jnp.inf, jnp.float32)
                    for first in chunks:
                        scores = dot_nt(key_scr[first:first + block, :], query_block)
                        score_scr[first:first + block, :] = scores
                        peak = jnp.maximum(peak, fold_rows(scores, jnp.max))
                    peak = jnp.max(peak, axis=0, keepdims=True)
                    total = jnp.zeros((8, block), jnp.float32)
                    for first in chunks:
                        lifted = jnp.exp(score_scr[first:first + block, :] - peak)
                        score_scr[first:first + block, :] = lifted
                        total = total + fold_rows(lifted, jnp.sum)
                    total = jnp.sum(total, axis=0, keepdims=True)
                    inverse = 1.0 / total
                    mixed = jnp.zeros((HEAD_DIM, block), jnp.float32)
                    rows = pl.ds(pl.multiple_of(head * HEAD_DIM, HEAD_DIM), HEAD_DIM)
                    for first in chunks:
                        weight = (score_scr[first:first + block, :] * inverse).astype(jnp.bfloat16)
                        mixed = mixed + dot_nn(value_t_scr[rows, first:first + block], weight)
                    mix_t_scr[rows, pl.ds(first_row, block)] = mixed
                    log_ref[group, head, :, pl.ds(first_row, block)] = peak + jnp.log(total)
                    return carry

                lax.fori_loop(0, total_rows // 3 // block, one_block, 0)
            return carry

        lax.fori_loop(0, heads, one_head, 0)
        mix_scr[group] = mix_t_scr[...].T.astype(jnp.bfloat16).reshape(seq_count, local_rows, local_width)
        own = pltpu.make_async_copy(
            mix_scr.at[group, me], mixture_ref.at[me, group], local_sem.at[group_count + group]
        )
        own.start()
        back.append(own)
        for step, other in enumerate(others):
            copy = pltpu.make_async_remote_copy(
                mix_scr.at[group, other], mixture_ref.at[me, group],
                back_send_sem.at[group, step], back_recv_sem.at[group, step],
                device_id=(grp, other), device_id_type=MESH,
            )
            copy.start()
            back.append(copy)
    for copy in back:
        copy.wait()


def attend_forward(bounds, qkv):
    seq_count, group_count, _, local_rows, local_width = qkv.shape
    total_rows = seq_count * local_rows
    heads = local_width // HEAD_DIM
    block = min(256, total_rows // 3)
    vmem = pl.BlockSpec(memory_space=pltpu.VMEM)
    return pl.pallas_call(
        functools.partial(forward_kernel, seq_count),
        out_shape=(
            jax.ShapeDtypeStruct(qkv.shape, jnp.bfloat16),
            jax.ShapeDtypeStruct((seq_count, group_count, local_rows, local_width), jnp.bfloat16),
            jax.ShapeDtypeStruct((group_count, heads, 1, total_rows), jnp.float32),
        ),
        in_specs=[pl.BlockSpec(memory_space=pltpu.SMEM), pl.BlockSpec(memory_space=pl.ANY)],
        out_specs=(vmem, vmem, vmem),
        scratch_shapes=[
            pltpu.VMEM((total_rows, local_width + 128), jnp.bfloat16),
            pltpu.VMEM((total_rows, local_width + 128), jnp.bfloat16),
            pltpu.VMEM((local_width, total_rows), jnp.bfloat16),
            pltpu.VMEM((total_rows, block), jnp.float32),
            pltpu.VMEM((local_width, total_rows), jnp.float32),
            pltpu.VMEM((group_count, seq_count, local_rows, local_width), jnp.bfloat16),
            pltpu.SemaphoreType.DMA((group_count, seq_count - 1)),
            pltpu.SemaphoreType.DMA((group_count, seq_count - 1)),
            pltpu.SemaphoreType.DMA((group_count, seq_count - 1)),
            pltpu.SemaphoreType.DMA((group_count, seq_count - 1)),
            pltpu.SemaphoreType.DMA((2 * group_count,)),
        ],
        compiler_params=pltpu.CompilerParams(
            collective_id=1, has_side_effects=True, vmem_limit_bytes=48 * 1024 * 1024
        ),
        name="attend_forward",
    )(bounds, qkv)


def backward_kernel(
    seq_count, bound_ref, kept_ref, grad_ref, log_ref, out_ref,
    taken_scr, key_scr, query_scr, key_t_scr, head_query_scr, head_grad_scr, prob_scr, weight_scr,
    query_t_scr, key_sum_scr, value_sum_scr, back_scr,
    send_sem, recv_sem, back_send_sem, back_recv_sem, local_sem,
):
    group_count, local_rows, local_width = grad_ref.shape[1], grad_ref.shape[2], grad_ref.shape[3]
    total_rows = seq_count * local_rows
    heads = local_width // HEAD_DIM
    me = lax.axis_index("seq")
    grp = lax.axis_index("grp")
    others = [lax.rem(me + step, seq_count) for step in range(1, seq_count)]
    block = min(256, total_rows // 3)
    enter([(grp, other) for other in others])
    copies = []
    for group in range(group_count):
        own = pltpu.make_async_copy(grad_ref.at[me, group], taken_scr.at[me, group], local_sem.at[group])
        own.start()
        row = [own]
        for step, other in enumerate(others):
            copy = pltpu.make_async_remote_copy(
                grad_ref.at[other, group], taken_scr.at[me, group],
                send_sem.at[group, step], recv_sem.at[group, step],
                device_id=(grp, other), device_id_type=MESH,
            )
            copy.start()
            row.append(copy)
        copies.append(row)
    back = []
    for group in range(group_count):
        for copy in copies[group]:
            copy.wait()
        boundary = bound_ref[group]
        keys = kept_ref[:, group, 1].reshape(total_rows, local_width)
        key_scr[:, :local_width] = keys
        key_scr[:, local_width:] = utter_features(boundary, total_rows, True)
        query_scr[:, local_width:] = utter_features(boundary, total_rows, False)
        key_t_scr[...] = keys.astype(jnp.float32).T.astype(jnp.bfloat16)
        key_sum_scr[...] = jnp.zeros_like(key_sum_scr)
        value_sum_scr[...] = jnp.zeros_like(value_sum_scr)

        def one_head(head, carry):
            queries = head_lanes(kept_ref[:, group, 0].reshape(total_rows, local_width), head)
            head_query_scr[...] = queries
            query_scr[:, :local_width] = queries * jnp.bfloat16(HEAD_DIM ** (-0.5))
            head_grad_scr[...] = head_lanes(taken_scr[:, group].reshape(total_rows, local_width), head)
            for third in range(3):
                first_key, last_key = key_span(third, total_rows)
                chunks = range(first_key, last_key, block)

                def one_block(index, carry):
                    first_row = pl.multiple_of(third * (total_rows // 3) + index * block, block)
                    own_rows = pl.ds(first_row, block)
                    query_block = query_scr[own_rows, :]
                    grad_block = head_grad_scr[own_rows, :]
                    plain_block = head_query_scr[own_rows, :]
                    log_block = log_ref[group, head, :, own_rows]
                    row_dot = jnp.zeros((8, block), jnp.float32)
                    for first in chunks:
                        scores = dot_nt(key_scr[first:first + block, :], query_block)
                        prob = jnp.exp(scores - log_block)
                        values = kept_ref[
                            first // local_rows:(first + block - 1) // local_rows + 1, group, 2
                        ].reshape(-1, local_width)
                        skip = first % local_rows
                        weight_grad = dot_nt(values[skip:skip + block], grad_block)
                        prob_scr[first:first + block, :] = prob
                        weight_scr[first:first + block, :] = weight_grad
                        row_dot = row_dot + fold_rows(prob * weight_grad, jnp.sum)
                    row_dot = jnp.sum(row_dot, axis=0, keepdims=True)
                    rows = pl.ds(pl.multiple_of(head * HEAD_DIM, HEAD_DIM), HEAD_DIM)
                    turned = jnp.zeros((HEAD_DIM, block), jnp.float32)
                    for first in chunks:
                        prob = prob_scr[first:first + block, :]
                        score_grad = (
                            HEAD_DIM ** (-0.5) * (prob * (weight_scr[first:first + block, :] - row_dot))
                        ).astype(jnp.bfloat16)
                        key_sum_scr[first:first + block, :] += dot_nn(score_grad, plain_block)
                        value_sum_scr[first:first + block, :] += dot_nn(
                            prob.astype(jnp.bfloat16), grad_block
                        )
                        turned = turned + dot_nn(key_t_scr[rows, first:first + block], score_grad)
                    query_t_scr[rows, own_rows] = turned
                    return carry

                lax.fori_loop(0, total_rows // 3 // block, one_block, 0)
            return carry

        lax.fori_loop(0, heads, one_head, 0)
        shape = (seq_count, local_rows, local_width)
        back_scr[:, group, 0] = query_t_scr[...].T.astype(jnp.bfloat16).reshape(shape)
        back_scr[:, group, 1] = key_sum_scr[...].astype(jnp.bfloat16).reshape(shape)
        back_scr[:, group, 2] = value_sum_scr[...].astype(jnp.bfloat16).reshape(shape)
        own = pltpu.make_async_copy(
            back_scr.at[me, group], out_ref.at[me, group], local_sem.at[group_count + group]
        )
        own.start()
        back.append(own)
        for step, other in enumerate(others):
            copy = pltpu.make_async_remote_copy(
                back_scr.at[other, group], out_ref.at[me, group],
                back_send_sem.at[group, step], back_recv_sem.at[group, step],
                device_id=(grp, other), device_id_type=MESH,
            )
            copy.start()
            back.append(copy)
    for copy in back:
        copy.wait()


def attend_backward(bounds, kept, grad, log_total):
    seq_count, group_count, _, local_rows, local_width = kept.shape
    total_rows = seq_count * local_rows
    block = min(256, total_rows // 3)
    vmem = pl.BlockSpec(memory_space=pltpu.VMEM)
    return pl.pallas_call(
        functools.partial(backward_kernel, seq_count),
        out_shape=jax.ShapeDtypeStruct(kept.shape, jnp.bfloat16),
        in_specs=[
            pl.BlockSpec(memory_space=pltpu.SMEM), vmem, pl.BlockSpec(memory_space=pl.ANY), vmem
        ],
        out_specs=vmem,
        scratch_shapes=[
            pltpu.VMEM(grad.shape, jnp.bfloat16),
            pltpu.VMEM((total_rows, local_width + 128), jnp.bfloat16),
            pltpu.VMEM((total_rows, local_width + 128), jnp.bfloat16),
            pltpu.VMEM((local_width, total_rows), jnp.bfloat16),
            pltpu.VMEM((total_rows, local_width), jnp.bfloat16),
            pltpu.VMEM((total_rows, local_width), jnp.bfloat16),
            pltpu.VMEM((total_rows, block), jnp.float32),
            pltpu.VMEM((total_rows, block), jnp.float32),
            pltpu.VMEM((local_width, total_rows), jnp.float32),
            pltpu.VMEM((total_rows, local_width), jnp.float32),
            pltpu.VMEM((total_rows, local_width), jnp.float32),
            pltpu.VMEM(kept.shape, jnp.bfloat16),
            pltpu.SemaphoreType.DMA((group_count, seq_count - 1)),
            pltpu.SemaphoreType.DMA((group_count, seq_count - 1)),
            pltpu.SemaphoreType.DMA((group_count, seq_count - 1)),
            pltpu.SemaphoreType.DMA((group_count, seq_count - 1)),
            pltpu.SemaphoreType.DMA((2 * group_count,)),
        ],
        compiler_params=pltpu.CompilerParams(
            collective_id=2, has_side_effects=True, vmem_limit_bytes=48 * 1024 * 1024
        ),
        name="attend_backward",
    )(bounds, kept, grad, log_total)


def shards(
    frames,
    shortcut,
    time_embed,
    lengths,
    kept_mask,
    target,
    combine,
    modulation,
    projection,
    readout,
    expand,
    contract,
):
    gathered = (
        lax.all_gather(combine, "seq", axis=0, tiled=True),
        lax.all_gather(projection, "seq", axis=0, tiled=True),
        lax.all_gather(readout, "seq", axis=0, tiled=True),
        lax.all_gather(expand, "seq", axis=0, tiled=True),
        lax.all_gather(contract, "seq", axis=0, tiled=True),
    )
    combine_full, projection_full, readout_full, expand_full, contract_full = (
        gathered
    )
    group_count = frames.shape[0]
    local_rows = frames.shape[1]
    width = HEADS * HEAD_DIM
    row_count = group_count * local_rows
    seq_count = lax.axis_size("seq")
    group_frames = local_rows * seq_count
    all_frames = group_frames * lax.axis_size("grp") * group_count
    utter_count = time_embed.shape[1]
    kept_float = kept_mask.astype(jnp.float32).reshape(row_count)
    kept_total = lax.psum(jnp.sum(kept_float), ("grp", "seq"))
    local_index = lax.axis_index("seq") * local_rows + jnp.arange(local_rows, dtype=jnp.int32)

    def local_info(length_row):
        return segment_info(length_row, local_index)

    member_info = jax.vmap(local_info)(lengths)
    member_float = member_info[1].astype(jnp.float32)
    position = member_info[2]
    cos_table, sin_table = rotary_tables(position.reshape(row_count))
    joined = jnp.concatenate([frames, shortcut], axis=2).reshape(row_count, 2 * width)
    hidden = product(joined, combine_full)
    silu_value, silu_pull = jax.vjp(jax.nn.silu, time_embed)
    condition = silu_value.astype(jnp.bfloat16)
    shard_rows = modulation.shape[0]
    condition_part = lax.dynamic_slice_in_dim(
        condition, lax.axis_index("seq") * shard_rows, shard_rows, 2
    ).reshape(group_count * utter_count, shard_rows)
    modulation_utter = lax.psum(product(condition_part, modulation), "seq").reshape(
        group_count, utter_count, 6 * width
    )
    modulation_frame = jnp.einsum(
        "gtu,gue->gte",
        member_float,
        modulation_utter,
        precision=precise,
        preferred_element_type=jnp.float32,
    ).reshape(row_count, 6 * width)
    shift_first, scale_first, gate_first, shift_second, scale_second, gate_second = jnp.split(
        modulation_frame, 6, axis=1
    )
    normed_value, first_pull = jax.vjp(modulate, hidden, shift_first, scale_first)
    normed = normed_value.astype(jnp.bfloat16)
    packed = product(normed, projection_full)
    query_raw, key_raw, value_raw = jnp.split(packed, 3, axis=1)
    head_shape = (row_count, HEADS, HEAD_DIM)
    split_shape = (group_count, local_rows, width)

    def rotate_local(vectors):
        return rotate(vectors, cos_table, sin_table)

    query_turned, query_pull = jax.vjp(rotate_local, query_raw.reshape(head_shape))
    key_turned, key_pull = jax.vjp(rotate_local, key_raw.reshape(head_shape))
    local_width = width // seq_count

    def by_target(vectors):
        return vectors.reshape(group_count, local_rows, seq_count, local_width).astype(jnp.bfloat16)

    qkv = jnp.transpose(
        jnp.stack([by_target(query_turned), by_target(key_turned), by_target(value_raw)]),
        (3, 1, 0, 2, 4),
    )
    bounds = lengths[:, 0]
    kept_heads, mixture_blocks, log_total = attend_forward(bounds, qkv)
    mixture = jnp.transpose(mixture_blocks, (1, 2, 0, 3)).reshape(row_count, width)
    branch = product(mixture, readout_full)
    middle = hidden + gate_first * branch
    second_value, second_pull = jax.vjp(modulate, middle, shift_second, scale_second)
    normed_second = second_value.astype(jnp.bfloat16)
    expanded = product(normed_second, expand_full)
    active_value, gelu_pull = jax.vjp(gelu_tanh, expanded)
    active = active_value.astype(jnp.bfloat16)
    contracted = product(active, contract_full)
    output = middle + gate_second * contracted
    loss_scale = all_frames / kept_total
    output_grad = (
        loss_scale
        * kept_float[:, None]
        * (output - target.reshape(row_count, width).astype(jnp.float32))
    )
    combine_back, projection_back, readout_back, expand_back, contract_back = (
        gathered
    )
    gate_second_grad = output_grad * contracted
    contracted_grad = (gate_second * output_grad).astype(jnp.bfloat16)
    contract_part = product_left(active, contracted_grad)
    active_grad = product_right(contracted_grad, contract_back)
    expanded_grad = gelu_pull(active_grad)[0].astype(jnp.bfloat16)
    expand_part = product_left(normed_second, expanded_grad)
    normed_second_grad = product_right(expanded_grad, expand_back)
    middle_extra, shift_second_grad, scale_second_grad = second_pull(normed_second_grad)
    middle_grad = output_grad + middle_extra
    gate_first_grad = middle_grad * branch
    branch_grad = (gate_first * middle_grad).astype(jnp.bfloat16)
    readout_part = product_left(mixture, branch_grad)
    mixture_grad = product_right(branch_grad, readout_back).astype(jnp.bfloat16)
    back_blocks = attend_backward(
        bounds,
        kept_heads,
        jnp.transpose(
            mixture_grad.reshape(group_count, local_rows, seq_count, local_width), (2, 0, 1, 3)
        ),
        log_total,
    )
    query_back, key_back, value_back = jnp.transpose(back_blocks, (2, 1, 3, 0, 4)).reshape(
        3, group_count, local_rows, width
    )
    query_unturned = query_pull(query_back.reshape(head_shape).astype(jnp.float32))[0].reshape(
        row_count, width
    )
    key_unturned = key_pull(key_back.reshape(head_shape).astype(jnp.float32))[0].reshape(
        row_count, width
    )
    packed_grad = jnp.concatenate(
        [
            query_unturned.astype(jnp.bfloat16),
            key_unturned.astype(jnp.bfloat16),
            value_back.reshape(row_count, width),
        ],
        axis=1,
    )
    projection_part = product_left(normed, packed_grad)
    normed_grad = product_right(packed_grad, projection_back)
    hidden_extra, shift_first_grad, scale_first_grad = first_pull(normed_grad)
    hidden_grad = (middle_grad + hidden_extra).astype(jnp.bfloat16)
    combine_part = product_left(joined, hidden_grad)
    joined_grad = product_right(hidden_grad, combine_back)
    frames_grad = joined_grad[:, :width].reshape(split_shape)
    shortcut_grad = joined_grad[:, width:].reshape(split_shape)
    modulation_frame_grad = jnp.concatenate(
        [
            shift_first_grad,
            scale_first_grad,
            gate_first_grad,
            shift_second_grad,
            scale_second_grad,
            gate_second_grad,
        ],
        axis=1,
    )
    utter_part = jnp.einsum(
        "gtu,gte->gue",
        member_float,
        modulation_frame_grad.reshape(group_count, local_rows, 6 * width),
        precision=precise,
        preferred_element_type=jnp.float32,
    )
    utter_grad = lax.psum(utter_part.astype(jnp.bfloat16), "seq")
    utter_rows = utter_grad.reshape(group_count * utter_count, 6 * width)
    condition_grad = lax.all_gather(
        product_right(utter_rows, modulation), "seq", axis=1, tiled=True
    ).reshape(group_count, utter_count, width)
    time_grad = silu_pull(condition_grad)[0]
    modulation_part = product_left(condition_part, utter_rows)
    scattered = (
        lax.psum_scatter(
            combine_part.astype(jnp.bfloat16), "seq", scatter_dimension=0, tiled=True
        ).astype(jnp.float32),
        lax.psum_scatter(
            projection_part.astype(jnp.bfloat16), "seq", scatter_dimension=0, tiled=True
        ).astype(jnp.float32),
        lax.psum_scatter(
            readout_part.astype(jnp.bfloat16), "seq", scatter_dimension=0, tiled=True
        ).astype(jnp.float32),
        lax.psum_scatter(
            expand_part.astype(jnp.bfloat16), "seq", scatter_dimension=0, tiled=True
        ).astype(jnp.float32),
        lax.psum_scatter(
            contract_part.astype(jnp.bfloat16), "seq", scatter_dimension=0, tiled=True
        ).astype(jnp.float32),
    )
    summed = (
        lax.psum(scattered[0].astype(jnp.bfloat16), "grp").astype(jnp.float32),
        lax.psum(modulation_part.astype(jnp.bfloat16), "grp").astype(jnp.float32),
        lax.psum(scattered[1].astype(jnp.bfloat16), "grp").astype(jnp.float32),
        lax.psum(scattered[2].astype(jnp.bfloat16), "grp").astype(jnp.float32),
        lax.psum(scattered[3].astype(jnp.bfloat16), "grp").astype(jnp.float32),
        lax.psum(scattered[4].astype(jnp.bfloat16), "grp").astype(jnp.float32),
    )
    return (
        output.astype(jnp.bfloat16).reshape(split_shape),
        frames_grad,
        shortcut_grad,
        time_grad,
        summed[0],
        summed[1],
        summed[2],
        summed[3],
        summed[4],
        summed[5],
    )


def solution(mesh):
    return jax.shard_map(
        shards,
        mesh=mesh,
        in_specs=(
            P("grp", "seq", None),
            P("grp", "seq", None),
            P("grp", None, None),
            P("grp", None),
            P("grp", "seq"),
            P("grp", "seq", None),
            P("seq", None),
            P("seq", None),
            P("seq", None),
            P("seq", None),
            P("seq", None),
            P("seq", None),
        ),
        out_specs=(
            P("grp", "seq", None),
            P("grp", "seq", None),
            P("grp", "seq", None),
            P("grp", None, None),
            P("seq", None),
            P("seq", None),
            P("seq", None),
            P("seq", None),
            P("seq", None),
            P("seq", None),
        ),
        check_vma=False,
    )
```

time: 1320 us -> 1070 us (0.81)
  waiting for transfers between devices: 737 us -> 509 us
  Pallas kernels: 0 us -> 218 us
  matrix products: 245 us -> 122 us
  local copies, waits for them, and re-layouts: 131 us -> 61.5 us
  starting transfers between devices: 30.7 us -> 1.06 us
  other arithmetic: 62.6 us -> 40.7 us
    pallas_call x0 -> x2, Pallas kernels: none -> 218 us  [the longest x1 136 us: attend_forward(): pl.pallas_call(functools.partial(forward_kernel, seq_count), out_shape=(j...]
    all_to_all x8 -> x0, waiting for transfers between devices: 187 us -> none  [the longest x1 51.4 us: shards(): lax.all_to_all(query_low, 'seq', split_axis=2, concat_axis=1, tiled=True)]
    dot_general x42 -> x0, matrix products: 115 us -> none  [the longest x12 37.4 us: masked_scores(): jnp.einsum('qhd,khd->hqk', query_block, key_all, preferred_element_type=j...]
    all_gather x1 -> x0, waiting for transfers between devices: 113 us -> none  [shards(): lax.all_gather(modulation, 'seq', axis=0, tiled=True)]
    all_gather x1, waiting for transfers between devices: 0.02 us -> 66.7 us  [shards(): lax.all_gather(contract, 'seq', axis=0, tiled=True)]
    all_to_all x8 -> x0, starting transfers between devices: 30.2 us -> none  [the longest x1 4.22 us: shards(): lax.all_to_all(jnp.stack(value_list), 'seq', split_axis=1, concat_axis=2,...]
    dynamic_slice x24 -> x0, local copies, waits for them, and re-layouts: 16.5 us -> none  [the longest x12 9.01 us: one_block(): lax.dynamic_slice_in_dim(segment_all, first_row, block_rows, 0)]
    while x98 -> x0, local copies, waits for them, and re-layouts: 16.5 us -> none
  transfers between devices with their start and end apart: 20 -> 12, of which waited for: 14 -> 8; matrix products, arithmetic and copies ran while one was open for 18% -> 16% of each run, Pallas kernels for 0% -> 21%
where the time goes in v1:
time: 1070 us; the launch traced here: 1060 us
  waiting for transfers between devices  509 us (48%)
  Pallas kernels  218 us (20%)
  matrix products  122 us (11%)
  blocking collectives  92.6 us (9%)
  local copies, waits for them, and re-layouts  61.5 us (6%)
  other arithmetic  40.7 us (4%)
  between operations  15.6 us (1%)
    pallas_call x1, Pallas kernels, attend_forward(): pl.pallas_call(functools.partial(forward_kernel, seq_count), out_shape=(j...  136 us
    psum x1, waiting for transfers between devices, shards(): lax.psum(scattered[0].astype(jnp.bfloat16), 'grp').astype(jnp.float32)  107 us
    reduce_scatter x1, waiting for transfers between devices, shards(): lax.psum_scatter(expand_part.astype(jnp.bfloat16), 'seq', scatter_dimensi...  90.4 us
    reduce_scatter x1, waiting for transfers between devices, shards(): lax.psum_scatter(contract_part.astype(jnp.bfloat16), 'seq', scatter_dimen...  90 us
    pallas_call x1, Pallas kernels, attend_backward(): pl.pallas_call(functools.partial(backward_kernel, seq_count), out_shape=j...  82 us
    all_gather x1, waiting for transfers between devices, shards(): lax.all_gather(contract, 'seq', axis=0, tiled=True)  66.7 us
    all_gather x1, waiting for transfers between devices, shards(): lax.all_gather(projection, 'seq', axis=0, tiled=True)  57.7 us
    reduce_scatter x1, waiting for transfers between devices, shards(): lax.psum_scatter(projection_part.astype(jnp.bfloat16), 'seq', scatter_dim...  45.8 us
  transfers between devices with their start and end apart: 12, of which 8 were waited for; matrix products, arithmetic and copies ran while one was open for 16% of the time, Pallas kernels for 21%

profile of v1, /device:TPU:0, one launch (start us, length us, event | category | flops | bytes accessed | tf_op | source)
XLA Modules:
  0.0 1060.1 jit_solution(16670577824062257059)
XLA Ops:
  13.7 42.2 %psum.64 = f32[]{:T(128)} all-reduce(f32[]{:T(128)} %convert_reduce_fusion), channel_id=1, replica_groups=mesh['grp'=4,'seq'=8] {'grp','seq'}, use_global_device_ids=true, to_apply=%region_9.10 | all-reduce | flops 1 | bytes 8 | tf_op jit(solution)/shard_map/psum | solution.py:433
  57.6 1.5 pad_maximum_fusion.1
  59.1 6.2 all-reduce.8.cloned.1.call-done
  65.3 8.5 fusion.24
  73.8 41.9 %all-gather.6.cloned.1.call-done = bf16[2048,1024]{1,0:T(8,128)(2,1)} async-done(((bf16[256,1024]{1,0:T(8,128)(2,1)}), bf16[2048,1024]{1,0:T(8,128)(2,1)}) %all-gather.6.cloned.1.call-update) | async-done | bytes 4194320 | tf_op jit(solution)/shard_map/all_gather | solution.py:415
  115.7 4.1 fusion.40
  121.0 2.3 fusion.9
  123.3 57.7 %all-gather.8.cloned.1.call-done = bf16[1024,3072]{1,0:T(8,128)(2,1)} async-done(((bf16[128,3072]{1,0:T(8,128)(2,1)}), bf16[1024,3072]{1,0:T(8,128)(2,1)}) %all-gather.8.cloned.1.call-update) | async-done | bytes 6291472 | tf_op jit(solution)/shard_map/all_gather | solution.py:416
  181.0 4.7 fusion.42
  185.7 2.0 fusion.38
  188.9 1.9 copy.33
  190.8 1.5 fusion.15
  193.6 3.0 copy.34
  196.6 1.8 subtract_convert_fusion.1
  198.4 1.4 pad_maximum_fusion.4
  199.9 3.1 convert_element_type.164
  202.9 1.9 copy.35
  204.8 3.3 convert_element_type.165
  208.1 1.9 copy.36
  210.0 1.9 maximum_bitcast_fusion.qkv_ref
  211.8 135.8 %attend_forward.1 = (bf16[8,2,3,192,128]{4,3,2,1,0:T(8,128)(2,1)S(1)}, bf16[8,2,192,128]{3,2,1,0:T(8,128)(2,1)S(1)}, f32[2,2,1,1536]{3,2,1,0:T(1,128)S(1)}) custom-call(s32[2]{0:T(128)S(1)} %slice_reduce_fusion.bound_ref, bf16[8,2,3,192,128]{4,3,2,1,0:T(8,128)(2,1)S(1)} %maximum_bitcast_fusion.qkv_ref), custom_call_target="tpu_custom_call" | custom-call | tf_op jit(solution)/shard_map/attend_forward/pallas_call | solution.py:223
  350.4 4.9 fusion.37
  355.7 3.1 fusion.8
  358.8 10.4 fusion.43
  369.2 66.7 %all-gather.14.cloned.1.call-done = bf16[4096,1024]{1,0:T(8,128)(2,1)} async-done(((bf16[512,1024]{1,0:T(8,128)(2,1)}), bf16[4096,1024]{1,0:T(8,128)(2,1)}) %all-gather.14.cloned.1.call-update) | async-done | bytes 8388624 | tf_op jit(solution)/shard_map/all_gather | solution.py:419
  435.9 11.4 %multiply_convert_fusion.2 = (bf16[384,1024]{1,0:T(8,128)(2,1)S(1)}, f32[384,1024]{1,0:T(8,128)S(1)}, bf16[384,1024]{1,0:T(8,128)(2,1)}, f32[384,1024]{1,0:T(8,128)}) fusion(f32[384,6144]{1,0:T(8,128)} %bitcast.91, bf16[2,192,1024]{2,1,0:T(8,128)(2,1)} %param.17, f32[384,1024]{1,0:T(8,128)S(1)} %get-tuple-element.31, f32[384]{0:T(512)S(1)} %mul.364, ...), kind=kOutput, calls=%fused_computation.43 | convolution fusion | flops 3238526976 | bytes 23332352 | tf_op jit(solution)/shard_map/dot_general | solution.py:20
  448.2 10.4 fusion.7
  458.7 7.3 multiply_reduce_fusion.1
  467.2 1.4 multiply_convert_fusion.1
  469.5 2.6 convolution_convert_fusion.5
  472.2 2.9 fusion.13
  476.7 82.0 %attend_backward.1 = bf16[8,2,3,192,128]{4,3,2,1,0:T(8,128)(2,1)S(1)} custom-call(s32[2]{0:T(128)S(1)} %slice_reduce_fusion.bound_ref, bf16[8,2,3,192,128]{4,3,2,1,0:T(8,128)(2,1)S(1)} %copy-done.2, bf16[8,2,192,128]{3,2,1,0:T(8,128)(2,1)S(1)} %bitcast.86, f32[2,2,1,1536]{3,2,1,0:T(1,128)S(1)} %get-tuple-element.15.log_ref), custom_call_target="tpu_custom_call" | custom-call | tf_op jit(solution)/shard_map/attend_backward/pallas_call | solution.py:367
  558.7 2.0 slice_convert_fusion.2
  560.7 4.0 copy.40
  564.7 3.7 reshape.267
  568.5 3.6 copy.44
  572.1 3.7 reshape.270
  575.8 4.0 copy.41
  579.8 3.7 reshape.268
  583.6 2.3 multiply_add_fusion.5
  586.1 1.7 copy-done.4
  588.0 7.5 constant_dynamic-update-slice_fusion.1
  595.6 3.4 fusion.34
  601.3 4.5 convolution_convert_fusion.4
  606.2 8.0 convolution_convert_fusion.3
  614.3 11.2 %convolution_convert_fusion = bf16[4096,1024]{1,0:T(8,128)(2,1)} fusion(bf16[384,1024]{1,0:T(8,128)(2,1)} %copy-done.31, f32[384,4096]{1,0:T(8,128)} %fusion.43), kind=kOutput, calls=%fused_computation.2 | convolution fusion | flops 3239575552 | bytes 15466496 | tf_op jit(solution)/shard_map/dot_general | solution.py:24
  625.8 10.1 convolution_convert_fusion.1
  636.0 2.9 constant_dynamic-update-slice_fusion
  641.4 1.4 multiply_dynamic-update-slice_fusion
  642.8 6.9 convolution_convert_fusion.2
  649.7 37.5 %psum.65 = bf16[2,2,6144]{2,1,0:T(2,128)(2,1)S(1)} all-reduce(bf16[2,2,6144]{2,1,0:T(2,128)(2,1)S(1)} %convolution_convert_fusion.2), channel_id=1, replica_groups=mesh['grp'=4,'seq'=8] {'seq'}, use_global_device_ids=true, to_apply=%region_14.15 | all-reduce | flops 24576 | bytes 98304 | tf_op jit(solution)/shard_map/psum | solution.py:570
  687.2 1.8 fusion
  689.0 45.8 %reduce-scatter.8.cloned.1.call-done = bf16[128,3072]{1,0:T(8,128)(2,1)} async-done(((bf16[1024,3072]{1,0:T(8,128)(2,1)}), bf16[128,3072]{1,0:T(8,128)(2,1)}) %reduce-scatter.8.cloned.1.call-update) | async-done | bytes 786448 | tf_op jit(solution)/shard_map/reduce_scatter | solution.py:581
  734.8 90.0 %reduce-scatter.14.cloned.1.call-done = bf16[512,1024]{1,0:T(8,128)(2,1)} async-done(((bf16[4096,1024]{1,0:T(8,128)(2,1)}), bf16[512,1024]{1,0:T(8,128)(2,1)}) %reduce-scatter.14.cloned.1.call-update) | async-done | bytes 1048592 | tf_op jit(solution)/shard_map/reduce_scatter | solution.py:590
  824.8 90.4 %reduce-scatter.12.cloned.1.call-done = bf16[128,4096]{1,0:T(8,128)(2,1)} async-done(((bf16[1024,4096]{1,0:T(8,128)(2,1)}), bf16[128,4096]{1,0:T(8,128)(2,1)}) %reduce-scatter.12.cloned.1.call-update) | async-done | bytes 1048592 | tf_op jit(solution)/shard_map/reduce_scatter | solution.py:587
  915.8 12.9 %all_gather.23 = f32[4,1024]{1,0:T(4,128)S(1)} all-gather(f32[4,128]{1,0:T(4,128)S(1)} %fusion.45), channel_id=1, replica_groups=mesh['grp'=4,'seq'=8] {'seq'}, dimensions={1}, use_global_device_ids=true | all-gather | bytes 18432 | tf_op jit(solution)/shard_map/all_gather | solution.py:572
  929.4 4.0 fusion.44
  933.4 1.9 fusion.39
  935.3 106.9 %all-reduce.10.cloned.1.call-done = (bf16[256,1024]{1,0:T(8,128)(2,1)}, bf16[128,6144]{1,0:T(8,128)(2,1)}, bf16[128,3072]{1,0:T(8,128)(2,1)}, bf16[128,1024]{1,0...) async-done(((bf16[256,1024]{1,0:T(8,128)(2,1)}, bf16[128,6144]{1,0:T(8,128)(2,1)}, bf16[128,3072]{1,0:T(8,128)(2,1)}, bf16[128,1024]{1,0:T(8,128)(2,1)}, ...) | async-done | bytes 5242896 | tf_op jit(solution)/shard_map/psum | solution.py:595
  1042.2 2.3 convert_element_type.188
  1044.5 1.8 convert_element_type.194
  1047.6 1.5 convert_element_type.196
  1049.1 1.6 convert_element_type.198
  1051.1 2.0 convert_element_type.190
  (140 shorter events, 27.6 us)
Async XLA Ops:
  7.2 1.6 copy-start
  7.2 58.1 %all-reduce.8.cloned.1.call-start = ((), (), s32[]{:S(2)}) async-start(), calls=%async_computation.6 | async-start | bytes 196608 | tf_op jit(solution)/shard_map/psum | solution.py:451
  9.1 4.0 copy-start.28
  9.1 46.8 %copy-start.29 = (s32[2,2]{1,0:T(2,128)S(1)}, s32[2,2]{1,0:T(2,128)}, u32[]{:S(2)}) copy-start(s32[2,2]{1,0:T(2,128)} %param.15) | copy-start | bytes 52
  9.9 105.9 %all-gather.6.cloned.1.call-start = ((), (), s32[]{:S(2)}) async-start(), calls=%async_computation.5 | async-start | bytes 4718592 | tf_op jit(solution)/shard_map/all_gather | solution.py:415
  10.6 170.4 %all-gather.8.cloned.1.call-start = ((), (), s32[]{:S(2)}) async-start(), calls=%async_computation.7 | async-start | bytes 7077888 | tf_op jit(solution)/shard_map/all_gather | solution.py:416
  11.3 339.1 %all-gather.10.cloned.1.call-start = ((), (), s32[]{:S(2)}) async-start(), calls=%async_computation.8 | async-start | bytes 2359296 | tf_op jit(solution)/shard_map/all_gather | solution.py:417
  11.9 346.9 %all-gather.12.cloned.1.call-start = ((), (), s32[]{:S(2)}) async-start(), calls=%async_computation.9 | async-start | bytes 9437184 | tf_op jit(solution)/shard_map/all_gather | solution.py:418
  12.5 423.4 %all-gather.14.cloned.1.call-start = ((), (), s32[]{:S(2)}) async-start(), calls=%async_computation.10 | async-start | bytes 9437184 | tf_op jit(solution)/shard_map/all_gather | solution.py:419
  13.1 675.9 %reduce-scatter.10.cloned.1.call-start = ((), (), s32[]{:S(2)}) async-start(), calls=%async_computation.13 | async-start | bytes 2359296 | tf_op jit(solution)/shard_map/reduce_scatter | solution.py:584
  59.1 56.7 %copy-start.13 = (bf16[2,192,2048]{2,1,0:T(8,128)(2,1)}, bf16[2,192,2048]{2,1,0:T(8,128)(2,1)S(1)}, u32[]{:S(2)}) copy-start(bf16[2,192,2048]{2,1,0:T(8,128)(2,1)S(1)} %pad_maximum_fusion.1) | copy-start | bytes 4718596
  119.8 1.1 copy-start.3
  123.3 62.4 %copy-start.19 = (bf16[384,1024]{1,0:T(8,128)(2,1)}, bf16[384,1024]{1,0:T(8,128)(2,1)S(1)}, u32[]{:S(2)}) copy-start(bf16[384,1024]{1,0:T(8,128)(2,1)S(1)} %fusion.9) | copy-start | bytes 2359300
  185.7 3.2 copy-start.11
  347.6 1.4 copy-start.1
  435.9 12.3 %copy-start.30 = (f32[384,4096]{1,0:T(8,128)S(1)}, f32[384,4096]{1,0:T(8,128)}, u32[]{:S(2)}) copy-start(f32[384,4096]{1,0:T(8,128)} %fusion.43) | copy-start | bytes 18874372
  435.9 22.7 %slice-start = ((s8[9437184]{0:T(1024)(128)(4,1)}), s8[4194304]{0:T(1024)(128)(4,1)S(1)}, s32[]{:S(2)}) async-start(s8[9437184]{0:T(1024)(128)(4,1)} %bitcast.94), calls=%async_computation.17 | async-start | bytes 8388608
  447.3 0.9 copy-start.31
  447.3 19.8 %copy-start.8 = (f32[384,1024]{1,0:T(8,128)}, f32[384,1024]{1,0:T(8,128)S(1)}, u32[]{:S(2)}) copy-start(f32[384,1024]{1,0:T(8,128)S(1)} %get-tuple-element.29) | copy-start | bytes 4718596
  448.2 10.4 slice-start.1
  448.2 10.4 slice-start.2
  466.0 1.2 copy-start.5
  467.2 2.3 copy-start.12
  468.6 0.9 copy-start.26
  472.1 216.9 %reduce-scatter.6.cloned.1.call-start = ((), (), s32[]{:S(2)}) async-start(), calls=%async_computation.11 | async-start | bytes 4718592 | tf_op jit(solution)/shard_map/reduce_scatter | solution.py:578
  475.0 1.7 copy-start.2
  585.9 2.0 copy-start.4
  585.9 2.2 copy-start.20
  586.0 9.6 copy-start.21
  586.1 9.5 copy-start.22
  595.6 3.4 copy-start.7
  595.6 3.4 copy-start.10
  599.0 2.3 copy-start.14
  600.4 0.9 copy-start.24
  605.8 129.0 %reduce-scatter.8.cloned.1.call-start = ((), (), s32[]{:S(2)}) async-start(), calls=%async_computation.12 | async-start | bytes 7077888 | tf_op jit(solution)/shard_map/reduce_scatter | solution.py:581
  614.3 210.6 %reduce-scatter.14.cloned.1.call-start = ((), (), s32[]{:S(2)}) async-start(), calls=%async_computation.15 | async-start | bytes 9437184 | tf_op jit(solution)/shard_map/reduce_scatter | solution.py:590
  625.6 289.7 %reduce-scatter.12.cloned.1.call-start = ((), (), s32[]{:S(2)}) async-start(), calls=%async_computation.14 | async-start | bytes 9437184 | tf_op jit(solution)/shard_map/reduce_scatter | solution.py:587
  635.9 406.3 %all-reduce.10.cloned.1.call-start = ((), (), s32[]{:S(2)}) async-start(), calls=%async_computation.16 | async-start | bytes 10485760 | tf_op jit(solution)/shard_map/psum | solution.py:595
  636.0 2.9 copy-start.6
  638.9 1.9 copy-start.9
  638.9 2.5 copy-start.15
  915.2 13.5 %copy-start.27 = (f32[2,2,1024]{2,1,0:T(2,128)S(1)}, f32[2,2,1024]{2,1,0:T(2,128)}, u32[]{:S(2)}) copy-start(f32[2,2,1024]{2,1,0:T(2,128)} %param.14) | copy-start | bytes 49156
  915.2 14.2 %copy-start.25 = (bf16[384,1024]{1,0:T(8,128)(2,1)S(1)}, bf16[384,1024]{1,0:T(8,128)(2,1)}, u32[]{:S(2)}) copy-start(bf16[384,1024]{1,0:T(8,128)(2,1)} %copy-done.24) | copy-start | bytes 2359300
  1042.2 4.1 copy-start.23
  1042.2 5.4 copy-start.18
  1047.6 1.5 copy-start.17
  1049.1 1.9 copy-start.16
Sparse Core Ops, SparseCore 0:
  10.9 54.3 all-reduce.7
  67.0 48.7 all-gather.5
  117.5 63.4 all-gather.7
  182.5 27.7 all-gather.9
  211.9 141.1 all-gather.11
  354.6 81.2 all-gather.13
  472.2 53.4 reduce-scatter.9
  605.9 57.8 reduce-scatter.5
  666.2 68.5 reduce-scatter.7
  737.0 87.7 reduce-scatter.13
  827.2 87.9 reduce-scatter.11
  920.8 121.4 all-reduce.9

commit v2 on v1

--- a/solution.py
+++ b/solution.py
@@ -1,4 +1,5 @@
 import functools
+import math
 
 import jax
 import jax.numpy as jnp
@@ -397,6 +398,148 @@
     )(bounds, kept, grad, log_total)
 
 
+def gather_kernel(plane, seq_count, count, *refs):
+    shards, fulls = refs[:count], refs[count:2 * count]
+    own_sem, z_send, z_recv, first_send, first_recv, second_send, second_recv, core_send, core_recv = refs[2 * count:]
+    rows_y, cols_x = plane
+    grp = lax.axis_index("grp")
+    me = lax.axis_index("seq")
+    gy, gx = grp // cols_x, lax.rem(grp, cols_x)
+    layers = seq_count // 2
+    layer, core = me // 2, lax.rem(me, 2)
+    beside = [gy * cols_x + lax.rem(gx + step, cols_x) for step in range(1, cols_x)]
+    beside_from = [lax.rem(gx + cols_x - step, cols_x) for step in range(1, cols_x)]
+    along = [lax.rem(gy + step, rows_y) * cols_x + gx for step in range(1, rows_y)]
+    along_from = [lax.rem(gy + rows_y - step, rows_y) for step in range(1, rows_y)]
+    lines = [lax.rem(layer + step, layers) * 2 + core for step in range(1, layers)]
+    line_from = [lax.rem(layer + layers - step, layers) * 2 + core for step in range(1, layers)]
+    partner = layer * 2 + 1 - core
+    enter(
+        [(grp, line) for line in lines]
+        + [(other, me) for other in beside + along]
+        + [(grp, partner)]
+    )
+    started = []
+
+    def push(src, dst, sends, recvs, slot, device):
+        copy = pltpu.make_async_remote_copy(
+            src, dst, sends.at[slot], recvs.at[slot], device_id=device, device_id_type=MESH
+        )
+        copy.start()
+        started.append(copy)
+        return copy
+
+    def piece(index, owner, y_from, y_many, x_from, x_many):
+        height = fulls[index].shape[1] // rows_y
+        width = fulls[index].shape[2] // (2 * cols_x)
+        return fulls[index].at[
+            owner,
+            pl.ds(pl.multiple_of(y_from * height, height), y_many * height),
+            pl.ds(pl.multiple_of(x_from * width, width), x_many * width),
+        ]
+
+    own = []
+    line_copies = []
+    for index in range(count):
+        height = shards[index].shape[0] // rows_y
+        width = shards[index].shape[1] // cols_x
+        source = shards[index].at[
+            pl.ds(pl.multiple_of(gy * height, height), height),
+            pl.ds(pl.multiple_of(gx * width, width), width),
+        ]
+        line_copies.append([
+            push(source, piece(index, me, gy, 1, 2 * gx, 2), z_send, z_recv, (index, step), (grp, line))
+            for step, line in enumerate(lines)
+        ])
+    for index in range(count):
+        copy = pltpu.make_async_copy(shards[index], fulls[index].at[me], own_sem.at[index])
+        copy.start()
+        own.append(copy)
+        push(shards[index], fulls[index].at[me], core_send, core_recv, (index, 0), (grp, partner))
+    spread = {}
+
+    def first(index, step):
+        line_copies[index][step].wait_recv()
+        owner = line_from[step]
+        spread[index, step] = [
+            push(part, part, first_send, first_recv, (index, step, 0, hop), (other, me))
+            for hop, other in enumerate(beside)
+            for part in [piece(index, owner, gy, 1, 2 * gx, 1)]
+        ] + [
+            push(part, part, first_send, first_recv, (index, step, 1, hop), (other, me))
+            for hop, other in enumerate(along)
+            for part in [piece(index, owner, gy, 1, 2 * gx + 1, 1)]
+        ]
+
+    def second(index, step):
+        for copy in spread[index, step]:
+            copy.wait_recv()
+        owner = line_from[step]
+        copies = []
+        for hop, other in enumerate(along):
+            for place, column in enumerate([gx] + beside_from):
+                part = piece(index, owner, gy, 1, 2 * column, 1)
+                copies.append(push(part, part, second_send, second_recv, (index, step, 0, hop, place), (other, me)))
+        for hop, other in enumerate(beside):
+            part = piece(index, owner, 0, rows_y, 2 * gx + 1, 1)
+            copies.append(push(part, part, second_send, second_recv, (index, step, 1, hop, 0), (other, me)))
+        spread[index, step] = copies
+
+    def third(index, step):
+        for copy in spread[index, step]:
+            copy.wait_recv()
+        part = fulls[index].at[line_from[step]]
+        spread[index, step] = [push(part, part, core_send, core_recv, (index, step + 1), (grp, partner))]
+
+    jobs = [(index, step) for index in range(count) for step in range(layers - 1)]
+    lag = layers - 1
+    for turn in range(len(jobs) + 2 * lag):
+        if turn < len(jobs):
+            first(*jobs[turn])
+        if 0 <= turn - lag < len(jobs):
+            second(*jobs[turn - lag])
+        if 0 <= turn - 2 * lag < len(jobs):
+            third(*jobs[turn - 2 * lag])
+    for copy in started:
+        copy.wait_send()
+    for copies in spread.values():
+        for copy in copies:
+            copy.wait_recv()
+    for index in range(count):
+        pltpu.make_async_remote_copy(
+            shards[index], fulls[index].at[me], core_send.at[index, 0], core_recv.at[index, 0],
+            device_id=(grp, partner), device_id_type=MESH,
+        ).wait_recv()
+        own[index].wait()
+
+
+def gather(collective, *shards):
+    seq_count = lax.axis_size("seq")
+    side = math.isqrt(lax.axis_size("grp"))
+    plane = (side, side)
+    layers = seq_count // 2
+    count = len(shards)
+    anywhere = pl.BlockSpec(memory_space=pl.ANY)
+    dma = pltpu.SemaphoreType.DMA
+    hops = max(side - 1, 1)
+    outs = pl.pallas_call(
+        functools.partial(gather_kernel, plane, seq_count, count),
+        out_shape=tuple(jax.ShapeDtypeStruct((seq_count,) + part.shape, part.dtype) for part in shards),
+        in_specs=[anywhere] * count,
+        out_specs=(anywhere,) * count,
+        scratch_shapes=[
+            dma((count,)),
+            dma((count, layers - 1)), dma((count, layers - 1)),
+            dma((count, layers - 1, 2, hops)), dma((count, layers - 1, 2, hops)),
+            dma((count, layers - 1, 2, hops, side)), dma((count, layers - 1, 2, hops, side)),
+            dma((count, layers)), dma((count, layers)),
+        ],
+        compiler_params=pltpu.CompilerParams(collective_id=collective, has_side_effects=True),
+        name="gather_weights_%d" % collective,
+    )(*shards)
+    return tuple(full.reshape(seq_count * part.shape[0], part.shape[1]) for full, part in zip(outs, shards))
+
+
 def shards(
     frames,
     shortcut,
@@ -411,13 +554,7 @@
     expand,
     contract,
 ):
-    gathered = (
-        lax.all_gather(combine, "seq", axis=0, tiled=True),
-        lax.all_gather(projection, "seq", axis=0, tiled=True),
-        lax.all_gather(readout, "seq", axis=0, tiled=True),
-        lax.all_gather(expand, "seq", axis=0, tiled=True),
-        lax.all_gather(contract, "seq", axis=0, tiled=True),
-    )
+    gathered = gather(3, combine, projection, readout, expand, contract)
     combine_full, projection_full, readout_full, expand_full, contract_full = (
         gathered
     )

time: 1070 us -> 968 us (0.905)
  waiting for transfers between devices: 509 us -> 333 us
  Pallas kernels: 218 us -> 302 us
    all_gather x5 -> x0, waiting for transfers between devices: 166 us -> none  [the longest x1 66.7 us: shards(): lax.all_gather(contract, 'seq', axis=0, tiled=True)]
    pallas_call x0 -> x1, Pallas kernels: none -> 131 us  [gather(): pl.pallas_call(functools.partial(gather_kernel, plane, seq_count, count),...]
    pallas_call x1, Pallas kernels: 136 us -> 87.5 us  [attend_forward(): pl.pallas_call(functools.partial(forward_kernel, seq_count), out_shape=(j...]
  transfers between devices with their start and end apart: 12 -> 7, of which waited for: 8 -> 4; matrix products, arithmetic and copies ran while one was open for 16% -> 11% of each run, Pallas kernels for 21% -> 22%
where the time goes in v2:
time: 968 us; the launch traced here: 958 us
  waiting for transfers between devices  333 us (34%)
  Pallas kernels  302 us (31%)
  matrix products  116 us (12%)
  blocking collectives  92.7 us (10%)
  local copies, waits for them, and re-layouts  56.7 us (6%)
  other arithmetic  40.9 us (4%)
  between operations  15.9 us (2%)
    pallas_call x1, Pallas kernels, gather(): pl.pallas_call(functools.partial(gather_kernel, plane, seq_count, count),...  131 us
    psum x1, waiting for transfers between devices, shards(): lax.psum(scattered[0].astype(jnp.bfloat16), 'grp').astype(jnp.float32)  107 us
    reduce_scatter x1, waiting for transfers between devices, shards(): lax.psum_scatter(expand_part.astype(jnp.bfloat16), 'seq', scatter_dimensi...  90.3 us
    reduce_scatter x1, waiting for transfers between devices, shards(): lax.psum_scatter(contract_part.astype(jnp.bfloat16), 'seq', scatter_dimen...  90 us
    pallas_call x1, Pallas kernels, attend_forward(): pl.pallas_call(functools.partial(forward_kernel, seq_count), out_shape=(j...  87.5 us
    pallas_call x1, Pallas kernels, attend_backward(): pl.pallas_call(functools.partial(backward_kernel, seq_count), out_shape=j...  82.8 us
    reduce_scatter x1, waiting for transfers between devices, shards(): lax.psum_scatter(projection_part.astype(jnp.bfloat16), 'seq', scatter_dim...  45.7 us
    psum x1, blocking collectives, shards(): kept_total = lax.psum(jnp.sum(kept_float), ('grp', 'seq'))  42.2 us
  transfers between devices with their start and end apart: 7, of which 4 were waited for; matrix products, arithmetic and copies ran while one was open for 11% of the time, Pallas kernels for 22%

profile of v2, /device:TPU:0, one launch (start us, length us, event | category | flops | bytes accessed | tf_op | source)
XLA Modules:
  0.0 957.8 jit_solution(3790623299311995618)
XLA Ops:
  10.0 1.3 convert_reduce_fusion
  11.3 42.2 %psum.64 = f32[]{:T(128)} all-reduce(f32[]{:T(128)} %convert_reduce_fusion), channel_id=1, replica_groups=mesh['grp'=4,'seq'=8] {'grp','seq'}, use_global_device_ids=true, to_apply=%region_9.10 | all-reduce | flops 1 | bytes 8 | tf_op jit(solution)/shard_map/psum | solution.py:570
  57.9 131.3 %gather_weights_3.1 = (bf16[8,256,1024]{2,1,0:T(8,128)(2,1)}, bf16[8,128,3072]{2,1,0:T(8,128)(2,1)}, bf16[8,128,1024]{2,1,0:T(8,128)(2,1)}, bf16[8,128,4096]{2,1,0:T(8,128)(2,1)}, bf16[8,512,1024]{2,1,0:T(8,128)(2,1)}) custom-call(bf16[256,1024]{1,0:T(8,128)(2,1)} %refs_0_.1, bf16[128,3072]{1,0:T(8,128)(2,1)} %refs_1_.1, bf16[128,1024]{1,0:T(8,128)(2,1)} %refs_2_.1, ...), custom_call_target="tpu_custom_call" | custom-call | tf_op jit(solution)/shard_map/gather_weights_3/pallas_call | solution.py:525
  189.3 4.5 fusion.40
  194.6 4.9 fusion.24
  200.0 7.5 fusion.42
  208.5 1.9 fusion.38
  210.3 1.9 copy.33
  212.2 1.3 copy.46
  214.6 3.0 copy.34
  217.6 1.8 subtract_convert_fusion.1
  219.4 1.4 pad_maximum_fusion.4
  220.8 3.3 convert_element_type.164
  224.2 1.9 copy.35
  226.0 3.1 convert_element_type.165
  229.1 1.9 copy.36
  231.0 1.9 maximum_bitcast_fusion.qkv_ref
  232.9 87.5 %attend_forward.1 = (bf16[8,2,3,192,128]{4,3,2,1,0:T(8,128)(2,1)S(1)}, bf16[8,2,192,128]{3,2,1,0:T(8,128)(2,1)S(1)}, f32[2,2,1,1536]{3,2,1,0:T(1,128)S(1)}) custom-call(s32[2]{0:T(128)S(1)} %slice_reduce_fusion.bound_ref, bf16[8,2,3,192,128]{4,3,2,1,0:T(8,128)(2,1)S(1)} %maximum_bitcast_fusion.qkv_ref), custom_call_target="tpu_custom_call" | custom-call | tf_op jit(solution)/shard_map/attend_forward/pallas_call | solution.py:224
  320.9 4.7 fusion.37
  326.0 2.4 fusion.8
  328.4 5.4 fusion.43
  333.8 10.8 %multiply_convert_fusion.2 = (bf16[384,1024]{1,0:T(8,128)(2,1)S(1)}, f32[384,1024]{1,0:T(8,128)S(1)}, bf16[384,1024]{1,0:T(8,128)(2,1)}, f32[384,1024]{1,0:T(8,128)}) fusion(f32[384,6144]{1,0:T(8,128)S(1)} %bitcast.100, bf16[2,192,1024]{2,1,0:T(8,128)(2,1)S(1)} %copy-done.32, f32[384,1024]{1,0:T(8,128)S(1)} %get-tuple-element.41, f32[384]{0:T(512)S(1)} %mul.364, ...), kind=kOutput, calls=%fused_computation.43 | convolution fusion | flops 3238526976 | bytes 23332352 | tf_op jit(solution)/shard_map/dot_general | solution.py:21
  344.6 10.8 %fusion.7 = bf16[384,4096]{1,0:T(8,128)(2,1)S(1)} fusion(f32[384,4096]{1,0:T(8,128)} %fusion.43, bf16[384,1024]{1,0:T(8,128)(2,1)S(1)} %get-tuple-element.38, bf16[4096,1024]{1,0:T(8,128)(2,1)} %bitcast.126), kind=kOutput, calls=%fused_computation.13 | convolution fusion | flops 3252682752 | bytes 18612224 | tf_op jit(solution)/shard_map/dot_general | solution.py:31
  355.5 7.4 multiply_reduce_fusion.1
  364.0 1.4 multiply_convert_fusion.1
  366.4 2.6 convolution_convert_fusion.5
  369.1 2.9 fusion.13
  372.3 1.3 copy-done.2
  373.6 82.8 %attend_backward.1 = bf16[8,2,3,192,128]{4,3,2,1,0:T(8,128)(2,1)S(1)} custom-call(s32[2]{0:T(128)S(1)} %slice_reduce_fusion.bound_ref, bf16[8,2,3,192,128]{4,3,2,1,0:T(8,128)(2,1)S(1)} %copy-done.2, bf16[8,2,192,128]{3,2,1,0:T(8,128)(2,1)S(1)} %bitcast.91, f32[2,2,1,1536]{3,2,1,0:T(1,128)S(1)} %get-tuple-element.25.log_ref), custom_call_target="tpu_custom_call" | custom-call | tf_op jit(solution)/shard_map/attend_backward/pallas_call | solution.py:368
  456.4 2.1 slice_convert_fusion.2
  458.5 4.0 copy.40
  462.5 3.8 reshape.287
  466.3 3.6 copy.44
  469.9 3.7 reshape.290
  473.6 4.0 copy.41
  477.6 3.8 reshape.288
  481.3 2.3 multiply_add_fusion.5
  483.9 1.7 copy-done.6
  485.8 7.4 constant_dynamic-update-slice_fusion.1
  493.2 3.4 fusion.34
  496.6 1.5 multiply_dynamic-update-slice_fusion.2
  499.0 4.5 convolution_convert_fusion.4
  503.7 8.0 convolution_convert_fusion.3
  511.8 11.2 %convolution_convert_fusion = bf16[4096,1024]{1,0:T(8,128)(2,1)} fusion(bf16[384,1024]{1,0:T(8,128)(2,1)} %copy-done.34, f32[384,4096]{1,0:T(8,128)} %fusion.43), kind=kOutput, calls=%fused_computation.2 | convolution fusion | flops 3239575552 | bytes 15466496 | tf_op jit(solution)/shard_map/dot_general | solution.py:25
  523.3 10.1 %convolution_convert_fusion.1 = bf16[1024,4096]{1,0:T(8,128)(2,1)} fusion(bf16[384,1024]{1,0:T(8,128)(2,1)} %copy-done.20, bf16[384,4096]{1,0:T(8,128)(2,1)} %copy-done.33), kind=kOutput, calls=%fused_computation.3 | convolution fusion | flops 3225419776 | bytes 12320768 | tf_op jit(solution)/shard_map/dot_general | solution.py:25
  533.5 2.9 constant_dynamic-update-slice_fusion
  536.5 1.6 multiply_dynamic-update-slice_fusion.1
  538.9 1.4 multiply_dynamic-update-slice_fusion
  540.4 6.9 convolution_convert_fusion.2
  547.3 37.5 %psum.65 = bf16[2,2,6144]{2,1,0:T(2,128)(2,1)S(1)} all-reduce(bf16[2,2,6144]{2,1,0:T(2,128)(2,1)S(1)} %convolution_convert_fusion.2), channel_id=1, replica_groups=mesh['grp'=4,'seq'=8] {'seq'}, use_global_device_ids=true, to_apply=%region_14.15 | all-reduce | flops 24576 | bytes 98304 | tf_op jit(solution)/shard_map/psum | solution.py:707
  584.7 1.8 fusion
  586.5 45.7 %reduce-scatter.8.cloned.1.call-done = bf16[128,3072]{1,0:T(8,128)(2,1)} async-done(((bf16[1024,3072]{1,0:T(8,128)(2,1)}), bf16[128,3072]{1,0:T(8,128)(2,1)}) %reduce-scatter.8.cloned.1.call-update) | async-done | bytes 786448 | tf_op jit(solution)/shard_map/reduce_scatter | solution.py:718
  632.2 90.0 %reduce-scatter.14.cloned.1.call-done = bf16[512,1024]{1,0:T(8,128)(2,1)} async-done(((bf16[4096,1024]{1,0:T(8,128)(2,1)}), bf16[512,1024]{1,0:T(8,128)(2,1)}) %reduce-scatter.14.cloned.1.call-update) | async-done | bytes 1048592 | tf_op jit(solution)/shard_map/reduce_scatter | solution.py:727
  722.2 90.3 %reduce-scatter.12.cloned.1.call-done = bf16[128,4096]{1,0:T(8,128)(2,1)} async-done(((bf16[1024,4096]{1,0:T(8,128)(2,1)}), bf16[128,4096]{1,0:T(8,128)(2,1)}) %reduce-scatter.12.cloned.1.call-update) | async-done | bytes 1048592 | tf_op jit(solution)/shard_map/reduce_scatter | solution.py:724
  813.1 13.0 %all_gather.3 = f32[4,1024]{1,0:T(4,128)S(1)} all-gather(f32[4,128]{1,0:T(4,128)S(1)} %fusion.45), channel_id=1, replica_groups=mesh['grp'=4,'seq'=8] {'seq'}, dimensions={1}, use_global_device_ids=true | all-gather | bytes 18432 | tf_op jit(solution)/shard_map/all_gather | solution.py:709
  826.8 4.0 fusion.44
  830.8 1.9 fusion.39
  832.7 107.0 %all-reduce.10.cloned.1.call-done = (bf16[256,1024]{1,0:T(8,128)(2,1)}, bf16[128,6144]{1,0:T(8,128)(2,1)}, bf16[128,3072]{1,0:T(8,128)(2,1)}, bf16[128,1024]{1,0...) async-done(((bf16[256,1024]{1,0:T(8,128)(2,1)}, bf16[128,6144]{1,0:T(8,128)(2,1)}, bf16[128,3072]{1,0:T(8,128)(2,1)}, bf16[128,1024]{1,0:T(8,128)(2,1)}, ...) | async-done | bytes 5242896 | tf_op jit(solution)/shard_map/psum | solution.py:732
  939.6 2.3 convert_element_type.188
  941.9 1.8 convert_element_type.194
  943.7 1.3 convert_element_type.192
  945.0 1.5 convert_element_type.196
  946.5 1.6 convert_element_type.198
  948.4 2.0 convert_element_type.190
  (137 shorter events, 17.6 us)
Async XLA Ops:
  7.2 1.7 copy-start
  7.2 49.5 %copy-start.22 = (bf16[2,192,1024]{2,1,0:T(8,128)(2,1)S(1)}, bf16[2,192,1024]{2,1,0:T(8,128)(2,1)}, u32[]{:S(2)}) copy-start(bf16[2,192,1024]{2,1,0:T(8,128)(2,1)} %param.13) | copy-start | bytes 2359300
  7.2 49.4 %copy-start.23 = (bf16[2,192,1024]{2,1,0:T(8,128)(2,1)S(1)}, bf16[2,192,1024]{2,1,0:T(8,128)(2,1)}, u32[]{:S(2)}) copy-start(bf16[2,192,1024]{2,1,0:T(8,128)(2,1)} %param.12) | copy-start | bytes 2359300
  7.2 187.4 %all-reduce.8.cloned.1.call-start = ((), (), s32[]{:S(2)}) async-start(), calls=%async_computation.5 | async-start | bytes 196608 | tf_op jit(solution)/shard_map/psum | solution.py:588
  9.9 576.6 %reduce-scatter.10.cloned.1.call-start = ((), (), s32[]{:S(2)}) async-start(), calls=%async_computation.8 | async-start | bytes 2359296 | tf_op jit(solution)/shard_map/reduce_scatter | solution.py:721
  189.3 5.1 copy-start.31
  193.8 5.7 copy-start.4
  199.5 7.9 copy-start.3
  200.0 7.5 copy-start.19
  232.8 88.1 %copy-start.5 = (f32[384,1024]{1,0:T(8,128)S(1)}, f32[384,1024]{1,0:T(8,128)}, u32[]{:S(2)}) copy-start(f32[384,1024]{1,0:T(8,128)} %copy-done.4) | copy-start | bytes 4718596
  232.8 88.1 %copy-start.13 = (bf16[8,128,1024]{2,1,0:T(8,128)(2,1)S(1)}, bf16[8,128,1024]{2,1,0:T(8,128)(2,1)}, u32[]{:S(2)}) copy-start(bf16[8,128,1024]{2,1,0:T(8,128)(2,1)} %get-tuple-element.21) | copy-start | bytes 6291460
  320.4 5.3 copy-start.1
  320.4 8.0 slice-start.3
  320.9 7.5 slice-start.4
  326.0 7.8 slice-start
  328.4 5.4 copy-start.20
  328.4 5.4 slice-start.1
  328.4 5.4 slice-start.2
  328.4 5.4 copy-start.32
  344.6 10.8 %copy-start.34 = (bf16[384,1024]{1,0:T(8,128)(2,1)}, bf16[384,1024]{1,0:T(8,128)(2,1)S(1)}, u32[]{:S(2)}) copy-start(bf16[384,1024]{1,0:T(8,128)(2,1)S(1)} %get-tuple-element.38) | copy-start | bytes 2359300
  344.6 19.4 %copy-start.10 = (f32[384,1024]{1,0:T(8,128)}, f32[384,1024]{1,0:T(8,128)S(1)}, u32[]{:S(2)}) copy-start(f32[384,1024]{1,0:T(8,128)S(1)} %get-tuple-element.39) | copy-start | bytes 4718596
  355.5 7.4 copy-start.33
  362.9 1.2 copy-start.7
  365.5 0.9 copy-start.29
  369.0 217.5 %reduce-scatter.6.cloned.1.call-start = ((), (), s32[]{:S(2)}) async-start(), calls=%async_computation.6 | async-start | bytes 4718592 | tf_op jit(solution)/shard_map/reduce_scatter | solution.py:715
  371.9 1.7 copy-start.2
  483.6 2.0 copy-start.6
  483.6 2.2 copy-start.21
  483.8 9.4 copy-start.24
  483.9 9.3 copy-start.25
  493.2 3.4 copy-start.9
  493.2 3.4 copy-start.12
  496.6 2.4 copy-start.14
  498.1 0.9 copy-start.27
  503.5 128.7 %reduce-scatter.8.cloned.1.call-start = ((), (), s32[]{:S(2)}) async-start(), calls=%async_computation.7 | async-start | bytes 7077888 | tf_op jit(solution)/shard_map/reduce_scatter | solution.py:718
  511.8 210.4 %reduce-scatter.14.cloned.1.call-start = ((), (), s32[]{:S(2)}) async-start(), calls=%async_computation.10 | async-start | bytes 9437184 | tf_op jit(solution)/shard_map/reduce_scatter | solution.py:727
  523.0 289.5 %reduce-scatter.12.cloned.1.call-start = ((), (), s32[]{:S(2)}) async-start(), calls=%async_computation.9 | async-start | bytes 9437184 | tf_op jit(solution)/shard_map/reduce_scatter | solution.py:724
  533.5 406.1 %all-reduce.10.cloned.1.call-start = ((), (), s32[]{:S(2)}) async-start(), calls=%async_computation.11 | async-start | bytes 10485760 | tf_op jit(solution)/shard_map/psum | solution.py:732
  533.5 3.0 copy-start.8
  536.5 1.8 copy-start.11
  536.5 2.5 copy-start.15
  812.5 13.6 %copy-start.30 = (f32[2,2,1024]{2,1,0:T(2,128)S(1)}, f32[2,2,1024]{2,1,0:T(2,128)}, u32[]{:S(2)}) copy-start(f32[2,2,1024]{2,1,0:T(2,128)} %param.14) | copy-start | bytes 49156
  812.5 14.3 %copy-start.28 = (bf16[384,1024]{1,0:T(8,128)(2,1)S(1)}, bf16[384,1024]{1,0:T(8,128)(2,1)}, u32[]{:S(2)}) copy-start(bf16[384,1024]{1,0:T(8,128)(2,1)} %copy-done.27) | copy-start | bytes 2359300
  939.6 4.1 copy-start.26
  939.6 5.4 copy-start.18
  945.0 1.5 copy-start.17
  946.5 1.9 copy-start.16
Sparse Core Ops, SparseCore 0:
  10.9 54.9 all-reduce.7
  369.1 53.5 reduce-scatter.9
  503.6 57.7 reduce-scatter.5
  563.7 68.4 reduce-scatter.7
  634.5 87.7 reduce-scatter.13
  724.5 87.9 reduce-scatter.11
  818.2 121.3 all-reduce.9

commit v3 on v2

--- a/solution.py
+++ b/solution.py
@@ -540,6 +540,250 @@
     return tuple(full.reshape(seq_count * part.shape[0], part.shape[1]) for full, part in zip(outs, shards))
 
 
+def add_rows(target, source, first_row, rows, first_col, cols):
+    step = 16
+    col = pl.multiple_of(first_col, 128)
+
+    def one(index, carry):
+        at = pl.ds(pl.multiple_of(first_row + index * step, step), step)
+        target[at, pl.ds(col, cols)] = target[at, pl.ds(col, cols)] + source[
+            pl.ds(pl.multiple_of(index * step, step), step), :
+        ]
+        return carry
+
+    lax.fori_loop(0, rows // step, one, 0)
+
+
+def reduce_kernel(plane, seq_count, count, *refs):
+    parts, outs = refs[:count], refs[count:2 * count]
+    rest = refs[2 * count:]
+    sums, partner_bufs, y_first, x_second, x_first, y_second, line_bufs = [
+        rest[index * count:(index + 1) * count] for index in range(7)
+    ]
+    load_sem, core_send, core_recv, first_send, first_recv, second_send, second_recv, z_send, z_recv, spread_send, spread_recv, late_send, late_recv = rest[7 * count:]
+    rows_y, cols_x = plane
+    grp = lax.axis_index("grp")
+    me = lax.axis_index("seq")
+    gy, gx = grp // cols_x, lax.rem(grp, cols_x)
+    layers = seq_count // 2
+    layer, core = me // 2, lax.rem(me, 2)
+    xs = [lax.rem(gx + step, cols_x) for step in range(1, cols_x)]
+    ys = [lax.rem(gy + step, rows_y) for step in range(1, rows_y)]
+    beside = [gy * cols_x + x for x in xs]
+    along = [y * cols_x + gx for y in ys]
+    beside_from = [lax.rem(gx + cols_x - step, cols_x) for step in range(1, cols_x)]
+    far = [lax.rem(layer + step, layers) for step in range(1, layers)]
+    partner = layer * 2 + 1 - core
+    enter(
+        [(grp, other * 2 + core) for other in far]
+        + [(other, me) for other in beside + along]
+        + [(grp, partner)]
+    )
+    started = []
+
+    def push(src, dst, sends, recvs, slot, device):
+        copy = pltpu.make_async_remote_copy(
+            src, dst, sends.at[slot], recvs.at[slot], device_id=device, device_id_type=MESH
+        )
+        copy.start()
+        started.append(copy)
+        return copy
+
+    def sizes(index):
+        _, rows, cols = parts[index].shape
+        return rows, cols, rows // rows_y, cols // (2 * cols_x)
+
+    def window(ref, row, rows, col, cols):
+        return ref.at[
+            pl.ds(pl.multiple_of(row, 16), rows), pl.ds(pl.multiple_of(col, 128), cols)
+        ]
+
+    order = far + [layer]
+    loads, swaps = {}, {}
+    for index in range(count):
+        for step, target in enumerate(order):
+            copy = pltpu.make_async_copy(
+                parts[index].at[target * 2 + core], sums[index].at[step], load_sem.at[index, step]
+            )
+            copy.start()
+            loads[index, step] = copy
+            swaps[index, step] = push(
+                parts[index].at[target * 2 + 1 - core], partner_bufs[index].at[step],
+                core_send, core_recv, (index, step), (grp, partner),
+            )
+    waiting = {}
+
+    def first(index, step):
+        rows, cols, height, width = sizes(index)
+        loads[index, step].wait()
+        swaps[index, step].wait_recv()
+        total = sums[index].at[step]
+        add_rows(total, partner_bufs[index].at[step], 0, rows, 0, cols)
+        copies = []
+        for hop, other in enumerate(along):
+            for column in range(cols_x):
+                copies.append(push(
+                    window(total, ys[hop] * height, height, 2 * column * width, width),
+                    y_first[index].at[step, hop, column],
+                    first_send, first_recv, (index, step, 0, hop, column), (other, me),
+                ))
+        for hop, other in enumerate(beside):
+            copies.append(push(
+                window(total, 0, rows, (2 * xs[hop] + 1) * width, width),
+                x_first[index].at[step, hop],
+                first_send, first_recv, (index, step, 1, hop, 0), (other, me),
+            ))
+        waiting[index, step] = copies
+
+    def second(index, step):
+        rows, cols, height, width = sizes(index)
+        for copy in waiting[index, step]:
+            copy.wait_recv()
+        total = sums[index].at[step]
+        for hop in range(rows_y - 1):
+            for column in range(cols_x):
+                add_rows(total, y_first[index].at[step, hop, column], gy * height, height, 2 * column * width, width)
+        for hop in range(cols_x - 1):
+            add_rows(total, x_first[index].at[step, hop], 0, rows, (2 * gx + 1) * width, width)
+        copies = []
+        for hop, other in enumerate(beside):
+            copies.append(push(
+                window(total, gy * height, height, 2 * xs[hop] * width, width),
+                x_second[index].at[step, hop],
+                second_send, second_recv, (index, step, 0, hop), (other, me),
+            ))
+        for hop, other in enumerate(along):
+            copies.append(push(
+                window(total, ys[hop] * height, height, (2 * gx + 1) * width, width),
+                y_second[index].at[step, hop],
+                second_send, second_recv, (index, step, 1, hop), (other, me),
+            ))
+        waiting[index, step] = copies
+
+    def third(index, step):
+        rows, cols, height, width = sizes(index)
+        for copy in waiting[index, step]:
+            copy.wait_recv()
+        total = sums[index].at[step]
+        for hop in range(cols_x - 1):
+            add_rows(total, x_second[index].at[step, hop], gy * height, height, 2 * gx * width, width)
+        for hop in range(rows_y - 1):
+            add_rows(total, y_second[index].at[step, hop], gy * height, height, (2 * gx + 1) * width, width)
+        waiting[index, step] = []
+        if step < layers - 1:
+            waiting[index, step].append(push(
+                window(total, gy * height, height, 2 * gx * width, 2 * width),
+                line_bufs[index].at[step], z_send, z_recv, (index, step), (grp, order[step] * 2 + core),
+            ))
+
+    def fourth(index):
+        rows, cols, height, width = sizes(index)
+        for step in range(layers - 1):
+            for copy in waiting[index, step]:
+                copy.wait_recv()
+        total = sums[index].at[layers - 1]
+        low_row = gy * height
+        low_col = pl.multiple_of(2 * gx * width, 128)
+
+        def one(turn, carry):
+            at = pl.ds(pl.multiple_of(low_row + turn * 16, 16), 16)
+            off = pl.ds(pl.multiple_of(turn * 16, 16), 16)
+            value = total[at, pl.ds(low_col, 2 * width)].astype(jnp.float32)
+            for step in range(layers - 1):
+                value = value + line_bufs[index][step, off, :].astype(jnp.float32)
+            outs[index][at, pl.ds(low_col, 2 * width)] = value.astype(jnp.bfloat16)
+            return carry
+
+        lax.fori_loop(0, height // 16, one, 0)
+        copies = []
+        for hop, other in enumerate(beside):
+            part = window(outs[index], low_row, height, 2 * gx * width, width)
+            copies.append(push(part, part, spread_send, spread_recv, (index, 0, hop), (other, me)))
+        for hop, other in enumerate(along):
+            part = window(outs[index], low_row, height, (2 * gx + 1) * width, width)
+            copies.append(push(part, part, spread_send, spread_recv, (index, 1, hop), (other, me)))
+        waiting[index] = copies
+
+    def fifth(index):
+        rows, cols, height, width = sizes(index)
+        for copy in waiting[index]:
+            copy.wait_recv()
+        copies = []
+        for hop, other in enumerate(along):
+            for place, column in enumerate([gx] + beside_from):
+                part = window(outs[index], gy * height, height, 2 * column * width, width)
+                copies.append(push(part, part, late_send, late_recv, (index, 0, hop, place), (other, me)))
+        for hop, other in enumerate(beside):
+            part = window(outs[index], 0, rows, (2 * gx + 1) * width, width)
+            copies.append(push(part, part, late_send, late_recv, (index, 1, hop, 0), (other, me)))
+        waiting[index] = copies
+
+    jobs = [(index, step) for index in range(count) for step in range(layers)]
+    lag = layers // 2
+    for turn in range(len(jobs) + 6 * lag):
+        if turn < len(jobs):
+            first(*jobs[turn])
+        if 0 <= turn - lag < len(jobs):
+            second(*jobs[turn - lag])
+        if 0 <= turn - 2 * lag < len(jobs):
+            third(*jobs[turn - 2 * lag])
+        done = turn - 4 * lag
+        if 0 <= done < len(jobs) and done % layers == layers - 1:
+            fourth(done // layers)
+        done = turn - 6 * lag
+        if 0 <= done < len(jobs) and done % layers == layers - 1:
+            fifth(done // layers)
+    for copy in started:
+        copy.wait_send()
+    for index in range(count):
+        for copy in waiting[index]:
+            copy.wait_recv()
+
+
+def reduce_shares(collective, *parts):
+    seq_count = lax.axis_size("seq")
+    side = math.isqrt(lax.axis_size("grp"))
+    layers = seq_count // 2
+    count = len(parts)
+    parts = [part.reshape(seq_count, part.shape[0] // seq_count, part.shape[1]) for part in parts]
+    anywhere = pl.BlockSpec(memory_space=pl.ANY)
+    vmem = pl.BlockSpec(memory_space=pltpu.VMEM)
+    dma = pltpu.SemaphoreType.DMA
+    hops = max(side - 1, 1)
+
+    def buffers(lead, row_cut, col_cut):
+        return [
+            pltpu.VMEM(lead + (part.shape[1] // row_cut, part.shape[2] // col_cut), jnp.bfloat16)
+            for part in parts
+        ]
+
+    return pl.pallas_call(
+        functools.partial(reduce_kernel, (side, side), seq_count, count),
+        out_shape=tuple(jax.ShapeDtypeStruct(part.shape[1:], part.dtype) for part in parts),
+        in_specs=[anywhere] * count,
+        out_specs=(vmem,) * count,
+        scratch_shapes=buffers((layers,), 1, 1)
+        + buffers((layers,), 1, 1)
+        + buffers((layers, hops, side), side, 2 * side)
+        + buffers((layers, hops), side, 2 * side)
+        + buffers((layers, hops), 1, 2 * side)
+        + buffers((layers, hops), side, 2 * side)
+        + buffers((layers - 1,), side, side)
+        + [
+            dma((count, layers)), dma((count, layers)), dma((count, layers)),
+            dma((count, layers, 2, hops, side)), dma((count, layers, 2, hops, side)),
+            dma((count, layers, 2, hops)), dma((count, layers, 2, hops)),
+            dma((count, layers - 1)), dma((count, layers - 1)),
+            dma((count, 2, hops)), dma((count, 2, hops)),
+            dma((count, 2, hops, side)), dma((count, 2, hops, side)),
+        ],
+        compiler_params=pltpu.CompilerParams(
+            collective_id=collective, has_side_effects=True, vmem_limit_bytes=60 * 1024 * 1024
+        ),
+        name="reduce_shares_%d" % collective,
+    )(*parts)
+
+
 def shards(
     frames,
     shortcut,
@@ -710,32 +954,21 @@
         product_right(utter_rows, modulation), "seq", axis=1, tiled=True
     ).reshape(group_count, utter_count, width)
     time_grad = silu_pull(condition_grad)[0]
-    modulation_part = product_left(condition_part, utter_rows)
-    scattered = (
-        lax.psum_scatter(
-            combine_part.astype(jnp.bfloat16), "seq", scatter_dimension=0, tiled=True
-        ).astype(jnp.float32),
-        lax.psum_scatter(
-            projection_part.astype(jnp.bfloat16), "seq", scatter_dimension=0, tiled=True
-        ).astype(jnp.float32),
-        lax.psum_scatter(
-            readout_part.astype(jnp.bfloat16), "seq", scatter_dimension=0, tiled=True
-        ).astype(jnp.float32),
-        lax.psum_scatter(
-            expand_part.astype(jnp.bfloat16), "seq", scatter_dimension=0, tiled=True
-        ).astype(jnp.float32),
-        lax.psum_scatter(
-            contract_part.astype(jnp.bfloat16), "seq", scatter_dimension=0, tiled=True
-        ).astype(jnp.float32),
-    )
-    summed = (
-        lax.psum(scattered[0].astype(jnp.bfloat16), "grp").astype(jnp.float32),
-        lax.psum(modulation_part.astype(jnp.bfloat16), "grp").astype(jnp.float32),
-        lax.psum(scattered[1].astype(jnp.bfloat16), "grp").astype(jnp.float32),
-        lax.psum(scattered[2].astype(jnp.bfloat16), "grp").astype(jnp.float32),
-        lax.psum(scattered[3].astype(jnp.bfloat16), "grp").astype(jnp.float32),
-        lax.psum(scattered[4].astype(jnp.bfloat16), "grp").astype(jnp.float32),
-    )
+    utter_all = lax.all_gather(utter_rows, "grp", axis=0, tiled=True)
+    condition_all = lax.all_gather(condition_part, "grp", axis=0, tiled=True)
+    modulation_grad = product_left(condition_all, utter_all)
+    combine_grad, projection_grad, readout_grad, expand_grad, contract_grad = [
+        share.astype(jnp.float32)
+        for share in reduce_shares(
+            4,
+            combine_part.astype(jnp.bfloat16),
+            projection_part.astype(jnp.bfloat16),
+            readout_part.astype(jnp.bfloat16),
+            expand_part.astype(jnp.bfloat16),
+            contract_part.astype(jnp.bfloat16),
+        )
+    ]
+    summed = (combine_grad, modulation_grad, projection_grad, readout_grad, expand_grad, contract_grad)
     return (
         output.astype(jnp.bfloat16).reshape(split_shape),
         frames_grad,

time: 968 us -> 775 us (0.80)
  waiting for transfers between devices: 333 us -> 0.02 us
  Pallas kernels: 302 us -> 448 us
  blocking collectives: 92.7 us -> 113 us
  matrix products: 116 us -> 106 us
    reduce_scatter x5 -> x0, waiting for transfers between devices: 226 us -> none  [the longest x1 90.3 us: shards(): lax.psum_scatter(expand_part.astype(jnp.bfloat16), 'seq', scatter_dimensi...]
    pallas_call x0 -> x1, Pallas kernels: none -> 165 us  [reduce_shares(): pl.pallas_call(functools.partial(reduce_kernel, (side, side), seq_count,...]
    psum x1 -> x0, waiting for transfers between devices: 107 us -> none  [shards(): lax.psum(scattered[0].astype(jnp.bfloat16), 'grp').astype(jnp.float32)]
    all_gather x0 -> x2, blocking collectives: none -> 18.3 us  [the longest x1 9.29 us: shards(): utter_all = lax.all_gather(utter_rows, 'grp', axis=0, tiled=True)]
    pallas_call x1, Pallas kernels: 82.8 us -> 72.8 us  [attend_backward(): pl.pallas_call(functools.partial(backward_kernel, seq_count), out_shape=j...]
  transfers between devices with their start and end apart: 7 -> 1, of which waited for: 4 -> 0; matrix products, arithmetic and copies ran while one was open for 11% -> 1% of each run, Pallas kernels for 22% -> 17%
where the time goes in v3:
time: 775 us; the launch traced here: 768 us
  Pallas kernels  448 us (58%)
  blocking collectives  113 us (15%)
  matrix products  106 us (14%)
  local copies, waits for them, and re-layouts  51.1 us (7%)
  other arithmetic  33.3 us (4%)
  between operations  15.7 us (2%)
    pallas_call x1, Pallas kernels, reduce_shares(): pl.pallas_call(functools.partial(reduce_kernel, (side, side), seq_count,...  165 us
    pallas_call x1, Pallas kernels, gather(): pl.pallas_call(functools.partial(gather_kernel, plane, seq_count, count),...  130 us
    pallas_call x1, Pallas kernels, attend_forward(): pl.pallas_call(functools.partial(forward_kernel, seq_count), out_shape=(j...  80.3 us
    pallas_call x1, Pallas kernels, attend_backward(): pl.pallas_call(functools.partial(backward_kernel, seq_count), out_shape=j...  72.8 us
    psum x1, blocking collectives, shards(): kept_total = lax.psum(jnp.sum(kept_float), ('grp', 'seq'))  41.5 us
    psum x1, blocking collectives, shards(): utter_grad = lax.psum(utter_part.astype(jnp.bfloat16), 'seq')  40.9 us
    dot_general x6, matrix products, product_left(): lax.dot_general(first_op, second_op, (((0,), (0,)), ((), ())), preferred_...  35.3 us
    dot_general x6, matrix products, product_right(): lax.dot_general(first_op, second_op, (((1,), (1,)), ((), ())), preferred_...  31.4 us
  transfers between devices with their start and end apart: 1, of which 0 were waited for; matrix products, arithmetic and copies ran while one was open for 1% of the time, Pallas kernels for 17%

profile of v3, /device:TPU:0, one launch (start us, length us, event | category | flops | bytes accessed | tf_op | source)
XLA Modules:
  0.0 767.6 jit_solution(12737245214684587022)
XLA Ops:
  7.3 0.9 add_divide_fusion
  8.2 0.7 fusion.24
  9.2 0.7 reshape.285
  9.9 0.8 reduce_window_sum.11
  10.8 0.7 sub.52
  11.6 1.3 pad_maximum_fusion.1
  12.9 129.8 %gather_weights_3.1 = (bf16[8,256,1024]{2,1,0:T(8,128)(2,1)}, bf16[8,128,3072]{2,1,0:T(8,128)(2,1)}, bf16[8,128,1024]{2,1,0:T(8,128)(2,1)}, bf16[8,128,4096]{2,1,0:T(8,128)(2,1)}, bf16[8,512,1024]{2,1,0:T(8,128)(2,1)}) custom-call(bf16[256,1024]{1,0:T(8,128)(2,1)} %refs_0_.1, bf16[128,3072]{1,0:T(8,128)(2,1)} %refs_1_.1, bf16[128,1024]{1,0:T(8,128)(2,1)} %refs_2_.1, ...), custom_call_target="tpu_custom_call" | custom-call | tf_op jit(solution)/shard_map/gather_weights_3/pallas_call | solution.py:525
  142.7 4.5 fusion.39
  148.4 41.5 %psum.22 = f32[]{:T(128)} all-reduce(f32[]{:T(128)} %convert_reduce_fusion), channel_id=1, replica_groups=mesh['grp'=4,'seq'=8] {'grp','seq'}, use_global_device_ids=true, to_apply=%region_9.10 | all-reduce | flops 1 | bytes 8 | tf_op jit(solution)/shard_map/psum | solution.py:814
  191.0 9.0 %all-gather = bf16[4,4,128]{2,1,0:T(4,128)(2,1)S(1)} all-gather(bf16[1,4,128]{2,1,0:T(4,128)(2,1)S(1)} %bitcast.133), channel_id=1, replica_groups=mesh['grp'=4,'seq'=8] {'grp'}, dimensions={0}, use_global_device_ids=true | all-gather | bytes 5120 | tf_op jit(solution)/shard_map/all_gather | solution.py:958
  200.1 4.9 fusion.23
  205.4 7.4 fusion.41
  213.0 1.9 fusion.37
  215.0 1.1 copy.48
  216.1 1.9 copy.44
  218.0 3.0 copy.45
  221.0 1.8 subtract_convert_fusion.1
  222.8 1.4 pad_maximum_fusion.4
  224.2 3.1 convert_element_type.149
  227.3 1.9 copy.47
  229.2 3.1 convert_element_type.148
  232.2 1.9 copy.46
  234.1 1.9 maximum_bitcast_fusion.qkv_ref
  236.0 80.3 %attend_forward.1 = (bf16[8,2,3,192,128]{4,3,2,1,0:T(8,128)(2,1)S(1)}, bf16[8,2,192,128]{3,2,1,0:T(8,128)(2,1)S(1)}, f32[2,2,1,1536]{3,2,1,0:T(1,128)S(1)}) custom-call(s32[2]{0:T(128)S(1)} %slice_reduce_fusion.bound_ref, bf16[8,2,3,192,128]{4,3,2,1,0:T(8,128)(2,1)S(1)} %maximum_bitcast_fusion.qkv_ref), custom_call_target="tpu_custom_call" | custom-call | tf_op jit(solution)/shard_map/attend_forward/pallas_call | solution.py:224
  316.9 4.2 fusion.36
  321.4 2.4 fusion.7
  323.9 3.4 fusion.42
  327.4 11.2 %multiply_convert_fusion.2 = (bf16[384,1024]{1,0:T(8,128)(2,1)S(1)}, f32[384,1024]{1,0:T(8,128)S(1)}, bf16[384,1024]{1,0:T(8,128)(2,1)}, f32[384,1024]{1,0:T(8,128)}) fusion(f32[384,6144]{1,0:T(8,128)S(1)} %bitcast.104, bf16[2,192,1024]{2,1,0:T(8,128)(2,1)S(1)} %copy-done.33, f32[384,1024]{1,0:T(8,128)S(1)} %get-tuple-element.45, f32[384]{0:T(512)S(1)} %mul.364, ...), kind=kOutput, calls=%fused_computation.41 | convolution fusion | flops 3238526976 | bytes 23332352 | tf_op jit(solution)/shard_map/dot_general | solution.py:21
  338.5 14.7 %fusion.6 = bf16[384,4096]{1,0:T(8,128)(2,1)} fusion(f32[384,4096]{1,0:T(8,128)} %copy-done.34, bf16[384,1024]{1,0:T(8,128)(2,1)S(1)} %get-tuple-element.42, bf16[4096,1024]{1,0:T(8,128)(2,1)} %bitcast.139), kind=kOutput, calls=%fused_computation.11 | convolution fusion | flops 3252682752 | bytes 18612224 | tf_op jit(solution)/shard_map/dot_general | solution.py:31
  353.2 7.1 multiply_reduce_fusion.1
  361.5 1.7 multiply_convert_fusion.1
  363.6 1.0 fusion.12
  365.0 72.8 %attend_backward.1 = bf16[8,2,3,192,128]{4,3,2,1,0:T(8,128)(2,1)S(1)} custom-call(s32[2]{0:T(128)S(1)} %slice_reduce_fusion.bound_ref, bf16[8,2,3,192,128]{4,3,2,1,0:T(8,128)(2,1)S(1)} %get-tuple-element.29.kept_ref, bf16[8,2,192,128]{3,2,1,0:T(8,128)(2,1)S(1)} %bitcast.95, f32[2,2,1,1536]{3,2,1,0:T(1,128)S(1)} %get-tuple-element.30.log_ref), custom_call_target="tpu_custom_call" | custom-call | tf_op jit(solution)/shard_map/attend_backward/pallas_call | solution.py:368
  437.8 2.1 slice_convert_fusion.2
  439.8 3.6 copy.55
  443.5 3.5 reshape.314
  447.0 4.0 copy.51
  451.0 3.7 reshape.307
  454.8 4.0 copy.52
  458.8 4.1 reshape.308
  462.9 2.3 multiply_add_fusion.5
  465.5 1.2 copy-done.4
  466.8 6.3 constant_dynamic-update-slice_fusion.1
  473.2 2.3 fusion.33
  475.8 1.9 copy-done.32
  477.7 1.8 fusion.43
  479.5 4.4 convolution_convert_fusion.4
  483.9 8.7 %convolution_convert_fusion.3 = bf16[1024,3072]{1,0:T(8,128)(2,1)} fusion(bf16[384,1024]{1,0:T(8,128)(2,1)S(1)} %copy-done.20, bf16[384,1024]{0,1:T(8,128)(2,1)S(1)} %copy-done.23, bf16[384,1024]{0,1:T(8,128)(2,1)S(1)} %bitcast.127, bf16[384,1024]{0,1:T(8,128)(2,1)S(1)} %bitcast.129), kind=kOutput, calls=%fused_computation.13 | convolution fusion | flops 2426142720 | bytes 9437184 | tf_op jit(solution)/shard_map/dot_general | solution.py:25
  492.6 2.6 convolution_convert_fusion.5
  495.3 6.9 convolution_convert_fusion.1
  502.2 10.4 %convolution_convert_fusion = bf16[4096,1024]{1,0:T(8,128)(2,1)} fusion(bf16[384,1024]{1,0:T(8,128)(2,1)S(1)} %copy-done.37, f32[384,4096]{1,0:T(8,128)} %copy-done.34), kind=kOutput, calls=%fused_computation.2 | convolution fusion | flops 3239575552 | bytes 15466496 | tf_op jit(solution)/shard_map/dot_general | solution.py:25
  512.6 1.9 fusion.38
  515.1 1.1 copy-done.9
  517.0 3.3 convolution_convert_fusion.2
  520.3 40.9 %psum.23 = bf16[4,6144]{1,0:T(4,128)(2,1)S(1)} all-reduce(bf16[4,6144]{1,0:T(4,128)(2,1)S(1)} %reshape.299), channel_id=1, replica_groups=mesh['grp'=4,'seq'=8] {'seq'}, use_global_device_ids=true, to_apply=%region_14.15 | all-reduce | flops 24576 | bytes 98304 | tf_op jit(solution)/shard_map/psum | solution.py:951
  561.7 12.7 %all_gather.9 = f32[4,1024]{1,0:T(4,128)S(1)} all-gather(f32[4,128]{1,0:T(4,128)S(1)} %fusion.44), channel_id=1, replica_groups=mesh['grp'=4,'seq'=8] {'seq'}, dimensions={1}, use_global_device_ids=true | all-gather | bytes 18432 | tf_op jit(solution)/shard_map/all_gather | solution.py:953
  575.1 165.2 %reduce_shares_4.1 = (bf16[256,1024]{1,0:T(8,128)(2,1)}, bf16[128,3072]{1,0:T(8,128)(2,1)}, bf16[128,1024]{1,0:T(8,128)(2,1)}, bf16[128,4096]{1,0:T(8,128)(2,1)}, bf16[512,1024]{1,0:T(8,128)(2,1)}) custom-call(bf16[8,256,1024]{2,1,0:T(8,128)(2,1)} %bitcast.114, bf16[8,128,3072]{2,1,0:T(8,128)(2,1)} %bitcast.111, bf16[8,128,1024]{2,1,0:T(8,128)(2,1)} %bitcast.119, ...), custom_call_target="tpu_custom_call" | custom-call | tf_op jit(solution)/shard_map/reduce_shares_4/pallas_call | solution.py:760
  740.4 2.2 convert_element_type.176
  742.5 9.3 %all-gather.1 = bf16[4,4,6144]{2,1,0:T(4,128)(2,1)S(1)} all-gather(bf16[1,4,6144]{2,1,0:T(4,128)(2,1)S(1)} %bitcast.130), channel_id=1, replica_groups=mesh['grp'=4,'seq'=8] {'grp'}, dimensions={0}, use_global_device_ids=true | all-gather | bytes 245760 | tf_op jit(solution)/shard_map/all_gather | solution.py:957
  751.9 2.4 convert_element_type.177
  754.3 0.8 convert_element_type.178
  755.1 1.5 convert_element_type.179
  756.7 1.6 convert_element_type.180
  758.2 2.3 fusion.45
  (128 shorter events, 9.0 us)
Async XLA Ops:
  7.2 1.7 copy-start
  7.2 4.4 copy-start.24
  7.2 4.4 copy-start.25
  7.2 192.8 %all-reduce.6.cloned.1.call-start = ((), (), s32[]{:S(2)}) async-start(), calls=%async_computation | async-start | bytes 196608 | tf_op jit(solution)/shard_map/psum | solution.py:832
  142.7 5.0 copy-start.30
  142.7 48.1 %copy-start.31 = (s32[2,2]{1,0:T(2,128)S(1)}, s32[2,2]{1,0:T(2,128)}, u32[]{:S(2)}) copy-start(s32[2,2]{1,0:T(2,128)} %param.15) | copy-start | bytes 52
  147.3 57.7 %copy-start.2 = (f32[384,1024]{1,0:T(8,128)}, f32[384,1024]{1,0:T(8,128)S(1)}, u32[]{:S(2)}) copy-start(f32[384,1024]{1,0:T(8,128)S(1)} %get-tuple-element.74) | copy-start | bytes 4718596
  204.9 7.9 %copy-start.1 = (f32[2,192,6144]{2,1,0:T(8,128)}, f32[2,192,6144]{2,1,0:T(8,128)S(1)}, u32[]{:S(2)}) copy-start(f32[2,192,6144]{2,1,0:T(8,128)S(1)} %fusion.23) | copy-start | bytes 28311556
  205.4 7.5 copy-start.19
  236.0 80.8 %copy-start.3 = (f32[384,1024]{1,0:T(8,128)S(1)}, f32[384,1024]{1,0:T(8,128)}, u32[]{:S(2)}) copy-start(f32[384,1024]{1,0:T(8,128)} %copy-done.2) | copy-start | bytes 4718596
  236.0 80.8 %copy-start.13 = (bf16[8,128,1024]{2,1,0:T(8,128)(2,1)S(1)}, bf16[8,128,1024]{2,1,0:T(8,128)(2,1)}, u32[]{:S(2)}) copy-start(bf16[8,128,1024]{2,1,0:T(8,128)(2,1)} %get-tuple-element.26) | copy-start | bytes 6291460
  316.3 7.5 slice-start.3
  316.8 4.3 copy-start.11
  316.8 7.0 slice-start.4
  321.4 5.9 slice-start
  323.8 3.5 copy-start.21
  323.8 3.5 slice-start.1
  323.8 3.5 slice-start.2
  323.8 3.5 copy-start.33
  327.3 11.2 %copy-start.34 = (f32[384,4096]{1,0:T(8,128)}, f32[384,4096]{1,0:T(8,128)S(1)}, u32[]{:S(2)}) copy-start(f32[384,4096]{1,0:T(8,128)S(1)} %fusion.42) | copy-start | bytes 18874372
  338.5 14.7 %copy-start.36 = (bf16[384,1024]{1,0:T(8,128)(2,1)}, bf16[384,1024]{1,0:T(8,128)(2,1)S(1)}, u32[]{:S(2)}) copy-start(bf16[384,1024]{1,0:T(8,128)(2,1)S(1)} %get-tuple-element.42) | copy-start | bytes 2359300
  338.5 23.0 %copy-start.8 = (f32[384,1024]{1,0:T(8,128)}, f32[384,1024]{1,0:T(8,128)S(1)}, u32[]{:S(2)}) copy-start(f32[384,1024]{1,0:T(8,128)S(1)} %get-tuple-element.43) | copy-start | bytes 4718596
  360.3 1.2 copy-start.5
  361.5 2.1 copy-start.14
  363.2 1.5 copy-start.26
  465.2 1.4 copy-start.4
  465.2 1.6 copy-start.23
  473.1 2.3 copy-start.7
  473.2 2.4 copy-start.10
  475.5 2.2 copy-start.32
  477.7 1.8 copy-start.15
  479.5 4.4 copy-start.20
  483.9 8.7 %copy-start.12 = (bf16[2,192,8,128]{3,2,1,0:T(8,128)(2,1)S(1)}, bf16[2,192,8,128]{3,2,1,0:T(8,128)(2,1)}, u32[]{:S(2)}) copy-start(bf16[2,192,8,128]{3,2,1,0:T(8,128)(2,1)} %copy-done.11) | copy-start | bytes 2359300
  483.9 8.7 %copy-start.27 = (bf16[384,1024]{1,0:T(8,128)(2,1)S(1)}, bf16[384,1024]{1,0:T(8,128)(2,1)}, u32[]{:S(2)}) copy-start(bf16[384,1024]{1,0:T(8,128)(2,1)} %copy-done.26) | copy-start | bytes 2359300
  492.6 2.6 copy-start.22
  492.6 2.6 copy-start.35
  495.3 6.9 copy-start.37
  512.6 2.0 copy-start.6
  514.8 1.4 copy-start.9
  514.8 1.9 copy-start.16
  517.0 57.4 %copy-start.29 = (f32[2,2,1024]{2,1,0:T(2,128)S(1)}, f32[2,2,1024]{2,1,0:T(2,128)}, u32[]{:S(2)}) copy-start(f32[2,2,1024]{2,1,0:T(2,128)} %param.14) | copy-start | bytes 49156
  740.3 14.0 %copy-start.28 = (bf16[128,1024]{1,0:T(8,128)(2,1)S(1)}, bf16[128,1024]{1,0:T(8,128)(2,1)}, u32[]{:S(2)}) copy-start(bf16[128,1024]{1,0:T(8,128)(2,1)} %get-tuple-element.33) | copy-start | bytes 786436
  742.5 12.6 %copy-start.18 = (bf16[128,4096]{1,0:T(8,128)(2,1)S(1)}, bf16[128,4096]{1,0:T(8,128)(2,1)}, u32[]{:S(2)}) copy-start(bf16[128,4096]{1,0:T(8,128)(2,1)} %get-tuple-element.34) | copy-start | bytes 3145732
  754.3 2.4 copy-start.17
Sparse Core Ops, SparseCore 0:
  10.9 80.7 all-reduce.5

commit v4 on v1

--- a/solution.py
+++ b/solution.py
@@ -1,4 +1,5 @@
 import functools
+import math
 
 import jax
 import jax.numpy as jnp
@@ -120,11 +121,425 @@
     return (max(third - 1, 0) * size, min(third + 2, 3) * size)
 
 
-def forward_kernel(
-    seq_count, bound_ref, qkv_ref, kept_ref, mixture_ref, log_ref,
-    key_scr, query_scr, value_t_scr, score_scr, mix_t_scr, mix_scr,
-    send_sem, recv_sem, back_send_sem, back_recv_sem, local_sem,
-):
+class Place:
+    def __init__(self, plane, seq_count):
+        self.rows_y, self.cols_x = rows_y, cols_x = plane
+        self.grp, self.me = grp, me = lax.axis_index("grp"), lax.axis_index("seq")
+        self.gy, self.gx = gy, gx = grp // cols_x, lax.rem(grp, cols_x)
+        self.layers = layers = seq_count // 2
+        self.layer, self.core = layer, core = me // 2, lax.rem(me, 2)
+        self.xs = [lax.rem(gx + step, cols_x) for step in range(1, cols_x)]
+        self.ys = [lax.rem(gy + step, rows_y) for step in range(1, rows_y)]
+        self.beside = [gy * cols_x + x for x in self.xs]
+        self.along = [y * cols_x + gx for y in self.ys]
+        self.beside_from = [lax.rem(gx + cols_x - step, cols_x) for step in range(1, cols_x)]
+        self.far = [lax.rem(layer + step, layers) for step in range(1, layers)]
+        self.line_from = [lax.rem(layer + layers - step, layers) * 2 + core for step in range(1, layers)]
+        self.lines = [target * 2 + core for target in self.far]
+        self.partner = layer * 2 + 1 - core
+        self.others = [lax.rem(me + step, seq_count) for step in range(1, seq_count)]
+        self.groups = [lax.rem(grp + step, rows_y * cols_x) for step in range(1, rows_y * cols_x)]
+        self.started = []
+
+    def push(self, src, dst, sends, recvs, slot, device):
+        copy = pltpu.make_async_remote_copy(
+            src, dst, sends.at[slot], recvs.at[slot], device_id=device, device_id_type=MESH
+        )
+        copy.start()
+        self.started.append(copy)
+        return copy
+
+    def sent(self):
+        for copy in self.started:
+            copy.wait_send()
+        self.started = []
+
+
+def window(ref, row, rows, col, cols):
+    return ref.at[pl.ds(pl.multiple_of(row, 16), rows), pl.ds(pl.multiple_of(col, 128), cols)]
+
+
+def piece_segments(shapes, side, width):
+    base, found = 0, []
+    for rows, cols in shapes:
+        height, many = rows // side, cols // side // width
+        if many == 1:
+            half = width // 2
+            found.append([[(base, 0, height, half, 0)], [(base, half, height, half, half)]])
+        else:
+            blocks = [(base + spot * height, 0, height, width, spot * width) for spot in range(many)]
+            found.append([blocks[:many // 2], blocks[many // 2:]])
+        base += height * many
+    return found, base
+
+
+class PlaneGather:
+    def __init__(self, place, shards, pieces, segments, fulls, own_sem, first_send, first_recv, second_send, second_recv, core_send, core_recv):
+        self.place, self.shards, self.pieces, self.fulls = place, shards, pieces, fulls
+        self.segments = segments
+        self.own_sem = own_sem
+        self.first = (first_send, first_recv)
+        self.second = (second_send, second_recv)
+        self.core = (core_send, core_recv)
+        self.jobs = [(index, step) for step in range(place.layers - 1) for index in range(len(shards))]
+        self.waiting, self.local, self.own = {}, {}, []
+
+    def sizes(self, index):
+        _, rows, cols = self.fulls[index].shape
+        return rows, rows // self.place.rows_y, cols // (2 * self.place.cols_x)
+
+    def begin(self):
+        place = self.place
+        for index, step in self.jobs:
+            self.spread_first(index, step)
+        for index, shard in enumerate(self.shards):
+            copy = pltpu.make_async_copy(shard, self.fulls[index].at[place.me], self.own_sem.at[index, place.layers - 1, 0, 0])
+            copy.start()
+            push = place.push(shard, self.fulls[index].at[place.me], *self.core, (index, 0), (place.grp, place.partner))
+            self.own.append((copy, push))
+
+    def spread_first(self, index, step):
+        place = self.place
+        rows, height, width = self.sizes(index)
+        full = self.fulls[index].at[place.line_from[step]]
+        piece = self.pieces[step]
+        first_row, first_col = place.gy * height, 2 * place.gx * width
+        self.local[index, step] = []
+        self.waiting[index, step] = []
+        for half, partners in enumerate((place.beside, place.along)):
+            for spot, (row, col, rows, cols, off) in enumerate(self.segments[index][half]):
+                source = piece.at[pl.ds(row, rows), pl.ds(col, cols)]
+                part = window(full, first_row, rows, first_col + off, cols)
+                copy = pltpu.make_async_copy(source, part, self.own_sem.at[index, step, half, spot])
+                copy.start()
+                self.local[index, step].append(copy)
+                for hop, other in enumerate(partners):
+                    self.waiting[index, step].append(place.push(
+                        source, part, *self.first, (index, step, half, hop, spot), (other, place.me)
+                    ))
+
+    def spread_second(self, index, step):
+        place = self.place
+        rows, height, width = self.sizes(index)
+        for copy in self.local.get((index, step), []):
+            copy.wait()
+        for copy in self.waiting[index, step]:
+            copy.wait_recv()
+        full = self.fulls[index].at[place.line_from[step]]
+        copies = []
+        for hop, other in enumerate(place.along):
+            for spot, column in enumerate([place.gx] + place.beside_from):
+                part = window(full, place.gy * height, height, 2 * column * width, width)
+                copies.append(place.push(part, part, *self.second, (index, step, 0, hop, spot), (other, place.me)))
+        for hop, other in enumerate(place.beside):
+            part = window(full, 0, rows, (2 * place.gx + 1) * width, width)
+            copies.append(place.push(part, part, *self.second, (index, step, 1, hop, 0), (other, place.me)))
+        self.waiting[index, step] = copies
+
+    def over_core(self, index, step):
+        place = self.place
+        for copy in self.waiting[index, step]:
+            copy.wait_recv()
+        full = self.fulls[index].at[place.line_from[step]]
+        self.waiting[index, step] = [
+            place.push(full, full, *self.core, (index, step + 1), (place.grp, place.partner))
+        ]
+
+    def middle(self):
+        for job in self.jobs:
+            self.spread_second(*job)
+
+    def late(self):
+        return [functools.partial(self.over_core, *job) for job in self.jobs]
+
+    def finish(self):
+        self.place.sent()
+        for job in self.jobs:
+            for copy in self.waiting[job]:
+                copy.wait_recv()
+        for copy, push in self.own:
+            copy.wait()
+            push.wait_recv()
+
+
+def add_rows(target, source, first_row, rows, first_col, cols, out=None):
+    step = 16
+    col = pl.multiple_of(first_col, 128)
+
+    def one(index, carry):
+        at = pl.ds(pl.multiple_of(first_row + index * step, step), step)
+        off = pl.ds(pl.multiple_of(index * step, step), step)
+        value = target[at, pl.ds(col, cols)] + source[off, :]
+        if out is None:
+            target[at, pl.ds(col, cols)] = value
+        else:
+            out[off, :] = value
+        return carry
+
+    lax.fori_loop(0, rows // step, one, 0)
+
+
+def add_segments(target, source, first_row, first_col, segments, out):
+    for row, col, rows, cols, off in segments:
+        begin = off - segments[0][4]
+        add_rows(
+            target, source.at[:, pl.ds(begin, cols)], first_row, rows, first_col + off, cols,
+            out.at[pl.ds(row, rows), pl.ds(col, cols)],
+        )
+
+
+def plane_sum_scratch(parts, side):
+    layers = parts[0].shape[0] // 2
+    hops = max(side - 1, 1)
+    count = len(parts)
+    dma = pltpu.SemaphoreType.DMA
+
+    def buffers(lead, row_cut, col_cut):
+        return [
+            pltpu.VMEM(lead + (part.shape[1] // row_cut, part.shape[2] // col_cut), jnp.bfloat16)
+            for part in parts
+        ]
+
+    return (
+        buffers((layers,), 1, 1)
+        + buffers((layers,), 1, 1)
+        + buffers((layers, hops, side), side, 2 * side)
+        + buffers((layers, hops), side, 2 * side)
+        + buffers((layers, hops), 1, 2 * side)
+        + buffers((layers, hops), side, 2 * side)
+        + [
+            dma((count, layers)), dma((count, layers)), dma((count, layers)),
+            dma((count, layers, 2, hops, side)), dma((count, layers, 2, hops, side)),
+            dma((count, layers, 2, hops)), dma((count, layers, 2, hops)),
+        ]
+    )
+
+
+def by_owner(parts, seq_count):
+    return [part.reshape(seq_count, part.shape[0] // seq_count, part.shape[1]) for part in parts]
+
+
+class PlaneSum:
+    def __init__(self, place, parts, pieces, segments, buffers, semaphores):
+        self.place, self.parts, self.pieces, self.segments = place, parts, pieces, segments
+        count = len(parts)
+        self.sums, self.swapped, self.y_first, self.x_second, self.x_first, self.y_second = [
+            buffers[index * count:(index + 1) * count] for index in range(6)
+        ]
+        self.load_sem = semaphores[0]
+        self.core, self.first_sem, self.second_sem = semaphores[1:3], semaphores[3:5], semaphores[5:7]
+        self.order = place.far + [place.layer]
+        self.jobs = [(index, step) for index in range(count) for step in range(place.layers)]
+        self.loads, self.swaps, self.waiting = {}, {}, {}
+
+    def sizes(self, index):
+        _, rows, cols = self.parts[index].shape
+        return rows, cols, rows // self.place.rows_y, cols // (2 * self.place.cols_x)
+
+    def begin(self):
+        place = self.place
+        for index, step in self.jobs:
+            target = self.order[step]
+            copy = pltpu.make_async_copy(
+                self.parts[index].at[target * 2 + place.core], self.sums[index].at[step], self.load_sem.at[index, step]
+            )
+            copy.start()
+            self.loads[index, step] = copy
+            self.swaps[index, step] = place.push(
+                self.parts[index].at[target * 2 + 1 - place.core], self.swapped[index].at[step],
+                *self.core, (index, step), (place.grp, place.partner),
+            )
+
+    def first(self, index, step):
+        place = self.place
+        rows, cols, height, width = self.sizes(index)
+        self.loads[index, step].wait()
+        self.swaps[index, step].wait_recv()
+        total = self.sums[index].at[step]
+        add_rows(total, self.swapped[index].at[step], 0, rows, 0, cols)
+        copies = []
+        for hop, other in enumerate(place.along):
+            for column in range(place.cols_x):
+                copies.append(place.push(
+                    window(total, place.ys[hop] * height, height, 2 * column * width, width),
+                    self.y_first[index].at[step, hop, column],
+                    *self.first_sem, (index, step, 0, hop, column), (other, place.me),
+                ))
+        for hop, other in enumerate(place.beside):
+            copies.append(place.push(
+                window(total, 0, rows, (2 * place.xs[hop] + 1) * width, width),
+                self.x_first[index].at[step, hop],
+                *self.first_sem, (index, step, 1, hop, 0), (other, place.me),
+            ))
+        self.waiting[index, step] = copies
+
+    def second(self, index, step):
+        place = self.place
+        rows, cols, height, width = self.sizes(index)
+        for copy in self.waiting[index, step]:
+            copy.wait_recv()
+        total = self.sums[index].at[step]
+        for hop in range(place.rows_y - 1):
+            for column in range(place.cols_x):
+                add_rows(
+                    total, self.y_first[index].at[step, hop, column],
+                    place.gy * height, height, 2 * column * width, width,
+                )
+        for hop in range(place.cols_x - 1):
+            add_rows(total, self.x_first[index].at[step, hop], 0, rows, (2 * place.gx + 1) * width, width)
+        copies = []
+        for hop, other in enumerate(place.beside):
+            copies.append(place.push(
+                window(total, place.gy * height, height, 2 * place.xs[hop] * width, width),
+                self.x_second[index].at[step, hop],
+                *self.second_sem, (index, step, 0, hop), (other, place.me),
+            ))
+        for hop, other in enumerate(place.along):
+            copies.append(place.push(
+                window(total, place.ys[hop] * height, height, (2 * place.gx + 1) * width, width),
+                self.y_second[index].at[step, hop],
+                *self.second_sem, (index, step, 1, hop), (other, place.me),
+            ))
+        self.waiting[index, step] = copies
+
+    def third(self, index, step):
+        place = self.place
+        rows, cols, height, width = self.sizes(index)
+        for copy in self.waiting[index, step]:
+            copy.wait_recv()
+        self.waiting[index, step] = []
+        total = self.sums[index].at[step]
+        out = self.pieces[index][step]
+        row, col = place.gy * height, 2 * place.gx * width
+        for hop in range(place.cols_x - 1):
+            source = self.x_second[index].at[step, hop]
+            if hop == place.cols_x - 2:
+                add_segments(total, source, row, col, self.segments[index][0], out)
+            else:
+                add_rows(total, source, row, height, col, width)
+        for hop in range(place.rows_y - 1):
+            source = self.y_second[index].at[step, hop]
+            if hop == place.rows_y - 2:
+                add_segments(total, source, row, col, self.segments[index][1], out)
+            else:
+                add_rows(total, source, row, height, col + width, width)
+
+    def steps(self, stage):
+        return [functools.partial(stage, *job) for job in self.jobs]
+
+    def finish(self):
+        self.place.sent()
+
+
+class PlaneSpread:
+    def __init__(self, place, outs, first_send, first_recv, second_send, second_recv):
+        self.place, self.outs = place, outs
+        self.first_sem, self.second_sem = (first_send, first_recv), (second_send, second_recv)
+        self.waiting = {}
+
+    def sizes(self, index):
+        rows, cols = self.outs[index].shape
+        return rows, rows // self.place.rows_y, cols // (2 * self.place.cols_x)
+
+    def total(self, index, piece, others, segments):
+        place = self.place
+        rows, height, width = self.sizes(index)
+        row = place.gy * height
+        col = pl.multiple_of(2 * place.gx * width, 128)
+        for first, left, _, cols, off in segments[0] + segments[1]:
+
+            def one(turn, carry):
+                at = pl.ds(pl.multiple_of(first + turn * 16, 16), 16)
+                value = piece[at, pl.ds(left, cols)].astype(jnp.float32)
+                for other in others:
+                    value = value + other[at, pl.ds(left, cols)].astype(jnp.float32)
+                self.outs[index][
+                    pl.ds(pl.multiple_of(row + turn * 16, 16), 16), pl.ds(pl.multiple_of(col + off, 128), cols)
+                ] = value.astype(jnp.bfloat16)
+                return carry
+
+            lax.fori_loop(0, height // 16, one, 0)
+        copies = []
+        for hop, other in enumerate(place.beside):
+            part = window(self.outs[index], row, height, 2 * place.gx * width, width)
+            copies.append(place.push(part, part, *self.first_sem, (index, 0, hop), (other, place.me)))
+        for hop, other in enumerate(place.along):
+            part = window(self.outs[index], row, height, (2 * place.gx + 1) * width, width)
+            copies.append(place.push(part, part, *self.first_sem, (index, 1, hop), (other, place.me)))
+        self.waiting[index] = copies
+
+    def second(self, index):
+        place = self.place
+        rows, height, width = self.sizes(index)
+        for copy in self.waiting[index]:
+            copy.wait_recv()
+        copies = []
+        for hop, other in enumerate(place.along):
+            for spot, column in enumerate([place.gx] + place.beside_from):
+                part = window(self.outs[index], place.gy * height, height, 2 * column * width, width)
+                copies.append(place.push(part, part, *self.second_sem, (index, 0, hop, spot), (other, place.me)))
+        for hop, other in enumerate(place.beside):
+            part = window(self.outs[index], 0, rows, (2 * place.gx + 1) * width, width)
+            copies.append(place.push(part, part, *self.second_sem, (index, 1, hop, 0), (other, place.me)))
+        self.waiting[index] = copies
+
+    def finish(self, index):
+        for copy in self.waiting[index]:
+            copy.wait_recv()
+
+
+def small_rows(seq_count, values):
+    rows = jnp.concatenate([values, jnp.zeros((32 - values.shape[0], values.shape[1]), jnp.float32)])
+    return rows.reshape(seq_count, 32 // seq_count, values.shape[1])
+
+
+class SmallSum:
+    def __init__(self, place, source, total, scratch, first_send, first_recv, second_send, second_recv):
+        self.place, self.source, self.total_ref, self.scratch = place, source, total, scratch
+        self.first_sem, self.second_sem = (first_send, first_recv), (second_send, second_recv)
+
+    def begin(self):
+        place = self.place
+        self.waiting = [
+            place.push(self.source.at[other], self.scratch.at[step], *self.first_sem, step, (place.grp, other))
+            for step, other in enumerate(place.others)
+        ]
+
+    def middle(self):
+        place = self.place
+        value = self.source[place.me]
+        for step, copy in enumerate(self.waiting):
+            copy.wait_recv()
+            value = value + self.scratch[step]
+        self.total_ref[place.me] = value
+        part = self.total_ref.at[place.me]
+        self.waiting = [
+            place.push(part, part, *self.second_sem, step, (place.grp, other))
+            for step, other in enumerate(place.others)
+        ]
+
+    def finish(self):
+        for copy in self.waiting:
+            copy.wait_recv()
+
+
+def small_scratch(source):
+    seq_count = source.shape[0]
+    dma = pltpu.SemaphoreType.DMA
+    return [pltpu.VMEM((seq_count - 1,) + source.shape[1:], jnp.float32)] + [dma((seq_count - 1,))] * 4
+
+
+def forward_kernel(plane, seq_count, count, *refs):
+    layers = seq_count // 2
+    bound_ref, qkv_ref, shards = refs[0], refs[1], refs[2:2 + count]
+    refs = refs[2 + count:]
+    pieces, refs = refs[:layers - 1], refs[layers - 1:]
+    kept_ref, mixture_ref, log_ref, fulls = refs[0], refs[1], refs[2], refs[3:3 + count]
+    (
+        key_scr, query_scr, value_t_scr, score_scr, mix_t_scr, mix_scr,
+        send_sem, recv_sem, back_send_sem, back_recv_sem, local_sem,
+    ) = refs[3 + count:14 + count]
+    own_sem, first_send, first_recv, second_send, second_recv, core_send, core_recv = refs[14 + count:]
     group_count, local_rows, local_width = qkv_ref.shape[1], qkv_ref.shape[3], qkv_ref.shape[4]
     total_rows = seq_count * local_rows
     heads = local_width // HEAD_DIM
@@ -133,7 +548,8 @@
     others = [lax.rem(me + step, seq_count) for step in range(1, seq_count)]
     origins = [lax.rem(me + seq_count - step, seq_count) for step in range(1, seq_count)]
     block = min(256, total_rows // 3)
-    enter([(grp, other) for other in others])
+    place = Place(plane, seq_count)
+    enter([(grp, other) for other in others] + [(other, me) for other in place.beside + place.along])
     copies = []
     for group in range(group_count):
         own = pltpu.make_async_copy(qkv_ref.at[me, group], kept_ref.at[me, group], local_sem.at[group])
@@ -148,10 +564,23 @@
             copy.start()
             row.append(copy)
         copies.append(row)
+    side = place.cols_x
+    segments, _ = piece_segments(
+        [shard.shape for shard in shards], side, min(shard.shape[1] for shard in shards) // side
+    )
+    spread = PlaneGather(
+        place, shards, pieces, segments, fulls,
+        own_sem, first_send, first_recv, second_send, second_recv, core_send, core_recv,
+    )
+    spread.begin()
     back = []
     for group in range(group_count):
         for copy in copies[group]:
             copy.wait()
+        if group == 0:
+            spread.middle()
+            hooks = spread.late()
+            held = len(hooks) // 3
         boundary = bound_ref[group]
         keys = kept_ref[:, group, 1].reshape(total_rows, local_width)
         values = kept_ref[:, group, 2].reshape(total_rows, local_width)
@@ -160,7 +589,7 @@
         query_scr[:, local_width:] = utter_features(boundary, total_rows, False)
         value_t_scr[...] = values.astype(jnp.float32).T.astype(jnp.bfloat16)
 
-        def one_head(head, carry):
+        for head in range(heads):
             queries = kept_ref[:, group, 0].reshape(total_rows, local_width)
             query_scr[:, :local_width] = head_lanes(queries, head) * jnp.bfloat16(HEAD_DIM ** (-0.5))
             for third in range(3):
@@ -184,7 +613,7 @@
                     total = jnp.sum(total, axis=0, keepdims=True)
                     inverse = 1.0 / total
                     mixed = jnp.zeros((HEAD_DIM, block), jnp.float32)
-                    rows = pl.ds(pl.multiple_of(head * HEAD_DIM, HEAD_DIM), HEAD_DIM)
+                    rows = slice(head * HEAD_DIM, (head + 1) * HEAD_DIM)
                     for first in chunks:
                         weight = (score_scr[first:first + block, :] * inverse).astype(jnp.bfloat16)
                         mixed = mixed + dot_nn(value_t_scr[rows, first:first + block], weight)
@@ -193,9 +622,8 @@
                     return carry
 
                 lax.fori_loop(0, total_rows // 3 // block, one_block, 0)
-            return carry
-
-        lax.fori_loop(0, heads, one_head, 0)
+                if group > 0 and len(hooks) > held:
+                    hooks.pop(0)()
         mix_scr[group] = mix_t_scr[...].T.astype(jnp.bfloat16).reshape(seq_count, local_rows, local_width)
         own = pltpu.make_async_copy(
             mix_scr.at[group, me], mixture_ref.at[me, group], local_sem.at[group_count + group]
@@ -210,25 +638,34 @@
             )
             copy.start()
             back.append(copy)
+    for hook in hooks:
+        hook()
     for copy in back:
         copy.wait()
-
-
-def attend_forward(bounds, qkv):
+    spread.finish()
+
+
+def attend_forward(bounds, qkv, shards, pieces):
+    side = math.isqrt(lax.axis_size("grp"))
+    hops = max(side - 1, 1)
+    count = len(shards)
+    dma = pltpu.SemaphoreType.DMA
+    anywhere = pl.BlockSpec(memory_space=pl.ANY)
+    layers = qkv.shape[0] // 2
     seq_count, group_count, _, local_rows, local_width = qkv.shape
     total_rows = seq_count * local_rows
     heads = local_width // HEAD_DIM
     block = min(256, total_rows // 3)
     vmem = pl.BlockSpec(memory_space=pltpu.VMEM)
     return pl.pallas_call(
-        functools.partial(forward_kernel, seq_count),
+        functools.partial(forward_kernel, (side, side), seq_count, count),
         out_shape=(
             jax.ShapeDtypeStruct(qkv.shape, jnp.bfloat16),
             jax.ShapeDtypeStruct((seq_count, group_count, local_rows, local_width), jnp.bfloat16),
             jax.ShapeDtypeStruct((group_count, heads, 1, total_rows), jnp.float32),
-        ),
-        in_specs=[pl.BlockSpec(memory_space=pltpu.SMEM), pl.BlockSpec(memory_space=pl.ANY)],
-        out_specs=(vmem, vmem, vmem),
+        ) + tuple(jax.ShapeDtypeStruct((seq_count,) + part.shape, part.dtype) for part in shards),
+        in_specs=[pl.BlockSpec(memory_space=pltpu.SMEM)] + [anywhere] * (count + layers),
+        out_specs=(vmem, vmem, vmem) + (anywhere,) * count,
         scratch_shapes=[
             pltpu.VMEM((total_rows, local_width + 128), jnp.bfloat16),
             pltpu.VMEM((total_rows, local_width + 128), jnp.bfloat16),
@@ -241,20 +678,30 @@
             pltpu.SemaphoreType.DMA((group_count, seq_count - 1)),
             pltpu.SemaphoreType.DMA((group_count, seq_count - 1)),
             pltpu.SemaphoreType.DMA((2 * group_count,)),
+            dma((count, layers, 2, 2)),
+            dma((count, layers - 1, 2, hops, 2)), dma((count, layers - 1, 2, hops, 2)),
+            dma((count, layers - 1, 2, hops, side)), dma((count, layers - 1, 2, hops, side)),
+            dma((count, layers)), dma((count, layers)),
         ],
         compiler_params=pltpu.CompilerParams(
             collective_id=1, has_side_effects=True, vmem_limit_bytes=48 * 1024 * 1024
         ),
         name="attend_forward",
-    )(bounds, qkv)
-
-
-def backward_kernel(
-    seq_count, bound_ref, kept_ref, grad_ref, log_ref, out_ref,
-    taken_scr, key_scr, query_scr, key_t_scr, head_query_scr, head_grad_scr, prob_scr, weight_scr,
-    query_t_scr, key_sum_scr, value_sum_scr, back_scr,
-    send_sem, recv_sem, back_send_sem, back_recv_sem, local_sem,
-):
+    )(bounds, qkv, *shards, *pieces)
+
+
+def backward_kernel(plane, seq_count, count, *refs):
+    layers = seq_count // 2
+    bound_ref, kept_ref, grad_ref, log_ref = refs[:4]
+    parts, refs = refs[4:4 + count], refs[4 + count:]
+    out_ref, refs = refs[0], refs[1:]
+    pieces, refs = refs[:layers], refs[layers:]
+    (
+        taken_scr, key_scr, query_scr, key_t_scr, head_query_scr, head_grad_scr, prob_scr, weight_scr,
+        query_t_scr, key_sum_scr, value_sum_scr, back_scr,
+        send_sem, recv_sem, back_send_sem, back_recv_sem, local_sem,
+    ) = refs[:17]
+    buffers, semaphores = refs[17:17 + 6 * count], refs[17 + 6 * count:]
     group_count, local_rows, local_width = grad_ref.shape[1], grad_ref.shape[2], grad_ref.shape[3]
     total_rows = seq_count * local_rows
     heads = local_width // HEAD_DIM
@@ -262,7 +709,8 @@
     grp = lax.axis_index("grp")
     others = [lax.rem(me + step, seq_count) for step in range(1, seq_count)]
     block = min(256, total_rows // 3)
-    enter([(grp, other) for other in others])
+    place = Place(plane, seq_count)
+    enter([(grp, other) for other in others] + [(other, me) for other in place.beside + place.along])
     copies = []
     for group in range(group_count):
         own = pltpu.make_async_copy(grad_ref.at[me, group], taken_scr.at[me, group], local_sem.at[group])
@@ -277,6 +725,20 @@
             copy.start()
             row.append(copy)
         copies.append(row)
+    side = place.cols_x
+    segments, _ = piece_segments(
+        [part.shape[1:] for part in parts], side, min(part.shape[2] for part in parts) // side
+    )
+    plane_sum = PlaneSum(place, parts, [pieces] * count, segments, buffers, semaphores)
+    plane_sum.begin()
+    firsts = plane_sum.steps(plane_sum.first)
+    seconds = plane_sum.steps(plane_sum.second)
+    units = 3 * heads * group_count
+    plan = [[] for _ in range(units + 1)]
+    for spot, hook in enumerate(firsts):
+        plan[spot * (units // 2 - 1) // len(firsts)].append(hook)
+    for spot, hook in enumerate(seconds):
+        plan[units - 5 + spot * 6 // len(seconds)].append(hook)
     back = []
     for group in range(group_count):
         for copy in copies[group]:
@@ -290,7 +752,7 @@
         key_sum_scr[...] = jnp.zeros_like(key_sum_scr)
         value_sum_scr[...] = jnp.zeros_like(value_sum_scr)
 
-        def one_head(head, carry):
+        for head in range(heads):
             queries = head_lanes(kept_ref[:, group, 0].reshape(total_rows, local_width), head)
             head_query_scr[...] = queries
             query_scr[:, :local_width] = queries * jnp.bfloat16(HEAD_DIM ** (-0.5))
@@ -319,7 +781,7 @@
                         weight_scr[first:first + block, :] = weight_grad
                         row_dot = row_dot + fold_rows(prob * weight_grad, jnp.sum)
                     row_dot = jnp.sum(row_dot, axis=0, keepdims=True)
-                    rows = pl.ds(pl.multiple_of(head * HEAD_DIM, HEAD_DIM), HEAD_DIM)
+                    rows = slice(head * HEAD_DIM, (head + 1) * HEAD_DIM)
                     turned = jnp.zeros((HEAD_DIM, block), jnp.float32)
                     for first in chunks:
                         prob = prob_scr[first:first + block, :]
@@ -335,9 +797,8 @@
                     return carry
 
                 lax.fori_loop(0, total_rows // 3 // block, one_block, 0)
-            return carry
-
-        lax.fori_loop(0, heads, one_head, 0)
+                for hook in plan.pop(0):
+                    hook()
         shape = (seq_count, local_rows, local_width)
         back_scr[:, group, 0] = query_t_scr[...].T.astype(jnp.bfloat16).reshape(shape)
         back_scr[:, group, 1] = key_sum_scr[...].astype(jnp.bfloat16).reshape(shape)
@@ -355,22 +816,32 @@
             )
             copy.start()
             back.append(copy)
+    for hook in plan[0] + plane_sum.steps(plane_sum.third):
+        hook()
     for copy in back:
         copy.wait()
-
-
-def attend_backward(bounds, kept, grad, log_total):
+    plane_sum.finish()
+
+
+def attend_backward(bounds, kept, grad, log_total, parts):
+    side = math.isqrt(lax.axis_size("grp"))
+    count = len(parts)
+    layers = kept.shape[0] // 2
+    anywhere = pl.BlockSpec(memory_space=pl.ANY)
+    parts = by_owner(parts, kept.shape[0])
+    width = min(part.shape[2] for part in parts) // side
+    _, piece_rows = piece_segments([part.shape[1:] for part in parts], side, width)
     seq_count, group_count, _, local_rows, local_width = kept.shape
     total_rows = seq_count * local_rows
     block = min(256, total_rows // 3)
     vmem = pl.BlockSpec(memory_space=pltpu.VMEM)
     return pl.pallas_call(
-        functools.partial(backward_kernel, seq_count),
-        out_shape=jax.ShapeDtypeStruct(kept.shape, jnp.bfloat16),
-        in_specs=[
-            pl.BlockSpec(memory_space=pltpu.SMEM), vmem, pl.BlockSpec(memory_space=pl.ANY), vmem
-        ],
-        out_specs=vmem,
+        functools.partial(backward_kernel, (side, side), seq_count, count),
+        out_shape=(jax.ShapeDtypeStruct(kept.shape, jnp.bfloat16),) + tuple(
+            jax.ShapeDtypeStruct((piece_rows, width), jnp.bfloat16) for _ in range(layers)
+        ),
+        in_specs=[pl.BlockSpec(memory_space=pltpu.SMEM), vmem, anywhere, vmem] + [anywhere] * count,
+        out_specs=(vmem,) * (1 + layers),
         scratch_shapes=[
             pltpu.VMEM(grad.shape, jnp.bfloat16),
             pltpu.VMEM((total_rows, local_width + 128), jnp.bfloat16),
@@ -389,12 +860,297 @@
             pltpu.SemaphoreType.DMA((group_count, seq_count - 1)),
             pltpu.SemaphoreType.DMA((group_count, seq_count - 1)),
             pltpu.SemaphoreType.DMA((2 * group_count,)),
-        ],
+        ] + plane_sum_scratch(parts, side),
         compiler_params=pltpu.CompilerParams(
-            collective_id=2, has_side_effects=True, vmem_limit_bytes=48 * 1024 * 1024
+            collective_id=2, has_side_effects=True, vmem_limit_bytes=60 * 1024 * 1024
         ),
         name="attend_backward",
-    )(bounds, kept, grad, log_total)
+    )(bounds, kept, grad, log_total, *parts)
+
+
+class WholeGather(PlaneGather):
+    def __init__(self, place, shards, fulls, line_send, line_recv, *semaphores):
+        super().__init__(place, shards, None, None, fulls, *semaphores)
+        self.line = (line_send, line_recv)
+        self.jobs = [(index, step) for index in range(len(shards)) for step in range(place.layers - 1)]
+        self.lines = {}
+
+    def begin(self):
+        place = self.place
+        for index, step in self.jobs:
+            rows, height, width = self.sizes(index)
+            row, col = place.gy * height, 2 * place.gx * width
+            self.lines[index, step] = place.push(
+                window(self.shards[index], row, height, col, 2 * width),
+                window(self.fulls[index].at[place.me], row, height, col, 2 * width),
+                *self.line, (index, step), (place.grp, place.lines[step]),
+            )
+        for index, shard in enumerate(self.shards):
+            copy = pltpu.make_async_copy(shard, self.fulls[index].at[place.me], self.own_sem.at[index, place.layers - 1, 0, 0])
+            copy.start()
+            push = place.push(shard, self.fulls[index].at[place.me], *self.core, (index, 0), (place.grp, place.partner))
+            self.own.append((copy, push))
+
+    def spread_first(self, index, step):
+        place = self.place
+        rows, height, width = self.sizes(index)
+        self.lines[index, step].wait_recv()
+        full = self.fulls[index].at[place.line_from[step]]
+        row, col = place.gy * height, 2 * place.gx * width
+        self.waiting[index, step] = []
+        for half, partners in enumerate((place.beside, place.along)):
+            part = window(full, row, height, col + half * width, width)
+            for hop, other in enumerate(partners):
+                self.waiting[index, step].append(
+                    place.push(part, part, *self.first, (index, step, half, hop, 0), (other, place.me))
+                )
+
+    def steps(self):
+        lag = self.place.layers - 1
+        done = []
+        for turn in range(len(self.jobs) + 2 * lag):
+            if turn < len(self.jobs):
+                done.append(functools.partial(self.spread_first, *self.jobs[turn]))
+            if 0 <= turn - lag < len(self.jobs):
+                done.append(functools.partial(self.spread_second, *self.jobs[turn - lag]))
+            if 0 <= turn - 2 * lag < len(self.jobs):
+                done.append(functools.partial(self.over_core, *self.jobs[turn - 2 * lag]))
+        return done
+
+
+def gather_kernel(plane, seq_count, count, *refs):
+    shards, (partial_ref, token_ref), refs = refs[:count], refs[count:count + 2], refs[count + 2:]
+    fulls, (total_ref, tokens_ref), refs = refs[:count], refs[count:count + 2], refs[count + 2:]
+    token_scr, token_send, token_recv = refs[:3]
+    small_refs, refs = refs[3:8], refs[8:]
+    place = Place(plane, seq_count)
+    enter([(place.grp, other) for other in place.others] + [(other, place.me) for other in place.groups])
+    whole = WholeGather(place, shards, fulls, *refs)
+    whole.begin()
+    small = SmallSum(place, partial_ref, total_ref, *small_refs)
+    small.begin()
+    hooks = whole.steps()
+    for hook in hooks[:len(hooks) // 2]:
+        hook()
+    small.middle()
+    for hook in hooks[len(hooks) // 2:]:
+        hook()
+    small.finish()
+    last = total_ref.shape[1] - 1
+    token_scr[...] = token_ref[...]
+    token_scr[4:5, :] = total_ref[seq_count - 1, last:last + 1, :128]
+    tokens_ref[place.grp] = token_scr[...]
+    tokens = [
+        place.push(token_scr, tokens_ref.at[place.grp], token_send, token_recv, step, (other, place.me))
+        for step, other in enumerate(place.groups)
+    ]
+    whole.finish()
+    for copy in tokens:
+        copy.wait_recv()
+
+
+def gather(collective, partial, token, *shards):
+    grp_count = lax.axis_size("grp")
+    seq_count = lax.axis_size("seq")
+    side = math.isqrt(grp_count)
+    layers = seq_count // 2
+    count = len(shards)
+    anywhere = pl.BlockSpec(memory_space=pl.ANY)
+    vmem = pl.BlockSpec(memory_space=pltpu.VMEM)
+    dma = pltpu.SemaphoreType.DMA
+    hops = max(side - 1, 1)
+    outs = pl.pallas_call(
+        functools.partial(gather_kernel, (side, side), seq_count, count),
+        out_shape=tuple(
+            jax.ShapeDtypeStruct((seq_count,) + part.shape, part.dtype) for part in shards
+        ) + (
+            jax.ShapeDtypeStruct(partial.shape, jnp.float32),
+            jax.ShapeDtypeStruct((grp_count,) + token.shape, jnp.float32),
+        ),
+        in_specs=[anywhere] * count + [vmem] * 2,
+        out_specs=(anywhere,) * count + (vmem,) * 2,
+        scratch_shapes=[
+            pltpu.VMEM(token.shape, jnp.float32), dma((grp_count - 1,)), dma((grp_count - 1,))
+        ] + small_scratch(partial) + [
+            dma((count, layers - 1)), dma((count, layers - 1)),
+            dma((count, layers, 1, 1)),
+            dma((count, layers - 1, 2, hops, 1)), dma((count, layers - 1, 2, hops, 1)),
+            dma((count, layers - 1, 2, hops, side)), dma((count, layers - 1, 2, hops, side)),
+            dma((count, layers)), dma((count, layers)),
+        ],
+        compiler_params=pltpu.CompilerParams(collective_id=collective, has_side_effects=True),
+        name="gather_weights",
+    )(*shards, partial, token)
+    return outs[:count], outs[count], outs[count + 1]
+
+
+def reduce_kernel(plane, seq_count, count, done_count, *refs):
+    layers = seq_count // 2
+    parts, refs = refs[:count], refs[count:]
+    finished, refs = refs[:layers], refs[layers:]
+    utter_ref, modulation_ref, refs = refs[0], refs[1], refs[2:]
+    outs, refs = refs[:count + done_count], refs[count + done_count:]
+    total_ref, utters_ref, conditions_ref, refs = refs[0], refs[1], refs[2], refs[3:]
+    condition_scr, token_send, token_recv, last_send, last_recv, line_send, line_recv = refs[:7]
+    small_refs, spread_sems, refs = refs[7:12], refs[12:16], refs[16:]
+    lines, refs = refs[:count], refs[count:]
+    pieces = [refs[index * layers:(index + 1) * layers] for index in range(count)]
+    refs = refs[count * layers:]
+    buffers, semaphores = refs[:6 * count], refs[6 * count:]
+    place = Place(plane, seq_count)
+    enter([(place.grp, other) for other in place.others] + [(other, place.me) for other in place.groups])
+    side = place.cols_x
+    segments = [
+        piece_segments([part.shape[1:]], side, part.shape[2] // side)[0][0] for part in parts
+    ]
+    done_segments, _ = piece_segments(
+        [out.shape for out in outs[count:]], side, min(out.shape[1] for out in outs[count:]) // side
+    )
+    plane_sum = PlaneSum(place, parts, pieces, segments, buffers, semaphores)
+    plane_sum.begin()
+    small = SmallSum(place, utter_ref, total_ref, *small_refs)
+    small.begin()
+    spread = PlaneSpread(place, outs, *spread_sems)
+    late = []
+    for index in range(done_count):
+        spread.total(count + index, finished[0], finished[1:], done_segments[index])
+        late.append(functools.partial(spread.second, count + index))
+    arrived = {}
+
+    def along_line(index, step):
+        plane_sum.third(index, step)
+        if step < layers - 1:
+            arrived[index, step] = place.push(
+                pieces[index][step], lines[index].at[step], line_send, line_recv, (index, step),
+                (place.grp, place.lines[step]),
+            )
+
+    def last(index):
+        for step in range(layers - 1):
+            arrived[index, step].wait_recv()
+        spread.total(index, pieces[index][layers - 1], [lines[index].at[step] for step in range(layers - 1)], segments[index])
+
+    jobs = plane_sum.jobs
+    lag = layers
+    hooks = []
+    for turn in range(len(jobs) + 4 * lag):
+        if turn < len(jobs):
+            hooks.append(functools.partial(plane_sum.first, *jobs[turn]))
+        if turn >= lag + 1 and late:
+            hooks.append(late.pop(0))
+        if 0 <= turn - lag < len(jobs):
+            hooks.append(functools.partial(plane_sum.second, *jobs[turn - lag]))
+        if 0 <= turn - 2 * lag < len(jobs):
+            hooks.append(functools.partial(along_line, *jobs[turn - 2 * lag]))
+        done = turn - 3 * lag
+        if 0 <= done < len(jobs) and done % layers == layers - 1:
+            hooks.append(functools.partial(last, done // layers))
+        done = turn - 4 * lag
+        if 0 <= done < len(jobs) and done % layers == layers - 1:
+            hooks.append(functools.partial(spread.second, done // layers))
+    middle = len(hooks) // 3
+    for hook in hooks[:middle]:
+        hook()
+    small.middle()
+    for hook in hooks[middle:2 * middle]:
+        hook()
+    small.finish()
+    utters_ref[place.grp] = total_ref[...]
+    tokens = [
+        place.push(total_ref, utters_ref.at[place.grp], token_send, token_recv, step, (other, place.me))
+        for step, other in enumerate(place.groups)
+    ]
+    block, width = total_ref.shape[1], total_ref.shape[2]
+    rows = modulation_ref.shape[1] // width
+    utter_rows = utter_ref.shape[0] * block // 8
+    condition_scr[...] = jnp.zeros_like(condition_scr)
+    shard_rows = modulation_ref.shape[0]
+    for spot in range(rows * utter_rows // block):
+        part, row = spot * block // utter_rows, spot * block % utter_rows
+        condition_scr[row:row + block, :shard_rows] += dot_nt(
+            total_ref[spot].astype(jnp.bfloat16), modulation_ref[:, part * width:(part + 1) * width]
+        )
+    conditions_ref[place.me] = condition_scr[...]
+    tokens += [
+        place.push(condition_scr, conditions_ref.at[place.me], last_send, last_recv, step, (place.grp, other))
+        for step, other in enumerate(place.others)
+    ]
+    for hook in hooks[2 * middle:]:
+        hook()
+    place.sent()
+    for copy in tokens:
+        copy.wait_recv()
+    for index in range(count + done_count):
+        spread.finish(index)
+
+
+def reduce_shares(collective, utter, modulation, parts, finished, done_shapes):
+    grp_count = lax.axis_size("grp")
+    seq_count = lax.axis_size("seq")
+    side = math.isqrt(grp_count)
+    layers = seq_count // 2
+    count, done_count = len(parts), len(done_shapes)
+    parts = by_owner(parts, seq_count)
+    anywhere = pl.BlockSpec(memory_space=pl.ANY)
+    vmem = pl.BlockSpec(memory_space=pltpu.VMEM)
+    dma = pltpu.SemaphoreType.DMA
+    hops = max(side - 1, 1)
+    pieces = [
+        pltpu.VMEM((part.shape[1] // side, part.shape[2] // side), jnp.bfloat16)
+        for part in parts for _ in range(layers)
+    ]
+    lines = [
+        pltpu.VMEM((layers - 1, part.shape[1] // side, part.shape[2] // side), jnp.bfloat16) for part in parts
+    ]
+    total = count + done_count
+    outs = pl.pallas_call(
+        functools.partial(reduce_kernel, (side, side), seq_count, count, done_count),
+        out_shape=tuple(jax.ShapeDtypeStruct(part.shape[1:], jnp.bfloat16) for part in parts) + tuple(
+            jax.ShapeDtypeStruct(shape, jnp.bfloat16) for shape in done_shapes
+        ) + (
+            jax.ShapeDtypeStruct(utter.shape, jnp.float32),
+            jax.ShapeDtypeStruct((grp_count,) + utter.shape, jnp.float32),
+            jax.ShapeDtypeStruct((seq_count, 8, 128), jnp.float32),
+        ),
+        in_specs=[anywhere] * count + [vmem] * (layers + 2),
+        out_specs=(vmem,) * (total + 3),
+        scratch_shapes=[
+            pltpu.VMEM((8, 128), jnp.float32),
+            dma((grp_count - 1,)), dma((grp_count - 1,)),
+            dma((seq_count - 1,)), dma((seq_count - 1,)),
+            dma((count, layers - 1)), dma((count, layers - 1)),
+        ] + small_scratch(utter) + [
+            dma((total, 2, hops)), dma((total, 2, hops)),
+            dma((total, 2, hops, side)), dma((total, 2, hops, side)),
+        ] + lines + pieces + plane_sum_scratch(parts, side),
+        compiler_params=pltpu.CompilerParams(
+            collective_id=collective, has_side_effects=True, vmem_limit_bytes=60 * 1024 * 1024
+        ),
+        name="reduce_shares",
+    )(*parts, *finished, utter, modulation)
+    return outs[:total], outs[total + 1], outs[total + 2]
+
+
+def line_shift(values, step):
+    seq_count = lax.axis_size("seq")
+    turned = [(spot, (spot + 2 * step) % seq_count) for spot in range(seq_count)]
+    return lax.ppermute(values, "seq", turned)
+
+
+def line_pieces(shards):
+    side = math.isqrt(lax.axis_size("grp"))
+    layers = lax.axis_size("seq") // 2
+    grp = lax.axis_index("grp")
+    width = min(shard.shape[1] for shard in shards) // side
+    blocks = []
+    for shard in shards:
+        height, cols = shard.shape[0] // side, shard.shape[1] // side
+        for off in range(0, cols, width):
+            blocks.append(lax.dynamic_slice(
+                shard, (grp // side * height, lax.rem(grp, side) * cols + off), (height, width)
+            ))
+    joined = jnp.concatenate(blocks)
+    return [line_shift(joined, step) for step in range(1, layers)]
 
 
 def shards(
@@ -411,16 +1167,6 @@
     expand,
     contract,
 ):
-    gathered = (
-        lax.all_gather(combine, "seq", axis=0, tiled=True),
-        lax.all_gather(projection, "seq", axis=0, tiled=True),
-        lax.all_gather(readout, "seq", axis=0, tiled=True),
-        lax.all_gather(expand, "seq", axis=0, tiled=True),
-        lax.all_gather(contract, "seq", axis=0, tiled=True),
-    )
-    combine_full, projection_full, readout_full, expand_full, contract_full = (
-        gathered
-    )
     group_count = frames.shape[0]
     local_rows = frames.shape[1]
     width = HEADS * HEAD_DIM
@@ -430,7 +1176,6 @@
     all_frames = group_frames * lax.axis_size("grp") * group_count
     utter_count = time_embed.shape[1]
     kept_float = kept_mask.astype(jnp.float32).reshape(row_count)
-    kept_total = lax.psum(jnp.sum(kept_float), ("grp", "seq"))
     local_index = lax.axis_index("seq") * local_rows + jnp.arange(local_rows, dtype=jnp.int32)
 
     def local_info(length_row):
@@ -440,15 +1185,29 @@
     member_float = member_info[1].astype(jnp.float32)
     position = member_info[2]
     cos_table, sin_table = rotary_tables(position.reshape(row_count))
-    joined = jnp.concatenate([frames, shortcut], axis=2).reshape(row_count, 2 * width)
-    hidden = product(joined, combine_full)
     silu_value, silu_pull = jax.vjp(jax.nn.silu, time_embed)
     condition = silu_value.astype(jnp.bfloat16)
     shard_rows = modulation.shape[0]
+    utter_rows = group_count * utter_count
     condition_part = lax.dynamic_slice_in_dim(
         condition, lax.axis_index("seq") * shard_rows, shard_rows, 2
-    ).reshape(group_count * utter_count, shard_rows)
-    modulation_utter = lax.psum(product(condition_part, modulation), "seq").reshape(
+    ).reshape(utter_rows, shard_rows)
+    partial = small_rows(
+        seq_count, product(condition_part, modulation).reshape(6 * utter_rows, width)
+    )
+    partial = partial.at[seq_count - 1, 32 // seq_count - 1, 0].set(jnp.sum(kept_float))
+    token = jnp.zeros((8, 128), jnp.float32)
+    token = token.at[:utter_rows, :shard_rows].set(condition_part.astype(jnp.float32))
+    late_shards = (readout, expand, contract)
+    (combine_full, projection_full), partial_total, tokens = gather(3, partial, token, combine, projection)
+    late_pieces = line_pieces(lax.optimization_barrier((late_shards, tokens))[0])
+    combine_full = combine_full.reshape(2 * width, width)
+    projection_full = projection_full.reshape(width, 3 * width)
+    kept_total = jnp.sum(tokens[:, 4, 0])
+    condition_all = tokens[:, :utter_rows, :shard_rows].reshape(-1, shard_rows).astype(jnp.bfloat16)
+    joined = jnp.concatenate([frames, shortcut], axis=2).reshape(row_count, 2 * width)
+    hidden = product(joined, combine_full)
+    modulation_utter = partial_total.reshape(32, width)[:6 * utter_rows].reshape(
         group_count, utter_count, 6 * width
     )
     modulation_frame = jnp.einsum(
@@ -483,7 +1242,12 @@
         (3, 1, 0, 2, 4),
     )
     bounds = lengths[:, 0]
-    kept_heads, mixture_blocks, log_total = attend_forward(bounds, qkv)
+    kept_heads, mixture_blocks, log_total, *late_full = attend_forward(
+        bounds, qkv, late_shards, late_pieces
+    )
+    readout_full = late_full[0].reshape(width, width)
+    expand_full = late_full[1].reshape(width, -1)
+    contract_full = late_full[2].reshape(-1, width)
     mixture = jnp.transpose(mixture_blocks, (1, 2, 0, 3)).reshape(row_count, width)
     branch = product(mixture, readout_full)
     middle = hidden + gate_first * branch
@@ -501,7 +1265,7 @@
         * (output - target.reshape(row_count, width).astype(jnp.float32))
     )
     combine_back, projection_back, readout_back, expand_back, contract_back = (
-        gathered
+        combine_full, projection_full, readout_full, expand_full, contract_full
     )
     gate_second_grad = output_grad * contracted
     contracted_grad = (gate_second * output_grad).astype(jnp.bfloat16)
@@ -516,14 +1280,19 @@
     branch_grad = (gate_first * middle_grad).astype(jnp.bfloat16)
     readout_part = product_left(mixture, branch_grad)
     mixture_grad = product_right(branch_grad, readout_back).astype(jnp.bfloat16)
-    back_blocks = attend_backward(
+    back_blocks, *plane_pieces = attend_backward(
         bounds,
         kept_heads,
         jnp.transpose(
             mixture_grad.reshape(group_count, local_rows, seq_count, local_width), (2, 0, 1, 3)
         ),
         log_total,
-    )
+        [part.astype(jnp.bfloat16) for part in (contract_part, expand_part, readout_part)],
+    )
+    layers = seq_count // 2
+    finished = [plane_pieces[layers - 1]] + [
+        line_shift(plane_pieces[step], step + 1) for step in range(layers - 1)
+    ]
     query_back, key_back, value_back = jnp.transpose(back_blocks, (2, 1, 3, 0, 4)).reshape(
         3, group_count, local_rows, width
     )
@@ -567,38 +1336,29 @@
         precision=precise,
         preferred_element_type=jnp.float32,
     )
-    utter_grad = lax.psum(utter_part.astype(jnp.bfloat16), "seq")
-    utter_rows = utter_grad.reshape(group_count * utter_count, 6 * width)
-    condition_grad = lax.all_gather(
-        product_right(utter_rows, modulation), "seq", axis=1, tiled=True
+    utter_block = jnp.transpose(
+        utter_part.reshape(utter_rows, 6, width), (1, 0, 2)
+    ).reshape(6 * utter_rows, width)
+    shares, utters, condition_back = reduce_shares(
+        4,
+        small_rows(seq_count, utter_block),
+        modulation,
+        [projection_part.astype(jnp.bfloat16), combine_part.astype(jnp.bfloat16)],
+        finished,
+        [contract.shape, expand.shape, readout.shape],
+    )
+    projection_grad, combine_grad, contract_grad, expand_grad, readout_grad = [
+        share.astype(jnp.float32) for share in shares
+    ]
+    utter_all = jnp.transpose(
+        utters.reshape(-1, 32, width)[:, :6 * utter_rows].reshape(-1, 6, utter_rows, width), (0, 2, 1, 3)
+    ).reshape(-1, 6 * width).astype(jnp.bfloat16)
+    modulation_grad = product_left(condition_all, utter_all)
+    condition_grad = jnp.transpose(
+        condition_back[:, :utter_rows, :shard_rows], (1, 0, 2)
     ).reshape(group_count, utter_count, width)
     time_grad = silu_pull(condition_grad)[0]
-    modulation_part = product_left(condition_part, utter_rows)
-    scattered = (
-        lax.psum_scatter(
-            combine_part.astype(jnp.bfloat16), "seq", scatter_dimension=0, tiled=True
-        ).astype(jnp.float32),
-        lax.psum_scatter(
-            projection_part.astype(jnp.bfloat16), "seq", scatter_dimension=0, tiled=True
-        ).astype(jnp.float32),
-        lax.psum_scatter(
-            readout_part.astype(jnp.bfloat16), "seq", scatter_dimension=0, tiled=True
-        ).astype(jnp.float32),
-        lax.psum_scatter(
-            expand_part.astype(jnp.bfloat16), "seq", scatter_dimension=0, tiled=True
-        ).astype(jnp.float32),
-        lax.psum_scatter(
-            contract_part.astype(jnp.bfloat16), "seq", scatter_dimension=0, tiled=True
-        ).astype(jnp.float32),
-    )
-    summed = (
-        lax.psum(scattered[0].astype(jnp.bfloat16), "grp").astype(jnp.float32),
-        lax.psum(modulation_part.astype(jnp.bfloat16), "grp").astype(jnp.float32),
-        lax.psum(scattered[1].astype(jnp.bfloat16), "grp").astype(jnp.float32),
-        lax.psum(scattered[2].astype(jnp.bfloat16), "grp").astype(jnp.float32),
-        lax.psum(scattered[3].astype(jnp.bfloat16), "grp").astype(jnp.float32),
-        lax.psum(scattered[4].astype(jnp.bfloat16), "grp").astype(jnp.float32),
-    )
+    summed = (combine_grad, modulation_grad, projection_grad, readout_grad, expand_grad, contract_grad)
     return (
         output.astype(jnp.bfloat16).reshape(split_shape),
         frames_grad,

time: 1070 us -> 619 us (0.58)
  waiting for transfers between devices: 509 us -> 18.7 us
  Pallas kernels: 218 us -> 351 us
  blocking collectives: 92.6 us -> 0 us
  matrix products: 122 us -> 102 us
  starting transfers between devices: 1.06 us -> 18.2 us
  local copies, waits for them, and re-layouts: 61.5 us -> 77.8 us
  between operations: 15.6 us -> 2.65 us
    reduce_scatter x5 -> x0, waiting for transfers between devices: 226 us -> none  [the longest x1 90.4 us: shards(): lax.psum_scatter(expand_part.astype(jnp.bfloat16), 'seq', scatter_dimensi...]
    all_gather x5 -> x0, waiting for transfers between devices: 166 us -> none  [the longest x1 66.7 us: shards(): lax.all_gather(contract, 'seq', axis=0, tiled=True)]
    pallas_call x2 -> x4, Pallas kernels: 218 us -> 351 us  [the longest x1 104 us: reduce_shares(): pl.pallas_call(functools.partial(reduce_kernel, (side, side), seq_count,...]
    psum x2 -> x0, waiting for transfers between devices: 113 us -> none  [the longest x1 107 us: shards(): lax.psum(scattered[0].astype(jnp.bfloat16), 'grp').astype(jnp.float32)]
    psum x2 -> x0, blocking collectives: 79.7 us -> none  [the longest x1 42.2 us: shards(): kept_total = lax.psum(jnp.sum(kept_float), ('grp', 'seq'))]
    ppermute x0 -> x6, waiting for transfers between devices: none -> 18.7 us  [line_shift(): return lax.ppermute(values, 'seq', turned)]
    ppermute x0 -> x6, starting transfers between devices: none -> 18.2 us  [line_shift(): return lax.ppermute(values, 'seq', turned)]
    all_gather x1 -> x0, blocking collectives: 12.9 us -> none  [shards(): lax.all_gather(product_right(utter_rows, modulation), 'seq', axis=1, tile...]
  transfers between devices with their start and end apart: 12 -> 6, of which waited for: 8 -> 2; matrix products, arithmetic and copies ran while one was open for 16% -> 12% of each run, Pallas kernels for 21% -> 0%
where the time goes in v4:
time: 619 us; the launch traced here: 609 us
  Pallas kernels  351 us (57%)
  matrix products  102 us (16%)
  local copies, waits for them, and re-layouts  77.8 us (13%)
  other arithmetic  38.4 us (6%)
  waiting for transfers between devices  18.7 us (3%)
  starting transfers between devices  18.2 us (3%)
    pallas_call x1, Pallas kernels, reduce_shares(): pl.pallas_call(functools.partial(reduce_kernel, (side, side), seq_count,...  104 us
    pallas_call x1, Pallas kernels, attend_backward(): pl.pallas_call(functools.partial(backward_kernel, (side, side), seq_count...  103 us
    pallas_call x1, Pallas kernels, attend_forward(): pl.pallas_call(functools.partial(forward_kernel, (side, side), seq_count,...  81.5 us
    pallas_call x1, Pallas kernels, gather(): pl.pallas_call(functools.partial(gather_kernel, (side, side), seq_count,...  63.4 us
    dot_general x6, matrix products, product_left(): lax.dot_general(first_op, second_op, (((0,), (0,)), ((), ())), preferred_...  35.6 us
    dot_general x5, matrix products, product_right(): lax.dot_general(first_op, second_op, (((1,), (1,)), ((), ())), preferred_...  30.9 us
    dot_general x6, matrix products, product(): return jnp.dot(first_op, second_op, preferred_element_type=jnp.float32)  28 us
    ppermute x6, waiting for transfers between devices, line_shift(): return lax.ppermute(values, 'seq', turned)  18.7 us
  transfers between devices with their start and end apart: 6, of which 2 were waited for; matrix products, arithmetic and copies ran while one was open for 12% of the time, Pallas kernels for 0%

profile of v4, /device:TPU:0, one launch (start us, length us, event | category | flops | bytes accessed | tf_op | source)
XLA Modules:
  0.0 608.7 jit_solution(6062313541523107069)
XLA Ops:
  0.7 1.4 convert_reduce_fusion
  4.2 1.8 fusion.41
  7.4 63.4 %gather_weights.1 = (bf16[8,256,1024]{2,1,0:T(8,128)(2,1)}, bf16[8,128,3072]{2,1,0:T(8,128)(2,1)}, f32[8,4,1024]{2,1,0:T(4,128)}, f32[4,8,128]{2,1,0:T(8,128)}) custom-call(bf16[256,1024]{1,0:T(8,128)(2,1)} %refs_0_.1, bf16[128,3072]{1,0:T(8,128)(2,1)} %refs_1_.1, f32[8,4,1024]{2,1,0:T(4,128)} %copy-done.30, f32[8,128]{1,0:T(8,128)} %pad_convert_fusion.refs_3_), custom_call_target="tpu_custom_call" | custom-call | tf_op jit(solution)/shard_map/gather_weights/pallas_call | solution.py:962
  74.8 6.2 %collective-permute-start.2 = (bf16[576,512]{1,0:T(8,128)(2,1)}, bf16[576,512]{1,0:T(8,128)(2,1)S(1)}, u32[]{:S(2)}, u32[]{:S(2)}) collective-permute-start(bf16[576,512]{1,0:T(8,128)(2,1)} %dynamic-slice_dynamic-update-slice_fusion), channel_id=1, source_target_pairs={{0,6},{1,7},{2,0},{3,1},{4,2},{5,3},{6,4},{7,5},{8,14},{9,15},{10,... | collective-permute-start | bytes 1769480 | tf_op jit(solution)/shard_map/ppermute | solution.py:1137
  81.0 1.8 collective-permute-start
  83.4 1.3 slice_reduce_fusion
  84.7 1.3 slice.115
  86.8 1.5 slice.83
  88.4 1.6 reshape.373
  90.0 1.5 pad_maximum_fusion.1
  91.5 4.7 fusion.40
  96.6 4.0 fusion.24
  101.0 2.7 fusion.42
  105.5 1.9 fusion.38
  108.0 1.3 convert_element_type.160
  110.1 1.3 convert_multiply_fusion
  111.3 1.4 mul.388
  112.7 3.0 copy.50
  115.7 1.3 copy.68
  118.1 3.0 copy.51
  122.1 2.3 subtract_convert_fusion.1
  124.4 1.4 pad_maximum_fusion.4
  125.8 4.1 convert_element_type.161
  130.0 3.6 copy.52
  133.5 3.8 convert_element_type.162
  137.4 3.6 copy.53
  141.7 3.3 maximum_bitcast_fusion.refs_1_
  145.0 81.5 %attend_forward.1 = (bf16[8,2,3,192,128]{4,3,2,1,0:T(8,128)(2,1)}, bf16[8,2,192,128]{3,2,1,0:T(8,128)(2,1)S(1)}, f32[2,2,1,1536]{3,2,1,0:T(1,128)S(1)}, bf16[8,1...) custom-call(s32[2]{0:T(128)S(1)} %slice_reduce_fusion.1.refs_0_, ...), custom_call_target="tpu_custom_call" | custom-call | tf_op jit(solution)/shard_map/attend_forward/pallas_call | solution.py:660
  228.0 4.3 fusion.37
  233.1 1.3 copy-done.44
  234.4 3.4 fusion.43
  237.8 11.2 %multiply_convert_fusion.2 = (bf16[384,1024]{1,0:T(8,128)(2,1)S(1)}, f32[384,1024]{1,0:T(8,128)S(1)}, bf16[384,1024]{1,0:T(8,128)(2,1)}, f32[384,1024]{1,0:T(8,128)}) fusion(f32[384,6144]{1,0:T(8,128)S(1)} %bitcast.109, bf16[2,192,1024]{2,1,0:T(8,128)(2,1)S(1)} %copy-done.46, f32[384,1024]{1,0:T(8,128)S(1)} %get-tuple-element.93, f32[384]{0:T(512)S(1)} %copy-done.43, ...), kind=kOutput, calls=%fused_computation.40 | convolution fusion | flops 3238526976 | bytes 23332352 | tf_op jit(solution)/shard_map/dot_general | solution.py:21
  249.0 14.7 %fusion.6 = bf16[384,4096]{1,0:T(8,128)(2,1)} fusion(f32[384,4096]{1,0:T(8,128)} %copy-done.47, bf16[384,1024]{1,0:T(8,128)(2,1)S(1)} %get-tuple-element.90, bf16[4096,1024]{1,0:T(8,128)(2,1)} %bitcast.148), kind=kOutput, calls=%fused_computation.10 | convolution fusion | flops 3252682752 | bytes 18612224 | tf_op jit(solution)/shard_map/dot_general | solution.py:31
  263.6 7.1 %multiply_reduce_fusion.1 = (f32[384]{0:T(512)S(1)}, f32[384,1024]{1,0:T(8,128)S(1)}) fusion(f32[384,1024]{1,0:T(8,128)S(1)} %get-tuple-element.93, f32[384]{0:T(512)S(1)} %broadcast_multiply_fusion, f32[384,6144]{1,0:T(8,128)S(1)} %bitcast.110, bf16[384,4096]{1,0:T(8,128)(2,1)} %fusion.6, bf16[1024,4096]{1,0:T(8,128)(2,1)} %bitcast.145), kind=kOutput, calls=%fused_computation.39 | convolution fusion | flops 3223191040 | bytes 16256000 | tf_op jit(solution)/shard_map/dot_general | solution.py:31
  271.9 1.4 multiply_convert_fusion.1
  275.1 2.6 convolution_convert_fusion.4
  277.7 10.6 %convolution_convert_fusion.1 = bf16[4096,1024]{1,0:T(8,128)(2,1)} fusion(bf16[384,1024]{1,0:T(8,128)(2,1)S(1)} %copy-done.50, f32[384,4096]{1,0:T(8,128)} %copy-done.47), kind=kOutput, calls=%fused_computation.3 | convolution fusion | flops 3239575552 | bytes 15466496 | tf_op jit(solution)/shard_map/dot_general | solution.py:25
  288.3 7.2 %convolution_convert_fusion = bf16[1024,4096]{1,0:T(8,128)(2,1)} fusion(bf16[384,1024]{1,0:T(8,128)(2,1)S(1)} %fusion.7, bf16[384,4096]{1,0:T(8,128)(2,1)S(1)} %copy-done.48), kind=kOutput, calls=%fused_computation.2 | convolution fusion | flops 3225419776 | bytes 12320768 | tf_op jit(solution)/shard_map/dot_general | solution.py:25
  296.7 102.8 %attend_backward.1 = (bf16[8,2,3,192,128]{4,3,2,1,0:T(8,128)(2,1)}, bf16[576,512]{1,0:T(8,128)(2,1)}, bf16[576,512]{1,0:T(8,128)(2,1)}, bf16[576,512]{1,0:T(8,128)(2,1)}, bf16[576,512]{1,0:T(8,128)(2,1)}) custom-call(s32[2]{0:T(128)} %copy-done.4, bf16[8,2,3,192,128]{4,3,2,1,0:T(8,128)(2,1)} %get-tuple-element.70.refs_1_, ...), custom_call_target="tpu_custom_call" | custom-call | tf_op jit(solution)/shard_map/attend_backward/pallas_call | solution.py:838
  399.5 3.7 slice_convert_fusion.2
  403.2 4.0 copy.57
  407.2 3.7 reshape.398
  411.0 3.6 copy.65
  414.6 3.5 reshape.400
  418.1 4.0 copy.58
  422.1 4.0 reshape.399
  426.1 2.3 multiply_add_fusion.5
  429.8 6.3 %constant_dynamic-update-slice_fusion.1 = (f32[384,6144]{1,0:T(8,128)S(1)}, f32[384]{0:T(512)S(1)}, f32[384,1024]{1,0:T(8,128)S(1)}) fusion(f32[384,6144]{1,0:T(8,128)} %bitcast.104, f32[384,1024]{1,0:T(8,128)S(1)} %copy-done.7, f32[384]{0:T(512)S(1)} %broadcast_multiply_fusion.1, bf16[1024,3072]{1,0:T(8,128)(2,1)} %bitcast.149, ...), kind=kOutput, calls=%fused_computation.78 | convolution fusion | flops 2424962560 | bytes 14945792 | tf_op jit(solution)/shard_map/dot_general | solution.py:31
  436.1 2.3 fusion.34
  438.7 1.9 copy-done.45
  440.6 1.8 fusion.44
  442.5 4.5 convolution_convert_fusion.3
  446.9 7.5 %collective-permute-start.3 = (bf16[576,512]{1,0:T(8,128)(2,1)}, bf16[576,512]{1,0:T(8,128)(2,1)}, u32[]{:S(2)}, u32[]{:S(2)}) collective-permute-start(bf16[576,512]{1,0:T(8,128)(2,1)} %get-tuple-element.74), channel_id=1, source_target_pairs={{0,2},{1,3},{2,4},{3,5},{4,6},{5,7},{6,0},{7,1},{8,10},{9,11},{10,... | collective-permute-start | bytes 1769480 | tf_op jit(solution)/shard_map/ppermute | solution.py:1137
  454.4 2.6 collective-permute-start.5
  459.5 3.3 fusion.23
  462.7 2.0 fusion.39
  465.7 8.5 %convolution_convert_fusion.2 = bf16[1024,3072]{1,0:T(8,128)(2,1)} fusion(bf16[384,1024]{1,0:T(8,128)(2,1)S(1)} %copy-done.21, bf16[384,1024]{0,1:T(8,128)(2,1)S(1)} %copy-done.23, bf16[384,1024]{0,1:T(8,128)(2,1)S(1)} %bitcast.140, bf16[384,1024]{0,1:T(8,128)(2,1)S(1)} %bitcast.138), kind=kOutput, calls=%fused_computation.12 | convolution fusion | flops 2426142720 | bytes 9437184 | tf_op jit(solution)/shard_map/dot_general | solution.py:25
  474.2 18.1 %collective-permute-done.4.refs_4_ = bf16[576,512]{1,0:T(8,128)(2,1)} collective-permute-done((bf16[576,512]{1,0:T(8,128)(2,1)}, bf16[576,512]{1,0:T(8,128)(2,1)}, u32[]{:S(2)}, u32[]{:S(2)}) %collective-permute-start.4) | collective-permute-done | bytes 589856 | tf_op jit(solution)/shard_map/ppermute | solution.py:1137
  492.9 103.5 %reduce_shares.1 = (bf16[128,3072]{1,0:T(8,128)(2,1)}, bf16[256,1024]{1,0:T(8,128)(2,1)}, bf16[512,1024]{1,0:T(8,128)(2,1)}, bf16[128,4096]{1,0:T(8,128)(2,1)}, ...) custom-call(bf16[8,128,3072]{2,1,0:T(8,128)(2,1)} %bitcast.116, ...), custom_call_target="tpu_custom_call" | custom-call | tf_op jit(solution)/shard_map/reduce_shares/pallas_call | solution.py:1106
  598.0 1.1 convert.33
  601.6 1.3 convert_element_type.192
  602.9 1.5 convert_element_type.194
  604.5 1.6 convert_element_type.195
  606.0 2.3 fusion.45
  (181 shorter events, 30.7 us)
Async XLA Ops:
  0.6 70.9 %copy-start = (bf16[128,4096]{1,0:T(8,128)(2,1)S(1)}, bf16[128,4096]{1,0:T(8,128)(2,1)}, u32[]{:S(2)}) copy-start(bf16[128,4096]{1,0:T(8,128)(2,1)} %refs_3_.1) | copy-start | bytes 3145732
  0.7 70.2 %copy-start.2 = (bf16[128,1024]{1,0:T(8,128)(2,1)S(1)}, bf16[128,1024]{1,0:T(8,128)(2,1)}, u32[]{:S(2)}) copy-start(bf16[128,1024]{1,0:T(8,128)(2,1)} %refs_2_.1) | copy-start | bytes 786436
  4.1 69.9 %copy-start.1 = (bf16[512,1024]{1,0:T(8,128)(2,1)S(1)}, bf16[512,1024]{1,0:T(8,128)(2,1)}, u32[]{:S(2)}) copy-start(bf16[512,1024]{1,0:T(8,128)(2,1)} %refs_4_.1) | copy-start | bytes 3145732
  4.1 81.8 %copy-start.40 = (s32[2,2]{1,0:T(2,128)S(1)}, s32[2,2]{1,0:T(2,128)}, u32[]{:S(2)}) copy-start(s32[2,2]{1,0:T(2,128)} %param.19) | copy-start | bytes 52
  6.8 0.7 copy-start.30
  74.8 70.2 %collective-permute-start.2 = (bf16[576,512]{1,0:T(8,128)(2,1)}, bf16[576,512]{1,0:T(8,128)(2,1)S(1)}, u32[]{:S(2)}, u32[]{:S(2)}) collective-permute-start(bf16[576,512]{1,0:T(8,128)(2,1)} %dynamic-slice_dynamic-update-slice_fusion), channel_id=1, source_target_pairs={{0,6},{1,7},{2,0},{3,1},{4,2},{5,3},{6,4},{7,5},{8,14},{9,15},{10,... | collective-permute-start | bytes 1769480 | tf_op jit(solution)/shard_map/ppermute | solution.py:1137
  81.0 64.0 %collective-permute-start.1 = (bf16[576,512]{1,0:T(8,128)(2,1)}, bf16[576,512]{1,0:T(8,128)(2,1)S(1)}, u32[]{:S(2)}, u32[]{:S(2)}) collective-permute-start(bf16[576,512]{1,0:T(8,128)(2,1)} %dynamic-slice_dynamic-update-slice_fusion), channel_id=1, source_target_pairs={{0,4},{1,5},{2,6},{3,7},{4,0},{5,1},{6,2},{7,3},{8,12},{9,13},{10,... | collective-permute-start | bytes 1769480 | tf_op jit(solution)/shard_map/ppermute | solution.py:1137
  81.0 64.0 %collective-permute-start = (bf16[576,512]{1,0:T(8,128)(2,1)}, bf16[576,512]{1,0:T(8,128)(2,1)}, u32[]{:S(2)}, u32[]{:S(2)}) collective-permute-start(bf16[576,512]{1,0:T(8,128)(2,1)} %dynamic-slice_dynamic-update-slice_fusion), channel_id=1, source_target_pairs={{0,2},{1,3},{2,4},{3,5},{4,6},{5,7},{6,0},{7,1},{8,10},{9,11},{10,... | collective-permute-start | bytes 1769480 | tf_op jit(solution)/shard_map/ppermute | solution.py:1137
  86.0 10.2 %copy-start.41 = (s32[192]{0:T(256)}, s32[192]{0:T(256)S(1)}, u32[]{:S(2)}) copy-start(s32[192]{0:T(256)S(1)} %iota_add_fusion) | copy-start | bytes 2308
  91.5 4.7 copy-start.15
  91.5 5.0 copy-start.35
  96.2 4.4 copy-start.6
  96.2 4.8 slice-start.3
  96.5 4.4 slice-start.4
  100.5 3.6 copy-start.5
  101.0 3.5 copy-start.20
  105.5 1.9 copy-start.39
  105.5 2.0 copy-start.42
  122.0 2.4 copy-start.31
  122.0 2.4 copy-start.33
  141.7 3.3 copy-start.4
  145.0 87.7 %slice-start = ((s8[9437184]{0:T(1024)(128)(4,1)}), s8[4194304]{0:T(1024)(128)(4,1)S(1)}, s32[]{:S(2)}) async-start(s8[9437184]{0:T(1024)(128)(4,1)} %bitcast.106), calls=%async_computation | async-start | bytes 8388608
  145.0 87.7 %slice-start.1 = ((s8[9437184]{0:T(1024)(128)(4,1)}), s8[1048576]{0:T(1024)(128)(4,1)S(1)}, s32[]{:S(2)}) async-start(s8[9437184]{0:T(1024)(128)(4,1)} %bitcast.106), calls=%async_computation.1 | async-start | bytes 2097152
  226.6 5.8 copy-start.3
  226.6 1.4 copy-start.7
  228.0 4.7 slice-start.2
  228.0 6.3 %copy-start.44 = (bf16[8,128,4096]{2,1,0:T(8,128)(2,1)S(1)}, bf16[8,128,4096]{2,1,0:T(8,128)(2,1)}, u32[]{:S(2)}) copy-start(bf16[8,128,4096]{2,1,0:T(8,128)(2,1)} %get-tuple-element.68) | copy-start | bytes 25165828
  234.4 3.4 copy-start.43
  234.4 3.4 copy-start.46
  237.8 11.2 %copy-start.47 = (f32[384,4096]{1,0:T(8,128)}, f32[384,4096]{1,0:T(8,128)S(1)}, u32[]{:S(2)}) copy-start(f32[384,4096]{1,0:T(8,128)S(1)} %fusion.43) | copy-start | bytes 18874372
  249.0 14.7 %copy-start.49 = (bf16[384,1024]{1,0:T(8,128)(2,1)}, bf16[384,1024]{1,0:T(8,128)(2,1)S(1)}, u32[]{:S(2)}) copy-start(bf16[384,1024]{1,0:T(8,128)(2,1)S(1)} %get-tuple-element.90) | copy-start | bytes 2359300
  249.0 22.9 %copy-start.11 = (f32[384,1024]{1,0:T(8,128)}, f32[384,1024]{1,0:T(8,128)S(1)}, u32[]{:S(2)}) copy-start(f32[384,1024]{1,0:T(8,128)S(1)} %get-tuple-element.91) | copy-start | bytes 4718596
  270.7 1.1 copy-start.8
  271.9 2.2 copy-start.14
  275.1 2.6 copy-start.50
  277.7 10.6 %copy-start.48 = (bf16[384,4096]{1,0:T(8,128)(2,1)S(1)}, bf16[384,4096]{1,0:T(8,128)(2,1)}, u32[]{:S(2)}) copy-start(bf16[384,4096]{1,0:T(8,128)(2,1)} %fusion.6) | copy-start | bytes 9437188
  422.1 4.0 copy-start.32
  422.1 4.0 copy-start.34
  428.4 1.4 copy-start.22
  428.5 7.5 %copy-start.24 = (bf16[384,16,64]{0,2,1:T(8,128)(2,1)}, bf16[384,16,64]{0,2,1:T(8,128)(2,1)S(1)}, u32[]{:S(2)}) copy-start(bf16[384,16,64]{0,2,1:T(8,128)(2,1)S(1)} %add_convert_fusion.2) | copy-start | bytes 2359300
  428.6 7.4 %copy-start.26 = (bf16[384,16,64]{0,2,1:T(8,128)(2,1)}, bf16[384,16,64]{0,2,1:T(8,128)(2,1)S(1)}, u32[]{:S(2)}) copy-start(bf16[384,16,64]{0,2,1:T(8,128)(2,1)S(1)} %add_convert_fusion.1) | copy-start | bytes 2359300
  436.1 2.3 copy-start.10
  436.1 2.4 copy-start.13
  438.4 2.2 copy-start.45
  440.6 1.8 copy-start.16
  442.4 14.6 %copy-start.9 = (f32[384,1024]{1,0:T(8,128)S(1)}, f32[384,1024]{1,0:T(8,128)}, u32[]{:S(2)}) copy-start(f32[384,1024]{1,0:T(8,128)} %copy-done.8) | copy-start | bytes 4718596
  446.9 27.3 %collective-permute-start.3 = (bf16[576,512]{1,0:T(8,128)(2,1)}, bf16[576,512]{1,0:T(8,128)(2,1)}, u32[]{:S(2)}, u32[]{:S(2)}) collective-permute-start(bf16[576,512]{1,0:T(8,128)(2,1)} %get-tuple-element.74), channel_id=1, source_target_pairs={{0,2},{1,3},{2,4},{3,5},{4,6},{5,7},{6,0},{7,1},{8,10},{9,11},{10,... | collective-permute-start | bytes 1769480 | tf_op jit(solution)/shard_map/ppermute | solution.py:1137
  454.4 37.8 %collective-permute-start.4 = (bf16[576,512]{1,0:T(8,128)(2,1)}, bf16[576,512]{1,0:T(8,128)(2,1)}, u32[]{:S(2)}, u32[]{:S(2)}) collective-permute-start(bf16[576,512]{1,0:T(8,128)(2,1)} %get-tuple-element.75), channel_id=1, source_target_pairs={{0,4},{1,5},{2,6},{3,7},{4,0},{5,1},{6,2},{7,3},{8,12},{9,13},{10,... | collective-permute-start | bytes 1769480 | tf_op jit(solution)/shard_map/ppermute | solution.py:1137
  454.4 38.5 %collective-permute-start.5 = (bf16[576,512]{1,0:T(8,128)(2,1)}, bf16[576,512]{1,0:T(8,128)(2,1)}, u32[]{:S(2)}, u32[]{:S(2)}) collective-permute-start(bf16[576,512]{1,0:T(8,128)(2,1)} %get-tuple-element.76), channel_id=1, source_target_pairs={{0,6},{1,7},{2,0},{3,1},{4,2},{5,3},{6,4},{7,5},{8,14},{9,15},{10,... | collective-permute-start | bytes 1769480 | tf_op jit(solution)/shard_map/ppermute | solution.py:1137
  457.2 1.4 copy-start.12
  457.2 1.9 copy-start.17
  462.7 3.0 copy-start.21
  462.7 3.0 copy-start.23
  462.7 3.0 copy-start.25
  462.7 3.0 copy-start.27
  492.9 104.4 %copy-start.37 = (f32[2,2,1024]{2,1,0:T(2,128)S(1)}, f32[2,2,1024]{2,1,0:T(2,128)}, u32[]{:S(2)}) copy-start(f32[2,2,1024]{2,1,0:T(2,128)} %param.18) | copy-start | bytes 49156
  596.5 3.2 copy-start.36
  596.5 4.1 copy-start.29
  599.2 2.5 copy-start.28
  600.6 2.4 copy-start.19
  602.9 1.5 copy-start.18
  604.5 1.6 copy-start.38

commit v5 on v4

--- a/solution.py
+++ b/solution.py
@@ -288,7 +288,7 @@
         )
 
 
-def plane_sum_scratch(parts, side):
+def plane_sum_scratch(parts, side, in_place=False):
     layers = parts[0].shape[0] // 2
     hops = max(side - 1, 1)
     count = len(parts)
@@ -301,7 +301,7 @@
         ]
 
     return (
-        buffers((layers,), 1, 1)
+        ([] if in_place else buffers((layers,), 1, 1))
         + buffers((layers,), 1, 1)
         + buffers((layers, hops, side), side, 2 * side)
         + buffers((layers, hops), side, 2 * side)
@@ -320,12 +320,14 @@
 
 
 class PlaneSum:
-    def __init__(self, place, parts, pieces, segments, buffers, semaphores):
+    def __init__(self, place, parts, pieces, segments, buffers, semaphores, in_place=False):
         self.place, self.parts, self.pieces, self.segments = place, parts, pieces, segments
         count = len(parts)
-        self.sums, self.swapped, self.y_first, self.x_second, self.x_first, self.y_second = [
-            buffers[index * count:(index + 1) * count] for index in range(6)
-        ]
+        buffers = (() if in_place else buffers[:count], *[
+            buffers[index * count:(index + 1) * count] for index in range(0 if in_place else 1, 5 if in_place else 6)
+        ])
+        self.in_place = in_place
+        self.sums, self.swapped, self.y_first, self.x_second, self.x_first, self.y_second = buffers
         self.load_sem = semaphores[0]
         self.core, self.first_sem, self.second_sem = semaphores[1:3], semaphores[3:5], semaphores[5:7]
         self.order = place.far + [place.layer]
@@ -345,17 +347,27 @@
             )
             copy.start()
             self.loads[index, step] = copy
-            self.swaps[index, step] = place.push(
-                self.parts[index].at[target * 2 + 1 - place.core], self.swapped[index].at[step],
-                *self.core, (index, step), (place.grp, place.partner),
-            )
+            self.swap(index, step)
+
+    def swap(self, index, step):
+        place = self.place
+        self.swaps[index, step] = place.push(
+            self.parts[index].at[self.order[step] * 2 + 1 - place.core], self.swapped[index].at[step],
+            *self.core, (index, step), (place.grp, place.partner),
+        )
+
+    def running(self, index, step):
+        if self.in_place:
+            return self.parts[index].at[self.order[step] * 2 + self.place.core]
+        return self.sums[index].at[step]
 
     def first(self, index, step):
         place = self.place
         rows, cols, height, width = self.sizes(index)
-        self.loads[index, step].wait()
+        if not self.in_place:
+            self.loads[index, step].wait()
         self.swaps[index, step].wait_recv()
-        total = self.sums[index].at[step]
+        total = self.running(index, step)
         add_rows(total, self.swapped[index].at[step], 0, rows, 0, cols)
         copies = []
         for hop, other in enumerate(place.along):
@@ -378,7 +390,7 @@
         rows, cols, height, width = self.sizes(index)
         for copy in self.waiting[index, step]:
             copy.wait_recv()
-        total = self.sums[index].at[step]
+        total = self.running(index, step)
         for hop in range(place.rows_y - 1):
             for column in range(place.cols_x):
                 add_rows(
@@ -408,7 +420,7 @@
         for copy in self.waiting[index, step]:
             copy.wait_recv()
         self.waiting[index, step] = []
-        total = self.sums[index].at[step]
+        total = self.running(index, step)
         out = self.pieces[index][step]
         row, col = place.gy * height, 2 * place.gx * width
         for hop in range(place.cols_x - 1):
@@ -424,8 +436,8 @@
             else:
                 add_rows(total, source, row, height, col + width, width)
 
-    def steps(self, stage):
-        return [functools.partial(stage, *job) for job in self.jobs]
+    def steps(self, stage, only=None):
+        return [functools.partial(stage, *job) for job in self.jobs if only is None or job[0] == only]
 
     def finish(self):
         self.place.sent()
@@ -984,38 +996,187 @@
     return outs[:count], outs[count], outs[count + 1]
 
 
-def reduce_kernel(plane, seq_count, count, done_count, *refs):
+def turn_lanes(values, cos, sin):
+    lane = lax.broadcasted_iota(jnp.int32, values.shape, 1)
+    ahead = pltpu.roll(values, values.shape[1] - HEAD_DIM // 2, 1)
+    behind = pltpu.roll(values, HEAD_DIM // 2, 1)
+    other = jnp.where(lax.rem(lane, HEAD_DIM) < HEAD_DIM // 2, ahead, behind)
+    return values * cos + other * sin
+
+
+def second_mask(bound_ref, group, me, local_rows, first, rows):
+    row = lax.broadcasted_iota(jnp.int32, (rows, 1), 0) + (me * local_rows + first)
+    return row >= bound_ref[group]
+
+
+def centered(values):
+    center = values - jnp.mean(values, axis=-1, keepdims=True)
+    scale = lax.rsqrt(jnp.mean(center * center, axis=-1, keepdims=True) + epsilon)
+    return center * scale, scale
+
+
+def back_kernel(plane, seq_count, *refs):
     layers = seq_count // 2
-    parts, refs = refs[:count], refs[count:]
-    finished, refs = refs[:layers], refs[layers:]
-    utter_ref, modulation_ref, refs = refs[0], refs[1], refs[2:]
-    outs, refs = refs[:count + done_count], refs[count + done_count:]
-    total_ref, utters_ref, conditions_ref, refs = refs[0], refs[1], refs[2], refs[3:]
-    condition_scr, token_send, token_recv, last_send, last_recv, line_send, line_recv = refs[:7]
-    small_refs, spread_sems, refs = refs[7:12], refs[12:16], refs[16:]
-    lines, refs = refs[:count], refs[count:]
-    pieces = [refs[index * layers:(index + 1) * layers] for index in range(count)]
-    refs = refs[count * layers:]
-    buffers, semaphores = refs[:6 * count], refs[6 * count:]
+    (
+        bound_ref, back_ref, cos_ref, sin_ref, normed_ref, hidden_ref, middle_ref, frames_ref, shortcut_ref,
+        combine_ref, projection_ref, mods_ref, late_ref, modulation_ref,
+    ) = refs[:14]
+    finished, refs = refs[14:14 + layers], refs[14 + layers:]
+    frames_out, shortcut_out, outs, refs = refs[0], refs[1], refs[2:7], refs[7:]
+    utters_ref, conditions_ref, refs = refs[0], refs[1], refs[2:]
+    (
+        packed_scr, combine_scr, projection_scr, normed_t_scr, joined_t_scr, grad_scr, low_scr,
+        frames_scr, shortcut_scr, total_ref, utter_scr, condition_scr,
+    ) = refs[:12]
+    parts, done_scr, lines, refs = refs[12:14], refs[14], refs[15:17], refs[17:]
+    pieces = [refs[index * layers:(index + 1) * layers] for index in range(2)]
+    refs = refs[2 * layers:]
+    buffers, semaphores, refs = refs[:10], refs[10:17], refs[17:]
+    small_refs, spread_sems, refs = refs[:5], refs[5:9], refs[9:]
+    weight_sem, out_sem, token_send, token_recv, last_send, last_recv, line_send, line_recv, done_send, done_recv = refs
+    group_count, local_rows, local_width = back_ref.shape[1], back_ref.shape[3], back_ref.shape[4]
+    row_count, width = normed_ref.shape
     place = Place(plane, seq_count)
-    enter([(place.grp, other) for other in place.others] + [(other, place.me) for other in place.groups])
+    me = place.me
     side = place.cols_x
+    enter([(place.grp, other) for other in place.others] + [(other, me) for other in place.groups])
+    arrived = {}
+    for step in range(layers - 1):
+        arrived[step] = place.push(
+            finished[step], done_scr.at[step], done_send, done_recv, step, (place.grp, place.lines[step])
+        )
+    weights = [
+        pltpu.make_async_copy(projection_ref, projection_scr, weight_sem.at[0]),
+        pltpu.make_async_copy(combine_ref, combine_scr, weight_sem.at[1]),
+    ]
+    for copy in weights:
+        copy.start()
+    for source in range(seq_count):
+        for kind in range(3):
+            for group in range(group_count):
+                packed_scr[
+                    group * local_rows:(group + 1) * local_rows,
+                    kind * width + source * local_width:kind * width + (source + 1) * local_width,
+                ] = back_ref[source, group, kind]
+
+    def turn(index, carry):
+        lanes = pl.ds(pl.multiple_of(index * 128, 128), 128)
+        packed_scr[:, lanes] = turn_lanes(
+            packed_scr[:, lanes].astype(jnp.float32), cos_ref[...], -sin_ref[...]
+        ).astype(jnp.bfloat16)
+        return carry
+
+    lax.fori_loop(0, 2 * width // 128, turn, 0)
+    normed_t_scr[...] = normed_ref[...].astype(jnp.float32).T.astype(jnp.bfloat16)
     segments = [
         piece_segments([part.shape[1:]], side, part.shape[2] // side)[0][0] for part in parts
     ]
     done_segments, _ = piece_segments(
-        [out.shape for out in outs[count:]], side, min(out.shape[1] for out in outs[count:]) // side
-    )
-    plane_sum = PlaneSum(place, parts, pieces, segments, buffers, semaphores)
-    plane_sum.begin()
-    small = SmallSum(place, utter_ref, total_ref, *small_refs)
+        [out.shape for out in outs[2:]], side, min(out.shape[1] for out in outs[2:]) // side
+    )
+    plane_sum = PlaneSum(place, parts, pieces, segments, buffers, semaphores, True)
+    spread = PlaneSpread(place, outs, *spread_sems)
+
+    def share(index, left, right, tile):
+        rows = parts[index].shape[1]
+
+        def fill(owner):
+            at = pl.ds(pl.multiple_of(owner * rows, rows), rows)
+
+            def one(turn, carry):
+                lanes = pl.ds(pl.multiple_of(turn * tile, tile), tile)
+                parts[index][owner, :, lanes] = dot_nn(left[at, :], right[:, lanes]).astype(jnp.bfloat16)
+                return carry
+
+            lax.fori_loop(0, parts[index].shape[2] // tile, one, 0)
+
+        for step, target in enumerate(plane_sum.order):
+            fill(target * 2 + 1 - place.core)
+            plane_sum.swap(index, step)
+        for target in plane_sum.order:
+            fill(target * 2 + place.core)
+
+    share(0, normed_t_scr, packed_scr, 512)
+    weights[0].wait()
+
+    def grad_tile(index, carry):
+        at = pl.ds(pl.multiple_of(index * 256, 256), 256)
+        grad_scr[:, at] = dot_nt(packed_scr[...], projection_scr[at, :])
+        return carry
+
+    lax.fori_loop(0, width // 256, grad_tile, 0)
+    for hook in plane_sum.steps(plane_sum.first, 0):
+        hook()
+    block, utter_rows = utter_scr.shape[1], 2 * group_count
+    utter_scr[...] = jnp.zeros_like(utter_scr)
+
+    def put(part, utter, value):
+        row = part * utter_rows + utter
+        utter_scr[row // block, row % block:row % block + 1, :] = value
+
+    for part in range(4):
+        for utter in range(utter_rows):
+            put(part + 2, utter, late_ref[part * utter_rows + utter:part * utter_rows + utter + 1, :])
+    chunk = 32
+    for group in range(group_count):
+
+        def norm_back(index, sums):
+            first = pl.multiple_of(index * chunk, chunk)
+            at = pl.ds(pl.multiple_of(group * local_rows + first, chunk), chunk)
+            second = second_mask(bound_ref, group, me, local_rows, first, chunk)
+            row = group * 2 * 6
+            scale_part = jnp.where(second, mods_ref[row + 7:row + 8, :], mods_ref[row + 1:row + 2, :])
+            grad = grad_scr[at, :]
+            normal, scale = centered(hidden_ref[at, :])
+            inner = grad * (1.0 + scale_part)
+            turned = scale * (
+                inner
+                - jnp.mean(inner, axis=-1, keepdims=True)
+                - normal * jnp.mean(inner * normal, axis=-1, keepdims=True)
+            )
+            low_scr[at, :] = (middle_ref[at, :] + turned).astype(jnp.bfloat16)
+            scaled = grad * normal
+            later = second.astype(jnp.float32)
+            shift_later, scale_later = grad * later, scaled * later
+            return (
+                sums[0] + fold_rows(grad - shift_later, jnp.sum),
+                sums[1] + fold_rows(shift_later, jnp.sum),
+                sums[2] + fold_rows(scaled - scale_later, jnp.sum),
+                sums[3] + fold_rows(scale_later, jnp.sum),
+            )
+
+        zero = jnp.zeros((8, width), jnp.float32)
+        sums = lax.fori_loop(0, local_rows // chunk, norm_back, (zero, zero, zero, zero))
+        for spot, value in enumerate(sums):
+            put(spot // 2, group * 2 + spot % 2, jnp.sum(value, axis=0, keepdims=True))
+    small = SmallSum(place, utter_scr, total_ref, *small_refs)
     small.begin()
-    spread = PlaneSpread(place, outs, *spread_sems)
-    late = []
-    for index in range(done_count):
-        spread.total(count + index, finished[0], finished[1:], done_segments[index])
-        late.append(functools.partial(spread.second, count + index))
-    arrived = {}
+    joined_t_scr[:width, :] = frames_ref[...].astype(jnp.float32).T.astype(jnp.bfloat16)
+    joined_t_scr[width:, :] = shortcut_ref[...].astype(jnp.float32).T.astype(jnp.bfloat16)
+    share(1, joined_t_scr, low_scr, 512)
+    for hook in plane_sum.steps(plane_sum.second, 0)[:layers // 2]:
+        hook()
+    weights[1].wait()
+
+    def joined_tile(index, carry):
+        at = pl.ds(pl.multiple_of(index * 256, 256), 256)
+        late = pl.ds(pl.multiple_of(width + index * 256, 256), 256)
+        frames_scr[:, at] = dot_nt(low_scr[...], combine_scr[at, :])
+        shortcut_scr[:, at] = dot_nt(low_scr[...], combine_scr[late, :])
+        return carry
+
+    lax.fori_loop(0, width // 256, joined_tile, 0)
+    grads = [
+        pltpu.make_async_copy(frames_scr, frames_out, out_sem.at[0]),
+        pltpu.make_async_copy(shortcut_scr, shortcut_out, out_sem.at[1]),
+    ]
+    for copy in grads:
+        copy.start()
+    for hook in plane_sum.steps(plane_sum.first, 1):
+        hook()
+    for hook in plane_sum.steps(plane_sum.second, 0)[layers // 2:]:
+        hook()
+    small.middle()
 
     def along_line(index, step):
         plane_sum.third(index, step)
@@ -1028,107 +1189,116 @@
     def last(index):
         for step in range(layers - 1):
             arrived[index, step].wait_recv()
-        spread.total(index, pieces[index][layers - 1], [lines[index].at[step] for step in range(layers - 1)], segments[index])
-
-    jobs = plane_sum.jobs
-    lag = layers
-    hooks = []
-    for turn in range(len(jobs) + 4 * lag):
-        if turn < len(jobs):
-            hooks.append(functools.partial(plane_sum.first, *jobs[turn]))
-        if turn >= lag + 1 and late:
-            hooks.append(late.pop(0))
-        if 0 <= turn - lag < len(jobs):
-            hooks.append(functools.partial(plane_sum.second, *jobs[turn - lag]))
-        if 0 <= turn - 2 * lag < len(jobs):
-            hooks.append(functools.partial(along_line, *jobs[turn - 2 * lag]))
-        done = turn - 3 * lag
-        if 0 <= done < len(jobs) and done % layers == layers - 1:
-            hooks.append(functools.partial(last, done // layers))
-        done = turn - 4 * lag
-        if 0 <= done < len(jobs) and done % layers == layers - 1:
-            hooks.append(functools.partial(spread.second, done // layers))
-    middle = len(hooks) // 3
-    for hook in hooks[:middle]:
-        hook()
-    small.middle()
-    for hook in hooks[middle:2 * middle]:
-        hook()
+        spread.total(
+            index, pieces[index][layers - 1], [lines[index].at[step] for step in range(layers - 1)], segments[index]
+        )
+
+    for step in range(layers):
+        plane_sum.second(1, step)
+        along_line(0, step)
     small.finish()
     utters_ref[place.grp] = total_ref[...]
     tokens = [
-        place.push(total_ref, utters_ref.at[place.grp], token_send, token_recv, step, (other, place.me))
+        place.push(total_ref, utters_ref.at[place.grp], token_send, token_recv, step, (other, me))
         for step, other in enumerate(place.groups)
     ]
-    block, width = total_ref.shape[1], total_ref.shape[2]
-    rows = modulation_ref.shape[1] // width
-    utter_rows = utter_ref.shape[0] * block // 8
     condition_scr[...] = jnp.zeros_like(condition_scr)
     shard_rows = modulation_ref.shape[0]
-    for spot in range(rows * utter_rows // block):
+    for spot in range(6 * utter_rows // block):
         part, row = spot * block // utter_rows, spot * block % utter_rows
         condition_scr[row:row + block, :shard_rows] += dot_nt(
             total_ref[spot].astype(jnp.bfloat16), modulation_ref[:, part * width:(part + 1) * width]
         )
-    conditions_ref[place.me] = condition_scr[...]
+    conditions_ref[me] = condition_scr[...]
     tokens += [
-        place.push(condition_scr, conditions_ref.at[place.me], last_send, last_recv, step, (place.grp, other))
+        place.push(condition_scr, conditions_ref.at[me], last_send, last_recv, step, (place.grp, other))
         for step, other in enumerate(place.others)
     ]
-    for hook in hooks[2 * middle:]:
-        hook()
+    for step in range(layers):
+        along_line(1, step)
+    for step in range(layers - 1):
+        arrived[step].wait_recv()
+    for index in range(2, 5):
+        spread.total(
+            index, finished[layers - 1], [done_scr.at[step] for step in range(layers - 1)], done_segments[index - 2]
+        )
+    last(0)
+    for index in range(2, 5):
+        spread.second(index)
+    last(1)
+    spread.second(0)
+    spread.second(1)
     place.sent()
     for copy in tokens:
         copy.wait_recv()
-    for index in range(count + done_count):
+    for copy in grads:
+        copy.wait()
+    for index in range(5):
         spread.finish(index)
 
 
-def reduce_shares(collective, utter, modulation, parts, finished, done_shapes):
+def finish_backward(bounds, back, cos, sin, normed, hidden, middle_grad, frames, shortcut, combine, projection, mods, late, modulation, finished, done_shapes):
     grp_count = lax.axis_size("grp")
     seq_count = lax.axis_size("seq")
     side = math.isqrt(grp_count)
     layers = seq_count // 2
-    count, done_count = len(parts), len(done_shapes)
-    parts = by_owner(parts, seq_count)
+    hops = max(side - 1, 1)
     anywhere = pl.BlockSpec(memory_space=pl.ANY)
     vmem = pl.BlockSpec(memory_space=pltpu.VMEM)
     dma = pltpu.SemaphoreType.DMA
-    hops = max(side - 1, 1)
-    pieces = [
-        pltpu.VMEM((part.shape[1] // side, part.shape[2] // side), jnp.bfloat16)
-        for part in parts for _ in range(layers)
+    row_count, width = normed.shape
+    low, full = jnp.bfloat16, jnp.float32
+    parts = [
+        jax.ShapeDtypeStruct((seq_count, weight.shape[0] // seq_count, weight.shape[1]), low)
+        for weight in (projection, combine)
     ]
-    lines = [
-        pltpu.VMEM((layers - 1, part.shape[1] // side, part.shape[2] // side), jnp.bfloat16) for part in parts
-    ]
-    total = count + done_count
-    outs = pl.pallas_call(
-        functools.partial(reduce_kernel, (side, side), seq_count, count, done_count),
-        out_shape=tuple(jax.ShapeDtypeStruct(part.shape[1:], jnp.bfloat16) for part in parts) + tuple(
-            jax.ShapeDtypeStruct(shape, jnp.bfloat16) for shape in done_shapes
-        ) + (
-            jax.ShapeDtypeStruct(utter.shape, jnp.float32),
-            jax.ShapeDtypeStruct((grp_count,) + utter.shape, jnp.float32),
-            jax.ShapeDtypeStruct((seq_count, 8, 128), jnp.float32),
+    out_shapes = [part.shape[1:] for part in parts] + list(done_shapes)
+    small = jax.ShapeDtypeStruct((seq_count, 32 // seq_count, width), full)
+    return pl.pallas_call(
+        functools.partial(back_kernel, (side, side), seq_count),
+        out_shape=(
+            jax.ShapeDtypeStruct((row_count, width), full),
+            jax.ShapeDtypeStruct((row_count, width), full),
+        ) + tuple(jax.ShapeDtypeStruct(shape, low) for shape in out_shapes) + (
+            jax.ShapeDtypeStruct((grp_count,) + small.shape, full),
+            jax.ShapeDtypeStruct((seq_count, 8, 128), full),
         ),
-        in_specs=[anywhere] * count + [vmem] * (layers + 2),
-        out_specs=(vmem,) * (total + 3),
+        in_specs=[pl.BlockSpec(memory_space=pltpu.SMEM)] + [vmem] * 8 + [anywhere] * 2 + [vmem] * (3 + layers),
+        out_specs=(anywhere,) * 2 + (vmem,) * 7,
         scratch_shapes=[
-            pltpu.VMEM((8, 128), jnp.float32),
+            pltpu.VMEM((row_count, 3 * width), low),
+            pltpu.VMEM(combine.shape, low),
+            pltpu.VMEM(projection.shape, low),
+            pltpu.VMEM((width, row_count), low),
+            pltpu.VMEM((2 * width, row_count), low),
+            pltpu.VMEM((row_count, width), full),
+            pltpu.VMEM((row_count, width), low),
+            pltpu.VMEM((row_count, width), full),
+            pltpu.VMEM((row_count, width), full),
+            pltpu.VMEM(small.shape, full),
+            pltpu.VMEM(small.shape, full),
+            pltpu.VMEM((8, 128), full),
+        ] + [pltpu.VMEM(part.shape, low) for part in parts] + [
+            pltpu.VMEM((layers - 1,) + finished[0].shape, low)
+        ] + [
+            pltpu.VMEM((layers - 1, part.shape[1] // side, part.shape[2] // side), low) for part in parts
+        ] + [
+            pltpu.VMEM((part.shape[1] // side, part.shape[2] // side), low)
+            for part in parts for _ in range(layers)
+        ] + plane_sum_scratch(parts, side, True) + small_scratch(small) + [
+            dma((5, 2, hops)), dma((5, 2, hops)),
+            dma((5, 2, hops, side)), dma((5, 2, hops, side)),
+            dma((2,)), dma((2,)),
             dma((grp_count - 1,)), dma((grp_count - 1,)),
             dma((seq_count - 1,)), dma((seq_count - 1,)),
-            dma((count, layers - 1)), dma((count, layers - 1)),
-        ] + small_scratch(utter) + [
-            dma((total, 2, hops)), dma((total, 2, hops)),
-            dma((total, 2, hops, side)), dma((total, 2, hops, side)),
-        ] + lines + pieces + plane_sum_scratch(parts, side),
+            dma((2, layers - 1)), dma((2, layers - 1)),
+            dma((layers - 1,)), dma((layers - 1,)),
+        ],
         compiler_params=pltpu.CompilerParams(
-            collective_id=collective, has_side_effects=True, vmem_limit_bytes=60 * 1024 * 1024
+            collective_id=4, has_side_effects=True, vmem_limit_bytes=60 * 1024 * 1024
         ),
-        name="reduce_shares",
-    )(*parts, *finished, utter, modulation)
-    return outs[:total], outs[total + 1], outs[total + 2]
+        name="finish_backward",
+    )(bounds, back, cos, sin, normed, hidden, middle_grad, frames, shortcut, combine, projection, mods, late, modulation, *finished)
 
 
 def line_shift(values, step):
@@ -1185,6 +1355,8 @@
     member_float = member_info[1].astype(jnp.float32)
     position = member_info[2]
     cos_table, sin_table = rotary_tables(position.reshape(row_count))
+    cos_lanes = jnp.tile(cos_table[:, 0], (1, 4))
+    sin_lanes = jnp.tile(jnp.concatenate([-sin_table[:, 0], sin_table[:, 0]], axis=1), (1, 2))
     silu_value, silu_pull = jax.vjp(jax.nn.silu, time_embed)
     condition = silu_value.astype(jnp.bfloat16)
     shard_rows = modulation.shape[0]
@@ -1289,64 +1461,39 @@
         log_total,
         [part.astype(jnp.bfloat16) for part in (contract_part, expand_part, readout_part)],
     )
-    layers = seq_count // 2
-    finished = [plane_pieces[layers - 1]] + [
-        line_shift(plane_pieces[step], step + 1) for step in range(layers - 1)
-    ]
-    query_back, key_back, value_back = jnp.transpose(back_blocks, (2, 1, 3, 0, 4)).reshape(
-        3, group_count, local_rows, width
-    )
-    query_unturned = query_pull(query_back.reshape(head_shape).astype(jnp.float32))[0].reshape(
-        row_count, width
-    )
-    key_unturned = key_pull(key_back.reshape(head_shape).astype(jnp.float32))[0].reshape(
-        row_count, width
-    )
-    packed_grad = jnp.concatenate(
-        [
-            query_unturned.astype(jnp.bfloat16),
-            key_unturned.astype(jnp.bfloat16),
-            value_back.reshape(row_count, width),
-        ],
-        axis=1,
-    )
-    projection_part = product_left(normed, packed_grad)
-    normed_grad = product_right(packed_grad, projection_back)
-    hidden_extra, shift_first_grad, scale_first_grad = first_pull(normed_grad)
-    hidden_grad = (middle_grad + hidden_extra).astype(jnp.bfloat16)
-    combine_part = product_left(joined, hidden_grad)
-    joined_grad = product_right(hidden_grad, combine_back)
-    frames_grad = joined_grad[:, :width].reshape(split_shape)
-    shortcut_grad = joined_grad[:, width:].reshape(split_shape)
-    modulation_frame_grad = jnp.concatenate(
-        [
-            shift_first_grad,
-            scale_first_grad,
-            gate_first_grad,
-            shift_second_grad,
-            scale_second_grad,
-            gate_second_grad,
-        ],
-        axis=1,
-    )
-    utter_part = jnp.einsum(
+    late_grads = jnp.concatenate(
+        [gate_first_grad, shift_second_grad, scale_second_grad, gate_second_grad], axis=1
+    )
+    late_part = jnp.einsum(
         "gtu,gte->gue",
         member_float,
-        modulation_frame_grad.reshape(group_count, local_rows, 6 * width),
+        late_grads.reshape(group_count, local_rows, 4 * width),
         precision=precise,
         preferred_element_type=jnp.float32,
     )
-    utter_block = jnp.transpose(
-        utter_part.reshape(utter_rows, 6, width), (1, 0, 2)
-    ).reshape(6 * utter_rows, width)
-    shares, utters, condition_back = reduce_shares(
-        4,
-        small_rows(seq_count, utter_block),
+    late_rows = jnp.transpose(
+        late_part.reshape(utter_rows, 4, width), (1, 0, 2)
+    ).reshape(4 * utter_rows, width)
+    frames_grad, shortcut_grad, *shares, utters, condition_back = finish_backward(
+        bounds,
+        back_blocks,
+        cos_lanes,
+        sin_lanes,
+        normed,
+        hidden,
+        middle_grad,
+        frames.reshape(row_count, width),
+        shortcut.reshape(row_count, width),
+        combine_full,
+        projection_full,
+        partial_total.reshape(32, width),
+        late_rows,
         modulation,
-        [projection_part.astype(jnp.bfloat16), combine_part.astype(jnp.bfloat16)],
-        finished,
+        plane_pieces,
         [contract.shape, expand.shape, readout.shape],
     )
+    frames_grad = frames_grad.reshape(split_shape)
+    shortcut_grad = shortcut_grad.reshape(split_shape)
     projection_grad, combine_grad, contract_grad, expand_grad, readout_grad = [
         share.astype(jnp.float32) for share in shares
     ]

time: 619 us -> 560 us (0.905)
  the two profiles are of different devices: /device:TPU:0 before, /device:TPU:8 now
where the time goes in v5:
time: 560 us; the launch traced here: 550 us
  Pallas kernels  372 us (66%)
  matrix products  77.9 us (14%)
  local copies, waits for them, and re-layouts  57.4 us (10%)
  other arithmetic  33 us (6%)
  starting transfers between devices  7.54 us (1%)
    pallas_call x1, Pallas kernels, finish_backward(): pl.pallas_call(functools.partial(back_kernel, (side, side), seq_count), o...  118 us
    pallas_call x1, Pallas kernels, attend_backward(): pl.pallas_call(functools.partial(backward_kernel, (side, side), seq_count...  103 us
    pallas_call x1, Pallas kernels, attend_forward(): pl.pallas_call(functools.partial(forward_kernel, (side, side), seq_count,...  88.9 us
    pallas_call x1, Pallas kernels, gather(): pl.pallas_call(functools.partial(gather_kernel, (side, side), seq_count,...  61.6 us
    dot_general x6, matrix products, product(): return jnp.dot(first_op, second_op, preferred_element_type=jnp.float32)  25.2 us
    dot_general x4, matrix products, product_left(): lax.dot_general(first_op, second_op, (((0,), (0,)), ((), ())), preferred_...  24.4 us
    dot_general x3, matrix products, product_right(): lax.dot_general(first_op, second_op, (((1,), (1,)), ((), ())), preferred_...  22.2 us
    convert_element_type x5, local copies, waits for them, and re-layouts, by_target(): vectors.reshape(group_count, local_rows, seq_count, local_width)  16.1 us
  transfers between devices with their start and end apart: 3, of which 0 were waited for; matrix products, arithmetic and copies ran while one was open for 12% of the time, Pallas kernels for 0%

profile of v5, /device:TPU:8, one launch (start us, length us, event | category | flops | bytes accessed | tf_op | source)
XLA Modules:
  0.0 549.9 jit_solution(1672793393830871542)
XLA Ops:
  0.7 0.8 add_divide_fusion
  2.8 1.8 fusion.36
  6.7 61.6 %gather_weights.1 = (bf16[8,256,1024]{2,1,0:T(8,128)(2,1)}, bf16[8,128,3072]{2,1,0:T(8,128)(2,1)}, f32[8,4,1024]{2,1,0:T(4,128)}, f32[4,8,128]{2,1,0:T(8,128)}) custom-call(bf16[256,1024]{1,0:T(8,128)(2,1)} %refs_0_.1, bf16[128,3072]{1,0:T(8,128)(2,1)} %refs_1_.1, f32[8,4,1024]{2,1,0:T(4,128)} %copy-done.17, f32[8,128]{1,0:T(8,128)} %pad_convert_fusion.refs_3_), custom_call_target="tpu_custom_call" | custom-call | tf_op jit(solution)/shard_map/gather_weights/pallas_call | solution.py:974
  72.2 5.3 collective-permute-start
  77.8 2.0 collective-permute-start.2
  79.8 1.5 slice.74
  81.3 1.6 reshape.380
  83.1 1.5 pad_maximum_fusion.1
  84.6 4.1 fusion.35
  89.2 4.0 fusion.24
  93.6 2.7 fusion.37
  97.2 1.0 fusion.13
  98.2 1.9 fusion.34
  101.2 1.3 slice_reduce_fusion
  102.5 1.6 reshape.396.refs_11_
  104.8 1.3 copy.61
  106.1 1.1 copy.51
  107.2 3.0 copy.47
  110.2 0.8 select_reduce_fusion
  111.0 1.3 subtract_convert_fusion.2
  112.2 0.8 convert_element_type.127
  113.0 3.0 copy.48
  116.0 1.5 fusion.21
  117.6 2.3 subtract_convert_fusion.1
  119.9 1.4 pad_maximum_fusion.2
  121.3 4.1 convert_element_type.129
  125.5 3.6 copy.50
  129.0 3.8 convert_element_type.128
  132.9 3.6 copy.49
  137.7 0.8 mul.316
  138.4 1.5 tile.8
  139.9 1.7 copy.55.refs_2_
  141.7 0.8 pad_maximum_fusion.4
  143.2 1.7 copy.56.refs_3_
  144.9 0.8 slice_reduce_fusion.1.refs_0_
  145.7 3.3 maximum_bitcast_fusion.refs_1_
  149.0 88.9 %attend_forward.1 = (bf16[8,2,3,192,128]{4,3,2,1,0:T(8,128)(2,1)}, bf16[8,2,192,128]{3,2,1,0:T(8,128)(2,1)S(1)}, f32[2,2,1,1536]{3,2,1,0:T(1,128)S(1)}, bf16[8,1...) custom-call(s32[2]{0:T(128)S(1)} %slice_reduce_fusion.1.refs_0_, ...), custom_call_target="tpu_custom_call" | custom-call | tf_op jit(solution)/shard_map/attend_forward/pallas_call | solution.py:672
  238.5 0.9 copy-done.7
  239.4 3.3 fusion.33
  243.4 1.7 copy-done.26
  245.1 3.4 fusion.38
  248.6 9.8 %fusion.29 = (f32[384,1024]{1,0:T(8,128)S(1)}, f32[384,1024]{1,0:T(8,128)S(1)}) fusion(bf16[2,192,1024]{2,1,0:T(8,128)(2,1)S(1)} %copy-done.10, f32[384]{0:T(512)S(1)} %mul.316, f32[384,1024]{1,0:T(8,128)S(1)} %get-tuple-element.95, f32[384,6144]{1,0:T(8,128)S(1)} %bitcast.102, bf16[4096,1024]{1,0:T(8,128)(2,1)} %bitcast.144, f32[384,4096]{1,0:T(8,128)S(1)} %fusion.38), kind=kOutput, calls=%fused_computation.94 | convolution fusion | flops 3237740544 | bytes 21759488 | tf_op jit(solution)/shard_map/dot_general | solution.py:21
  258.8 14.1 %fusion.6 = bf16[384,4096]{1,0:T(8,128)(2,1)} fusion(f32[384,4096]{1,0:T(8,128)} %copy-done.27, bf16[384,1024]{1,0:T(8,128)(2,1)S(1)} %multiply_convert_fusion.2, bf16[4096,1024]{1,0:T(8,128)(2,1)} %bitcast.145), kind=kOutput, calls=%fused_computation.10 | convolution fusion | flops 3252682752 | bytes 18612224 | tf_op jit(solution)/shard_map/dot_general | solution.py:31
  272.8 10.5 %convolution_convert_fusion.1 = bf16[4096,1024]{1,0:T(8,128)(2,1)} fusion(bf16[384,1024]{1,0:T(8,128)(2,1)S(1)} %multiply_convert_fusion.2, f32[384,4096]{1,0:T(8,128)} %copy-done.27), kind=kOutput, calls=%fused_computation.3 | convolution fusion | flops 3239575552 | bytes 15466496 | tf_op jit(solution)/shard_map/dot_general | solution.py:25
  283.3 7.1 %multiply_reduce_fusion = (f32[384]{0:T(512)S(1)}, f32[384,1024]{1,0:T(8,128)S(1)}) fusion(f32[384,1024]{1,0:T(8,128)S(1)} %get-tuple-element.95, f32[384]{0:T(512)S(1)} %broadcast_multiply_fusion, f32[384,6144]{1,0:T(8,128)S(1)} %bitcast.104, bf16[384,4096]{1,0:T(8,128)(2,1)} %fusion.6, bf16[1024,4096]{1,0:T(8,128)(2,1)} %bitcast.142), kind=kOutput, calls=%fused_computation.29 | convolution fusion | flops 3223191040 | bytes 16256000 | tf_op jit(solution)/shard_map/dot_general | solution.py:31
  290.4 9.0 %convolution_convert_fusion = bf16[1024,4096]{1,0:T(8,128)(2,1)} fusion(bf16[384,1024]{1,0:T(8,128)(2,1)S(1)} %fusion.7, bf16[384,4096]{1,0:T(8,128)(2,1)} %fusion.6), kind=kOutput, calls=%fused_computation.2 | convolution fusion | flops 3225419776 | bytes 12320768 | tf_op jit(solution)/shard_map/dot_general | solution.py:25
  300.2 1.5 fusion.31
  302.0 1.8 copy-done.11
  303.8 1.0 fusion.12
  304.8 2.6 convolution_convert_fusion.2
  307.6 1.1 copy.77
  309.3 2.2 fusion.23
  312.3 103.2 %attend_backward.1 = (bf16[8,2,3,192,128]{4,3,2,1,0:T(8,128)(2,1)}, bf16[576,512]{1,0:T(8,128)(2,1)}, bf16[576,512]{1,0:T(8,128)(2,1)}, bf16[576,512]{1,0:T(8,128)(2,1)}, bf16[576,512]{1,0:T(8,128)(2,1)}) custom-call(s32[2]{0:T(128)} %copy-done.4, bf16[8,2,3,192,128]{4,3,2,1,0:T(8,128)(2,1)} %get-tuple-element.72.refs_1_, ...), custom_call_target="tpu_custom_call" | custom-call | tf_op jit(solution)/shard_map/attend_backward/pallas_call | solution.py:850
  415.6 118.2 %finish_backward.1 = (f32[384,1024]{1,0:T(8,128)}, f32[384,1024]{1,0:T(8,128)}, bf16[128,3072]{1,0:T(8,128)(2,1)}, bf16[256,1024]{1,0:T(8,128)(2,1)}, bf16[512,1...) custom-call(s32[2]{0:T(128)} %copy-done.4, ...), custom_call_target="tpu_custom_call" | custom-call | tf_op jit(solution)/shard_map/finish_backward/pallas_call | solution.py:1257
  535.2 2.2 convert_element_type.143
  537.4 1.1 convert.31
  539.1 1.3 convert_element_type.148
  540.4 0.8 convert_element_type.149
  541.2 1.5 convert_element_type.150
  542.7 1.6 convert_element_type.151
  544.3 2.3 fusion.39
  546.6 1.1 copy.87
  547.7 0.8 copy-done.12
  548.5 1.1 copy.88
  (116 shorter events, 18.6 us)
Async XLA Ops:
  0.6 4.1 copy-start.23
  0.7 67.7 %copy-start.2 = (bf16[128,1024]{1,0:T(8,128)(2,1)S(1)}, bf16[128,1024]{1,0:T(8,128)(2,1)}, u32[]{:S(2)}) copy-start(bf16[128,1024]{1,0:T(8,128)(2,1)} %refs_2_.1) | copy-start | bytes 786436
  0.7 68.4 %copy-start = (bf16[128,4096]{1,0:T(8,128)(2,1)S(1)}, bf16[128,4096]{1,0:T(8,128)(2,1)}, u32[]{:S(2)}) copy-start(bf16[128,4096]{1,0:T(8,128)(2,1)} %refs_3_.1) | copy-start | bytes 3145732
  2.8 68.7 %copy-start.1 = (bf16[512,1024]{1,0:T(8,128)(2,1)S(1)}, bf16[512,1024]{1,0:T(8,128)(2,1)}, u32[]{:S(2)}) copy-start(bf16[512,1024]{1,0:T(8,128)(2,1)} %refs_4_.1) | copy-start | bytes 3145732
  4.7 78.3 %copy-start.24 = (s32[2,2]{1,0:T(2,128)S(1)}, s32[2,2]{1,0:T(2,128)}, u32[]{:S(2)}) copy-start(s32[2,2]{1,0:T(2,128)} %param.19) | copy-start | bytes 52
  6.1 0.7 copy-start.17
  72.2 76.7 %collective-permute-start = (bf16[576,512]{1,0:T(8,128)(2,1)}, bf16[576,512]{1,0:T(8,128)(2,1)S(1)}, u32[]{:S(2)}, u32[]{:S(2)}) collective-permute-start(bf16[576,512]{1,0:T(8,128)(2,1)} %dynamic-slice_dynamic-update-slice_fusion), channel_id=1, source_target_pairs={{0,2},{1,3},{2,4},{3,5},{4,6},{5,7},{6,0},{7,1},{8,10},{9,11},{10,... | collective-permute-start | bytes 1769480 | tf_op jit(solution)/shard_map/ppermute | solution.py:1307
  77.6 71.4 %collective-permute-start.1 = (bf16[576,512]{1,0:T(8,128)(2,1)}, bf16[576,512]{1,0:T(8,128)(2,1)S(1)}, u32[]{:S(2)}, u32[]{:S(2)}) collective-permute-start(bf16[576,512]{1,0:T(8,128)(2,1)} %dynamic-slice_dynamic-update-slice_fusion), channel_id=1, source_target_pairs={{0,4},{1,5},{2,6},{3,7},{4,0},{5,1},{6,2},{7,3},{8,12},{9,13},{10,... | collective-permute-start | bytes 1769480 | tf_op jit(solution)/shard_map/ppermute | solution.py:1307
  77.8 71.2 %collective-permute-start.2 = (bf16[576,512]{1,0:T(8,128)(2,1)}, bf16[576,512]{1,0:T(8,128)(2,1)}, u32[]{:S(2)}, u32[]{:S(2)}) collective-permute-start(bf16[576,512]{1,0:T(8,128)(2,1)} %dynamic-slice_dynamic-update-slice_fusion), channel_id=1, source_target_pairs={{0,6},{1,7},{2,0},{3,1},{4,2},{5,3},{6,4},{7,5},{8,14},{9,15},{10,... | collective-permute-start | bytes 1769480 | tf_op jit(solution)/shard_map/ppermute | solution.py:1307
  83.1 5.9 %copy-start.25 = (s32[192]{0:T(256)}, s32[192]{0:T(256)S(1)}, u32[]{:S(2)}) copy-start(s32[192]{0:T(256)S(1)} %iota_add_fusion) | copy-start | bytes 2308
  84.6 4.6 copy-start.20
  88.7 4.5 copy-start.6
  88.8 4.9 slice-start.3
  89.2 4.4 slice-start.4
  93.2 3.5 copy-start.5
  93.6 3.6 copy-start.9
  117.6 2.3 copy-start.18
  117.6 2.3 copy-start.19
  145.7 3.3 copy-start.4
  149.0 94.0 %slice-start = ((s8[9437184]{0:T(1024)(128)(4,1)}), s8[4194304]{0:T(1024)(128)(4,1)S(1)}, s32[]{:S(2)}) async-start(s8[9437184]{0:T(1024)(128)(4,1)} %bitcast.99), calls=%async_computation | async-start | bytes 8388608
  149.0 94.0 %slice-start.1 = ((s8[9437184]{0:T(1024)(128)(4,1)}), s8[1048576]{0:T(1024)(128)(4,1)S(1)}, s32[]{:S(2)}) async-start(s8[9437184]{0:T(1024)(128)(4,1)} %bitcast.99), calls=%async_computation.1 | async-start | bytes 2097152
  237.9 4.8 copy-start.3
  237.9 1.4 copy-start.7
  239.4 3.7 slice-start.2
  239.4 5.8 %copy-start.26 = (bf16[8,128,4096]{2,1,0:T(8,128)(2,1)S(1)}, bf16[8,128,4096]{2,1,0:T(8,128)(2,1)}, u32[]{:S(2)}) copy-start(bf16[8,128,4096]{2,1,0:T(8,128)(2,1)} %get-tuple-element.70) | copy-start | bytes 25165828
  245.1 3.4 copy-start.10
  248.5 9.9 %copy-start.27 = (f32[384,4096]{1,0:T(8,128)}, f32[384,4096]{1,0:T(8,128)S(1)}, u32[]{:S(2)}) copy-start(f32[384,4096]{1,0:T(8,128)S(1)} %fusion.38) | copy-start | bytes 18874372
  301.6 3.2 copy-start.8
  301.6 2.2 copy-start.11
  415.5 119.0 %copy-start.22 = (f32[2,2,1024]{2,1,0:T(2,128)S(1)}, f32[2,2,1024]{2,1,0:T(2,128)}, u32[]{:S(2)}) copy-start(f32[2,2,1024]{2,1,0:T(2,128)} %param.18) | copy-start | bytes 49156
  535.2 3.9 copy-start.16
  538.5 1.9 copy-start.21
  538.8 2.4 copy-start.15
  540.4 2.4 copy-start.14
  544.3 2.3 copy-start.13
  546.6 2.0 copy-start.12

commit v6 on v5

--- a/solution.py
+++ b/solution.py
@@ -188,6 +188,9 @@
         _, rows, cols = self.fulls[index].shape
         return rows, rows // self.place.rows_y, cols // (2 * self.place.cols_x)
 
+    def owner(self, step):
+        return self.place.line_from[step]
+
     def begin(self):
         place = self.place
         for index, step in self.jobs:
@@ -201,8 +204,8 @@
     def spread_first(self, index, step):
         place = self.place
         rows, height, width = self.sizes(index)
-        full = self.fulls[index].at[place.line_from[step]]
-        piece = self.pieces[step]
+        full = self.fulls[index].at[self.owner(step)]
+        piece = self.pieces.at[step]
         first_row, first_col = place.gy * height, 2 * place.gx * width
         self.local[index, step] = []
         self.waiting[index, step] = []
@@ -225,7 +228,7 @@
             copy.wait()
         for copy in self.waiting[index, step]:
             copy.wait_recv()
-        full = self.fulls[index].at[place.line_from[step]]
+        full = self.fulls[index].at[self.owner(step)]
         copies = []
         for hop, other in enumerate(place.along):
             for spot, column in enumerate([place.gx] + place.beside_from):
@@ -240,7 +243,7 @@
         place = self.place
         for copy in self.waiting[index, step]:
             copy.wait_recv()
-        full = self.fulls[index].at[place.line_from[step]]
+        full = self.fulls[index].at[self.owner(step)]
         self.waiting[index, step] = [
             place.push(full, full, *self.core, (index, step + 1), (place.grp, place.partner))
         ]
@@ -252,14 +255,17 @@
     def late(self):
         return [functools.partial(self.over_core, *job) for job in self.jobs]
 
+    def arrive(self, index):
+        for job in self.jobs:
+            if job[0] == index:
+                for copy in self.waiting[job]:
+                    copy.wait_recv()
+        copy, push = self.own[index]
+        copy.wait()
+        push.wait_recv()
+
     def finish(self):
         self.place.sent()
-        for job in self.jobs:
-            for copy in self.waiting[job]:
-                copy.wait_recv()
-        for copy, push in self.own:
-            copy.wait()
-            push.wait_recv()
 
 
 def add_rows(target, source, first_row, rows, first_col, cols, out=None):
@@ -545,7 +551,7 @@
     layers = seq_count // 2
     bound_ref, qkv_ref, shards = refs[0], refs[1], refs[2:2 + count]
     refs = refs[2 + count:]
-    pieces, refs = refs[:layers - 1], refs[layers - 1:]
+    pieces, refs = refs[0], refs[1:]
     kept_ref, mixture_ref, log_ref, fulls = refs[0], refs[1], refs[2], refs[3:3 + count]
     (
         key_scr, query_scr, value_t_scr, score_scr, mix_t_scr, mix_scr,
@@ -563,7 +569,8 @@
     place = Place(plane, seq_count)
     enter([(grp, other) for other in others] + [(other, me) for other in place.beside + place.along])
     copies = []
-    for group in range(group_count):
+
+    def begin_group(group):
         own = pltpu.make_async_copy(qkv_ref.at[me, group], kept_ref.at[me, group], local_sem.at[group])
         own.start()
         row = [own]
@@ -576,6 +583,8 @@
             copy.start()
             row.append(copy)
         copies.append(row)
+
+    begin_group(0)
     side = place.cols_x
     segments, _ = piece_segments(
         [shard.shape for shard in shards], side, min(shard.shape[1] for shard in shards) // side
@@ -589,6 +598,8 @@
     for group in range(group_count):
         for copy in copies[group]:
             copy.wait()
+        if group + 1 < group_count:
+            begin_group(group + 1)
         if group == 0:
             spread.middle()
             hooks = spread.late()
@@ -654,6 +665,8 @@
         hook()
     for copy in back:
         copy.wait()
+    for index in range(count):
+        spread.arrive(index)
     spread.finish()
 
 
@@ -676,7 +689,7 @@
             jax.ShapeDtypeStruct((seq_count, group_count, local_rows, local_width), jnp.bfloat16),
             jax.ShapeDtypeStruct((group_count, heads, 1, total_rows), jnp.float32),
         ) + tuple(jax.ShapeDtypeStruct((seq_count,) + part.shape, part.dtype) for part in shards),
-        in_specs=[pl.BlockSpec(memory_space=pltpu.SMEM)] + [anywhere] * (count + layers),
+        in_specs=[pl.BlockSpec(memory_space=pltpu.SMEM)] + [anywhere] * (2 + count),
         out_specs=(vmem, vmem, vmem) + (anywhere,) * count,
         scratch_shapes=[
             pltpu.VMEM((total_rows, local_width + 128), jnp.bfloat16),
@@ -699,7 +712,7 @@
             collective_id=1, has_side_effects=True, vmem_limit_bytes=48 * 1024 * 1024
         ),
         name="attend_forward",
-    )(bounds, qkv, *shards, *pieces)
+    )(bounds, qkv, *shards, pieces)
 
 
 def backward_kernel(plane, seq_count, count, *refs):
@@ -724,7 +737,8 @@
     place = Place(plane, seq_count)
     enter([(grp, other) for other in others] + [(other, me) for other in place.beside + place.along])
     copies = []
-    for group in range(group_count):
+
+    def begin_group(group):
         own = pltpu.make_async_copy(grad_ref.at[me, group], taken_scr.at[me, group], local_sem.at[group])
         own.start()
         row = [own]
@@ -737,6 +751,8 @@
             copy.start()
             row.append(copy)
         copies.append(row)
+
+    begin_group(0)
     side = place.cols_x
     segments, _ = piece_segments(
         [part.shape[1:] for part in parts], side, min(part.shape[2] for part in parts) // side
@@ -755,6 +771,8 @@
     for group in range(group_count):
         for copy in copies[group]:
             copy.wait()
+        if group + 1 < group_count:
+            begin_group(group + 1)
         boundary = bound_ref[group]
         keys = kept_ref[:, group, 1].reshape(total_rows, local_width)
         key_scr[:, :local_width] = keys
@@ -880,23 +898,88 @@
     )(bounds, kept, grad, log_total, *parts)
 
 
+class LineChain:
+    def __init__(self, place, sources, slots, sends, recvs):
+        self.place, self.sources, self.slots = place, sources, slots
+        self.sends, self.recvs = sends, recvs
+        self.pushed = []
+        middle = []
+        low, high = 0, place.layers - 2
+        while low <= high:
+            middle += [low] if low == high else [low, high]
+            low, high = low + 1, high - 1
+        first, last = place.layer == 0, place.layer == place.layers - 1
+        self.ranks = [
+            jnp.where(first, place.layers - 2 - rank, jnp.where(last, rank, step)).astype(jnp.int32)
+            for rank, step in enumerate(middle)
+        ]
+
+    def owner(self, step):
+        place = self.place
+        return lax.rem(place.layer + place.layers - 1 - step, place.layers) * 2 + place.core
+
+    def copy(self, index, source, owner, slot, target, send_slot):
+        return pltpu.make_async_remote_copy(
+            source, self.slots(index, owner, slot),
+            self.sends.at[index, send_slot], self.recvs.at[index, slot],
+            device_id=(self.place.grp, target * 2 + self.place.core), device_id_type=MESH,
+        )
+
+    def push(self, when, *given):
+        self.pushed.append((when, given))
+
+        @pl.when(when)
+        def _():
+            self.copy(*given).start()
+
+    def begin(self, index):
+        place = self.place
+        source = self.sources[index]
+        self.push(place.layer < place.layers - 1, index, source, place.me, 0, place.layer + 1, 0)
+        self.push(place.layer > 0, index, source, place.me, place.layers - 2, place.layer - 1, 1)
+
+    def forward(self, index, rank):
+        place = self.place
+        step = self.ranks[rank]
+        owner = self.owner(step)
+        held = self.slots(index, owner, step)
+        self.copy(index, held, owner, step, place.layer, 0).wait_recv()
+        below = step < place.layer
+        going = (below & (place.layer < place.layers - 1)) | ((step >= place.layer) & (place.layer > 0))
+        slot = jnp.where(below, step + 1, step - 1)
+        target = jnp.where(below, place.layer + 1, place.layer - 1)
+        self.push(going, index, held, owner, slot, target, rank + 2)
+        return owner
+
+    def sent(self):
+        for when, given in self.pushed:
+
+            @pl.when(when)
+            def _(given=given):
+                self.copy(*given).wait_send()
+
+
 class WholeGather(PlaneGather):
     def __init__(self, place, shards, fulls, line_send, line_recv, *semaphores):
         super().__init__(place, shards, None, None, fulls, *semaphores)
-        self.line = (line_send, line_recv)
-        self.jobs = [(index, step) for index in range(len(shards)) for step in range(place.layers - 1)]
-        self.lines = {}
+
+        def piece(ref, index):
+            rows, height, width = self.sizes(index)
+            return window(ref, place.gy * height, height, 2 * place.gx * width, 2 * width)
+
+        self.chain = LineChain(
+            place, [piece(shard, index) for index, shard in enumerate(shards)],
+            lambda index, owner, slot: piece(fulls[index].at[owner], index), line_send, line_recv,
+        )
+        self.jobs = [(index, rank) for index in range(len(shards)) for rank in range(place.layers - 1)]
+
+    def owner(self, step):
+        return self.chain.owner(self.chain.ranks[step])
 
     def begin(self):
         place = self.place
-        for index, step in self.jobs:
-            rows, height, width = self.sizes(index)
-            row, col = place.gy * height, 2 * place.gx * width
-            self.lines[index, step] = place.push(
-                window(self.shards[index], row, height, col, 2 * width),
-                window(self.fulls[index].at[place.me], row, height, col, 2 * width),
-                *self.line, (index, step), (place.grp, place.lines[step]),
-            )
+        for index in range(len(self.shards)):
+            self.chain.begin(index)
         for index, shard in enumerate(self.shards):
             copy = pltpu.make_async_copy(shard, self.fulls[index].at[place.me], self.own_sem.at[index, place.layers - 1, 0, 0])
             copy.start()
@@ -906,8 +989,7 @@
     def spread_first(self, index, step):
         place = self.place
         rows, height, width = self.sizes(index)
-        self.lines[index, step].wait_recv()
-        full = self.fulls[index].at[place.line_from[step]]
+        full = self.fulls[index].at[self.chain.forward(index, step)]
         row, col = place.gy * height, 2 * place.gx * width
         self.waiting[index, step] = []
         for half, partners in enumerate((place.beside, place.along)):
@@ -917,102 +999,205 @@
                     place.push(part, part, *self.first, (index, step, half, hop, 0), (other, place.me))
                 )
 
-    def steps(self):
-        lag = self.place.layers - 1
-        done = []
-        for turn in range(len(self.jobs) + 2 * lag):
-            if turn < len(self.jobs):
-                done.append(functools.partial(self.spread_first, *self.jobs[turn]))
-            if 0 <= turn - lag < len(self.jobs):
-                done.append(functools.partial(self.spread_second, *self.jobs[turn - lag]))
-            if 0 <= turn - 2 * lag < len(self.jobs):
-                done.append(functools.partial(self.over_core, *self.jobs[turn - 2 * lag]))
-        return done
-
-
-def gather_kernel(plane, seq_count, count, *refs):
-    shards, (partial_ref, token_ref), refs = refs[:count], refs[count:count + 2], refs[count + 2:]
-    fulls, (total_ref, tokens_ref), refs = refs[:count], refs[count:count + 2], refs[count + 2:]
-    token_scr, token_send, token_recv = refs[:3]
-    small_refs, refs = refs[3:8], refs[8:]
+    def finish(self):
+        super().finish()
+        self.chain.sent()
+
+
+def turn_lanes(values, cos, sin):
+    lane = lax.broadcasted_iota(jnp.int32, values.shape, 1)
+    ahead = pltpu.roll(values, values.shape[1] - HEAD_DIM // 2, 1)
+    behind = pltpu.roll(values, HEAD_DIM // 2, 1)
+    other = jnp.where(lax.rem(lane, HEAD_DIM) < HEAD_DIM // 2, ahead, behind)
+    return values * cos + other * sin
+
+
+def second_mask(bound_ref, group, me, local_rows, first, rows):
+    row = lax.broadcasted_iota(jnp.int32, (rows, 1), 0) + (me * local_rows + first)
+    return row >= bound_ref[group]
+
+
+def centered(values):
+    center = values - jnp.mean(values, axis=-1, keepdims=True)
+    scale = lax.rsqrt(jnp.mean(center * center, axis=-1, keepdims=True) + epsilon)
+    return center * scale, scale
+
+
+def front_kernel(plane, seq_count, late_count, *refs):
+    layers = seq_count // 2
+    bound_ref, frames_ref, shortcut_ref, cos_ref, sin_ref, partial_ref, token_ref = refs[:7]
+    shards, late_shards, refs = refs[7:9], refs[9:9 + late_count], refs[9 + late_count:]
+    fulls_out, late_out, refs = refs[:2], refs[2], refs[3:]
+    hidden_ref, normed_ref, qkv_ref, total_ref, tokens_ref = refs[:5]
+    fulls, refs = refs[5:7], refs[7:]
+    token_scr, token_send, token_recv, out_sem = refs[:4]
+    small_refs, (late_scr, late_send, late_recv, late_sem), refs = refs[4:9], refs[9:13], refs[13:]
+    group_count, local_rows, local_width = qkv_ref.shape[1], qkv_ref.shape[3], qkv_ref.shape[4]
+    row_count, width = hidden_ref.shape
     place = Place(plane, seq_count)
-    enter([(place.grp, other) for other in place.others] + [(other, place.me) for other in place.groups])
+    me = place.me
+    enter([(place.grp, other) for other in place.others] + [(other, me) for other in place.groups])
     whole = WholeGather(place, shards, fulls, *refs)
     whole.begin()
     small = SmallSum(place, partial_ref, total_ref, *small_refs)
     small.begin()
-    hooks = whole.steps()
-    for hook in hooks[:len(hooks) // 2]:
-        hook()
+    side = place.cols_x
+    cut = late_scr.shape[1]
+    late_own, base = [], 0
+    for index, shard in enumerate(late_shards):
+        height, cols = shard.shape[0] // side, shard.shape[1] // side
+        for spot in range(cols // cut):
+            late_own.append(pltpu.make_async_copy(
+                window(shard, place.gy * height, height, place.gx * cols + spot * cut, cut),
+                late_scr.at[pl.ds(base, height), :],
+                late_sem.at[len(late_own)],
+            ))
+            late_own[-1].start()
+            base += height
+    late_chain = LineChain(place, [late_scr], lambda index, owner, slot: late_out.at[slot], late_send, late_recv)
+    combine_jobs = [job for job in whole.jobs if job[0] == 0]
+    projection_jobs = [job for job in whole.jobs if job[0] == 1]
+    for job in combine_jobs:
+        whole.spread_first(*job)
+    for job, late in zip(combine_jobs, projection_jobs):
+        whole.spread_second(*job)
+        whole.spread_first(*late)
+    for copy in late_own:
+        copy.wait()
+    late_chain.begin(0)
     small.middle()
-    for hook in hooks[len(hooks) // 2:]:
-        hook()
+    for job, late in zip(combine_jobs, projection_jobs):
+        whole.over_core(*job)
+        whole.spread_second(*late)
+    whole.arrive(0)
+    outs = [pltpu.make_async_copy(fulls[0], fulls_out[0], out_sem.at[0])]
+    outs[0].start()
+    late_chain.forward(0, 0)
+    half = seq_count // 2
+
+    def hidden_tile(index, carry):
+        at = pl.ds(pl.multiple_of(index * 256, 256), 256)
+        upper = fulls[0][0:half, :, at].reshape(width, 256)
+        lower = fulls[0][half:seq_count, :, at].reshape(width, 256)
+        hidden_ref[:, at] = dot_nn(frames_ref[...], upper) + dot_nn(shortcut_ref[...], lower)
+        return carry
+
+    lax.fori_loop(0, width // 256, hidden_tile, 0)
     small.finish()
     last = total_ref.shape[1] - 1
     token_scr[...] = token_ref[...]
     token_scr[4:5, :] = total_ref[seq_count - 1, last:last + 1, :128]
     tokens_ref[place.grp] = token_scr[...]
     tokens = [
-        place.push(token_scr, tokens_ref.at[place.grp], token_send, token_recv, step, (other, place.me))
+        place.push(token_scr, tokens_ref.at[place.grp], token_send, token_recv, step, (other, me))
         for step, other in enumerate(place.groups)
     ]
+    block = total_ref.shape[1]
+
+    def vector(group, part, second):
+        def row(utter):
+            at = (group * 2 + utter) * 6 + part
+            return total_ref[at // block, at % block:at % block + 1, :]
+
+        return jnp.where(second, row(1), row(0))
+
+    chunk = 32
+    for group in range(group_count):
+
+        def norm_rows(index, carry):
+            first = pl.multiple_of(index * chunk, chunk)
+            at = pl.ds(pl.multiple_of(group * local_rows + first, chunk), chunk)
+            second = second_mask(bound_ref, group, me, local_rows, first, chunk)
+            normal, _ = centered(hidden_ref[at, :])
+            normed_ref[at, :] = (
+                normal * (1.0 + vector(group, 1, second)) + vector(group, 0, second)
+            ).astype(jnp.bfloat16)
+            return carry
+
+        lax.fori_loop(0, local_rows // chunk, norm_rows, 0)
+    for job in projection_jobs:
+        whole.over_core(*job)
+    whole.arrive(1)
+    late_chain.forward(0, 1)
+    outs.append(pltpu.make_async_copy(fulls[1], fulls_out[1], out_sem.at[1]))
+    outs[1].start()
+    each = 256 // local_width
+
+    def head_tile(index, carry):
+        for kind in range(3):
+            at = pl.ds(pl.multiple_of(kind * width + index * 256, 256), 256)
+            packed = dot_nn(normed_ref[...], fulls[1][:, :, at].reshape(width, 256))
+            for half in range(2):
+                lanes = packed[:, half * 128:(half + 1) * 128]
+                if kind < 2:
+                    lanes = turn_lanes(lanes, cos_ref[...], sin_ref[...])
+                lanes = lanes.astype(jnp.bfloat16)
+                for spot in range(each // 2):
+                    cut = lanes[:, spot * local_width:(spot + 1) * local_width]
+                    for group in range(group_count):
+                        qkv_ref[index * each + half * (each // 2) + spot, group, kind] = cut[
+                            group * local_rows:(group + 1) * local_rows
+                        ]
+        return carry
+
+    lax.fori_loop(0, width // 256, head_tile, 0)
+    for rank in range(2, layers - 1):
+        late_chain.forward(0, rank)
     whole.finish()
+    late_chain.sent()
     for copy in tokens:
         copy.wait_recv()
-
-
-def gather(collective, partial, token, *shards):
+    for copy in outs:
+        copy.wait()
+
+
+def front(bounds, frames, shortcut, cos, sin, partial, token, combine, projection, late_shards):
     grp_count = lax.axis_size("grp")
     seq_count = lax.axis_size("seq")
     side = math.isqrt(grp_count)
     layers = seq_count // 2
-    count = len(shards)
     anywhere = pl.BlockSpec(memory_space=pl.ANY)
     vmem = pl.BlockSpec(memory_space=pltpu.VMEM)
     dma = pltpu.SemaphoreType.DMA
     hops = max(side - 1, 1)
-    outs = pl.pallas_call(
-        functools.partial(gather_kernel, (side, side), seq_count, count),
-        out_shape=tuple(
-            jax.ShapeDtypeStruct((seq_count,) + part.shape, part.dtype) for part in shards
-        ) + (
-            jax.ShapeDtypeStruct(partial.shape, jnp.float32),
-            jax.ShapeDtypeStruct((grp_count,) + token.shape, jnp.float32),
+    shards = (combine, projection)
+    group_count = bounds.shape[0]
+    row_count, width = frames.shape
+    low, full = jnp.bfloat16, jnp.float32
+    cut = min(shard.shape[1] for shard in late_shards) // side
+    late_rows = sum(shard.shape[0] // side * (shard.shape[1] // side // cut) for shard in late_shards)
+    most = max(shard.shape[1] // side // cut for shard in late_shards)
+    wholes = [(seq_count,) + part.shape for part in shards]
+    return pl.pallas_call(
+        functools.partial(front_kernel, (side, side), seq_count, len(late_shards)),
+        out_shape=tuple(jax.ShapeDtypeStruct(shape, low) for shape in wholes) + (
+            jax.ShapeDtypeStruct((layers - 1, late_rows, cut), low),
+            jax.ShapeDtypeStruct((row_count, width), full),
+            jax.ShapeDtypeStruct((row_count, width), low),
+            jax.ShapeDtypeStruct(
+                (seq_count, group_count, 3, row_count // group_count, width // seq_count), low
+            ),
+            jax.ShapeDtypeStruct(partial.shape, full),
+            jax.ShapeDtypeStruct((grp_count,) + token.shape, full),
         ),
-        in_specs=[anywhere] * count + [vmem] * 2,
-        out_specs=(anywhere,) * count + (vmem,) * 2,
-        scratch_shapes=[
-            pltpu.VMEM(token.shape, jnp.float32), dma((grp_count - 1,)), dma((grp_count - 1,))
+        in_specs=[pl.BlockSpec(memory_space=pltpu.SMEM)] + [vmem] * 6 + [anywhere] * (2 + len(late_shards)),
+        out_specs=(anywhere,) * 3 + (vmem,) * 5,
+        scratch_shapes=[pltpu.VMEM(shape, low) for shape in wholes] + [
+            pltpu.VMEM(token.shape, full), dma((grp_count - 1,)), dma((grp_count - 1,)), dma((2,)),
         ] + small_scratch(partial) + [
-            dma((count, layers - 1)), dma((count, layers - 1)),
-            dma((count, layers, 1, 1)),
-            dma((count, layers - 1, 2, hops, 1)), dma((count, layers - 1, 2, hops, 1)),
-            dma((count, layers - 1, 2, hops, side)), dma((count, layers - 1, 2, hops, side)),
-            dma((count, layers)), dma((count, layers)),
+            pltpu.VMEM((late_rows, cut), low),
+            dma((1, layers + 1)), dma((1, layers - 1)), dma((len(late_shards) * most,)),
+            dma((2, layers + 1)), dma((2, layers - 1)),
+            dma((2, layers, 1, 1)),
+            dma((2, layers - 1, 2, hops, 1)), dma((2, layers - 1, 2, hops, 1)),
+            dma((2, layers - 1, 2, hops, side)), dma((2, layers - 1, 2, hops, side)),
+            dma((2, layers)), dma((2, layers)),
         ],
-        compiler_params=pltpu.CompilerParams(collective_id=collective, has_side_effects=True),
-        name="gather_weights",
-    )(*shards, partial, token)
-    return outs[:count], outs[count], outs[count + 1]
-
-
-def turn_lanes(values, cos, sin):
-    lane = lax.broadcasted_iota(jnp.int32, values.shape, 1)
-    ahead = pltpu.roll(values, values.shape[1] - HEAD_DIM // 2, 1)
-    behind = pltpu.roll(values, HEAD_DIM // 2, 1)
-    other = jnp.where(lax.rem(lane, HEAD_DIM) < HEAD_DIM // 2, ahead, behind)
-    return values * cos + other * sin
-
-
-def second_mask(bound_ref, group, me, local_rows, first, rows):
-    row = lax.broadcasted_iota(jnp.int32, (rows, 1), 0) + (me * local_rows + first)
-    return row >= bound_ref[group]
-
-
-def centered(values):
-    center = values - jnp.mean(values, axis=-1, keepdims=True)
-    scale = lax.rsqrt(jnp.mean(center * center, axis=-1, keepdims=True) + epsilon)
-    return center * scale, scale
+        compiler_params=pltpu.CompilerParams(
+            collective_id=3, has_side_effects=True, vmem_limit_bytes=48 * 1024 * 1024
+        ),
+        name="front",
+    )(bounds, frames, shortcut, cos, sin, partial, token, *shards, *late_shards)
 
 
 def back_kernel(plane, seq_count, *refs):
@@ -1301,28 +1486,6 @@
     )(bounds, back, cos, sin, normed, hidden, middle_grad, frames, shortcut, combine, projection, mods, late, modulation, *finished)
 
 
-def line_shift(values, step):
-    seq_count = lax.axis_size("seq")
-    turned = [(spot, (spot + 2 * step) % seq_count) for spot in range(seq_count)]
-    return lax.ppermute(values, "seq", turned)
-
-
-def line_pieces(shards):
-    side = math.isqrt(lax.axis_size("grp"))
-    layers = lax.axis_size("seq") // 2
-    grp = lax.axis_index("grp")
-    width = min(shard.shape[1] for shard in shards) // side
-    blocks = []
-    for shard in shards:
-        height, cols = shard.shape[0] // side, shard.shape[1] // side
-        for off in range(0, cols, width):
-            blocks.append(lax.dynamic_slice(
-                shard, (grp // side * height, lax.rem(grp, side) * cols + off), (height, width)
-            ))
-    joined = jnp.concatenate(blocks)
-    return [line_shift(joined, step) for step in range(1, layers)]
-
-
 def shards(
     frames,
     shortcut,
@@ -1371,14 +1534,24 @@
     token = jnp.zeros((8, 128), jnp.float32)
     token = token.at[:utter_rows, :shard_rows].set(condition_part.astype(jnp.float32))
     late_shards = (readout, expand, contract)
-    (combine_full, projection_full), partial_total, tokens = gather(3, partial, token, combine, projection)
-    late_pieces = line_pieces(lax.optimization_barrier((late_shards, tokens))[0])
+    bounds = lengths[:, 0]
+    combine_full, projection_full, *rest = front(
+        bounds,
+        frames.reshape(row_count, width),
+        shortcut.reshape(row_count, width),
+        cos_lanes,
+        sin_lanes,
+        partial,
+        token,
+        combine,
+        projection,
+        late_shards,
+    )
+    late_pieces, hidden, normed, qkv, partial_total, tokens = rest
     combine_full = combine_full.reshape(2 * width, width)
     projection_full = projection_full.reshape(width, 3 * width)
     kept_total = jnp.sum(tokens[:, 4, 0])
     condition_all = tokens[:, :utter_rows, :shard_rows].reshape(-1, shard_rows).astype(jnp.bfloat16)
-    joined = jnp.concatenate([frames, shortcut], axis=2).reshape(row_count, 2 * width)
-    hidden = product(joined, combine_full)
     modulation_utter = partial_total.reshape(32, width)[:6 * utter_rows].reshape(
         group_count, utter_count, 6 * width
     )
@@ -1392,28 +1565,8 @@
     shift_first, scale_first, gate_first, shift_second, scale_second, gate_second = jnp.split(
         modulation_frame, 6, axis=1
     )
-    normed_value, first_pull = jax.vjp(modulate, hidden, shift_first, scale_first)
-    normed = normed_value.astype(jnp.bfloat16)
-    packed = product(normed, projection_full)
-    query_raw, key_raw, value_raw = jnp.split(packed, 3, axis=1)
-    head_shape = (row_count, HEADS, HEAD_DIM)
     split_shape = (group_count, local_rows, width)
-
-    def rotate_local(vectors):
-        return rotate(vectors, cos_table, sin_table)
-
-    query_turned, query_pull = jax.vjp(rotate_local, query_raw.reshape(head_shape))
-    key_turned, key_pull = jax.vjp(rotate_local, key_raw.reshape(head_shape))
     local_width = width // seq_count
-
-    def by_target(vectors):
-        return vectors.reshape(group_count, local_rows, seq_count, local_width).astype(jnp.bfloat16)
-
-    qkv = jnp.transpose(
-        jnp.stack([by_target(query_turned), by_target(key_turned), by_target(value_raw)]),
-        (3, 1, 0, 2, 4),
-    )
-    bounds = lengths[:, 0]
     kept_heads, mixture_blocks, log_total, *late_full = attend_forward(
         bounds, qkv, late_shards, late_pieces
     )

time: 560 us -> 514 us (0.918)
  the two profiles are of different devices: /device:TPU:8 before, /device:TPU:10 now
where the time goes in v6:
time: 514 us; the launch traced here: 509 us
  Pallas kernels  388 us (75%)
  matrix products  80.8 us (16%)
  other arithmetic  19.5 us (4%)
  local copies, waits for them, and re-layouts  18.6 us (4%)
    pallas_call x1, Pallas kernels, finish_backward(): pl.pallas_call(functools.partial(back_kernel, (side, side), seq_count), o...  119 us
    pallas_call x1, Pallas kernels, attend_backward(): pl.pallas_call(functools.partial(backward_kernel, (side, side), seq_count...  99.9 us
    pallas_call x1, Pallas kernels, attend_forward(): pl.pallas_call(functools.partial(forward_kernel, (side, side), seq_count,...  85.3 us
    pallas_call x1, Pallas kernels, front(): pl.pallas_call(functools.partial(front_kernel, (side, side), seq_count, l...  84.4 us
    dot_general x3, matrix products, product_right(): lax.dot_general(first_op, second_op, (((1,), (1,)), ((), ())), preferred_...  33.4 us
    dot_general x4, matrix products, product_left(): lax.dot_general(first_op, second_op, (((0,), (0,)), ((), ())), preferred_...  23.2 us
    dot_general x4, matrix products, product(): return jnp.dot(first_op, second_op, preferred_element_type=jnp.float32)  18 us

profile of v6, /device:TPU:10, one launch (start us, length us, event | category | flops | bytes accessed | tf_op | source)
XLA Modules:
  0.0 509.3 jit_solution(4462641666031546811)
XLA Ops:
  0.7 1.4 convert_reduce_fusion
  2.1 0.8 slice_reduce_fusion.1.refs_0_
  3.0 0.8 reduce_window_sum.11
  3.8 0.7 sub.36
  4.5 0.1 fusion.19
  4.6 0.1 select_reduce_fusion
  4.8 0.7 add_divide_fusion
  5.5 0.7 fusion.22
  6.2 1.7 fusion.31
  8.1 0.7 scatter.12.refs_5_
  8.8 0.9 fusion.18
  9.7 0.1 copy.42.refs_4_.refs_3_
  9.8 1.5 tile.8
  11.3 1.1 copy.41.refs_3_.refs_2_
  12.5 1.1 copy-done.9
  13.6 1.0 copy-done.10
  14.6 84.4 %front.1 = (bf16[8,256,1024]{2,1,0:T(8,128)(2,1)}, bf16[8,128,3072]{2,1,0:T(8,128)(2,1)}, bf16[3,576,512]{2,1,0:T(8,128)(2,1)}, f32[384,1024]{1,0:T(8,128)}, bf1...) custom-call(s32[2]{0:T(128)S(1)} %slice_reduce_fusion.1.refs_0_, ...), custom_call_target="tpu_custom_call" | custom-call | tf_op jit(solution)/shard_map/front/pallas_call | solution.py:1171
  99.1 0.9 copy-done.8
  100.0 0.6 copy-done.13
  100.6 0.6 slice_reduce_fusion
  102.0 0.7 slice.74
  102.7 0.7 reshape.291.refs_11_
  103.4 0.1 reshape.278
  103.5 4.0 fusion.21
  107.5 85.3 %attend_forward.1 = (bf16[8,2,3,192,128]{4,3,2,1,0:T(8,128)(2,1)}, bf16[8,2,192,128]{3,2,1,0:T(8,128)(2,1)S(1)}, f32[2,2,1,1536]{3,2,1,0:T(1,128)S(1)}, bf16[8,1...) custom-call(s32[2]{0:T(128)S(1)} %slice_reduce_fusion.1.refs_0_, ...), custom_call_target="tpu_custom_call" | custom-call | tf_op jit(solution)/shard_map/attend_forward/pallas_call | solution.py:685
  192.9 0.5 copy.43
  193.4 3.0 fusion.30
  196.5 0.3 multiply_reduce_fusion.1
  196.8 0.4 fusion.7
  197.2 3.4 fusion.32
  200.7 9.9 %fusion.26 = (f32[384,1024]{1,0:T(8,128)S(1)}, f32[384,1024]{1,0:T(8,128)S(1)}) fusion(bf16[2,192,1024]{2,1,0:T(8,128)(2,1)S(1)} %copy-done.16, f32[384]{0:T(512)S(1)} %mul.205, f32[384,1024]{1,0:T(8,128)S(1)} %get-tuple-element.97, f32[384,6144]{1,0:T(8,128)S(1)} %bitcast.86, bf16[4096,1024]{1,0:T(8,128)(2,1)} %bitcast.120, f32[384,4096]{1,0:T(8,128)S(1)} %fusion.32), kind=kOutput, calls=%fused_computation.71 | convolution fusion | flops 3237740544 | bytes 21759488 | tf_op jit(solution)/shard_map/dot_general | solution.py:21
  210.6 0.3 multiply_convert_fusion.2
  210.9 0.9 copy-done.25
  211.8 25.3 %fusion.6 = bf16[384,4096]{1,0:T(8,128)(2,1)} fusion(f32[384,4096]{1,0:T(8,128)} %copy-done.29, bf16[384,1024]{1,0:T(8,128)(2,1)S(1)} %multiply_convert_fusion.2, bf16[4096,1024]{1,0:T(8,128)(2,1)} %bitcast.121), kind=kOutput, calls=%fused_computation.10 | convolution fusion | flops 3252682752 | bytes 18612224 | tf_op jit(solution)/shard_map/dot_general | solution.py:31
  237.1 7.1 %multiply_reduce_fusion = (f32[384]{0:T(512)S(1)}, f32[384,1024]{1,0:T(8,128)S(1)}) fusion(f32[384,1024]{1,0:T(8,128)S(1)} %get-tuple-element.97, f32[384]{0:T(512)S(1)} %broadcast_multiply_fusion, f32[384,6144]{1,0:T(8,128)S(1)} %bitcast.88, bf16[384,4096]{1,0:T(8,128)(2,1)} %fusion.6, bf16[1024,4096]{1,0:T(8,128)(2,1)} %bitcast.116), kind=kOutput, calls=%fused_computation.22 | convolution fusion | flops 3223191040 | bytes 16256000 | tf_op jit(solution)/shard_map/dot_general | solution.py:31
  244.2 11.2 %convolution_convert_fusion.1 = bf16[4096,1024]{1,0:T(8,128)(2,1)} fusion(bf16[384,1024]{1,0:T(8,128)(2,1)} %copy-done.25, f32[384,4096]{1,0:T(8,128)} %copy-done.29), kind=kOutput, calls=%fused_computation.3 | convolution fusion | flops 3239575552 | bytes 15466496 | tf_op jit(solution)/shard_map/dot_general | solution.py:25
  255.4 0.7 fusion.29
  256.1 1.5 fusion.28
  257.6 0.4 multiply_convert_fusion.1
  257.9 1.8 copy-done.17
  259.7 1.0 fusion.10
  260.8 0.2 copy.53
  260.9 1.0 copy.67
  262.0 0.7 pad_maximum_fusion
  262.7 2.2 fusion.20
  265.1 0.6 reshape.294.refs_12_
  265.7 2.6 convolution_convert_fusion.2
  268.3 7.1 %convolution_convert_fusion = bf16[1024,4096]{1,0:T(8,128)(2,1)} fusion(bf16[384,1024]{1,0:T(8,128)(2,1)S(1)} %fusion.7, bf16[384,4096]{1,0:T(8,128)(2,1)S(1)} %copy-done.30), kind=kOutput, calls=%fused_computation.2 | convolution fusion | flops 3225419776 | bytes 12320768 | tf_op jit(solution)/shard_map/dot_general | solution.py:25
  275.5 99.9 %attend_backward.1 = (bf16[8,2,3,192,128]{4,3,2,1,0:T(8,128)(2,1)}, bf16[576,512]{1,0:T(8,128)(2,1)}, bf16[576,512]{1,0:T(8,128)(2,1)}, bf16[576,512]{1,0:T(8,128)(2,1)}, bf16[576,512]{1,0:T(8,128)(2,1)}) custom-call(s32[2]{0:T(128)} %copy-done.12, bf16[8,2,3,192,128]{4,3,2,1,0:T(8,128)(2,1)} %get-tuple-element.70.refs_1_, ...), custom_call_target="tpu_custom_call" | custom-call | tf_op jit(solution)/shard_map/attend_backward/pallas_call | solution.py:868
  375.4 118.6 %finish_backward.1 = (f32[384,1024]{1,0:T(8,128)}, f32[384,1024]{1,0:T(8,128)}, bf16[128,3072]{1,0:T(8,128)(2,1)}, bf16[256,1024]{1,0:T(8,128)(2,1)}, bf16[512,1...) custom-call(s32[2]{0:T(128)} %copy-done.12, ...), custom_call_target="tpu_custom_call" | custom-call | tf_op jit(solution)/shard_map/finish_backward/pallas_call | solution.py:1442
  494.0 0.9 slice_bitcast_fusion
  494.9 0.6 fusion.17
  495.5 1.1 convert.11
  496.7 0.2 copy.51
  497.0 0.1 copy.50
  497.1 0.1 copy.54
  497.2 1.8 convert_element_type.109
  499.0 1.1 convert_element_type.103
  500.1 1.3 convert_element_type.108
  501.4 1.5 convert_element_type.110
  502.9 1.6 convert_element_type.111
  504.5 2.3 fusion.33
  506.8 1.1 copy.72
  507.9 1.1 copy.73
  (83 shorter events, 0.7 us)
Async XLA Ops:
  0.6 11.8 %copy-start = (bf16[128,4096]{1,0:T(8,128)(2,1)S(1)}, bf16[128,4096]{1,0:T(8,128)(2,1)}, u32[]{:S(2)}) copy-start(bf16[128,4096]{1,0:T(8,128)(2,1)} %refs_3_.1) | copy-start | bytes 3145732
  0.7 11.8 %copy-start.7 = (bf16[128,1024]{1,0:T(8,128)(2,1)S(1)}, bf16[128,1024]{1,0:T(8,128)(2,1)}, u32[]{:S(2)}) copy-start(bf16[128,1024]{1,0:T(8,128)(2,1)} %refs_2_.1) | copy-start | bytes 786436
  0.7 11.8 %copy-start.3 = (bf16[2,192,1024]{2,1,0:T(8,128)(2,1)S(1)}, bf16[2,192,1024]{2,1,0:T(8,128)(2,1)}, u32[]{:S(2)}) copy-start(bf16[2,192,1024]{2,1,0:T(8,128)(2,1)} %param.17) | copy-start | bytes 2359300
  0.7 11.8 %copy-start.2 = (bf16[2,192,1024]{2,1,0:T(8,128)(2,1)S(1)}, bf16[2,192,1024]{2,1,0:T(8,128)(2,1)}, u32[]{:S(2)}) copy-start(bf16[2,192,1024]{2,1,0:T(8,128)(2,1)} %param.16) | copy-start | bytes 2359300
  2.9 104.6 %copy-start.12 = (s32[2]{0:T(128)}, s32[2]{0:T(128)S(1)}, u32[]{:S(2)}) copy-start(s32[2]{0:T(128)S(1)} %slice_reduce_fusion.1.refs_0_) | copy-start | bytes 28
  9.8 89.3 %copy-start.4 = (f32[384,128]{1,0:T(8,128)}, f32[384,128]{1,0:T(8,128)S(1)}, u32[]{:S(2)}) copy-start(f32[384,128]{1,0:T(8,128)S(1)} %copy.42.refs_4_.refs_3_) | copy-start | bytes 589828
  11.3 90.5 %copy-start.28 = (s32[2,192]{1,0:T(2,128)S(1)}, s32[2,192]{1,0:T(2,128)}, u32[]{:S(2)}) copy-start(s32[2,192]{1,0:T(2,128)} %param.20) | copy-start | bytes 4612
  12.5 1.1 copy-start.9
  13.6 1.0 copy-start.10
  14.6 88.8 %copy-start.5 = (f32[384,128]{1,0:T(8,128)}, f32[384,128]{1,0:T(8,128)S(1)}, u32[]{:S(2)}) copy-start(f32[384,128]{1,0:T(8,128)S(1)} %copy.41.refs_3_.refs_2_) | copy-start | bytes 589828
  99.1 0.9 copy-start.8
  100.0 0.6 copy-start.13
  103.5 4.0 copy-start.1
  103.5 4.0 copy-start.6
  107.5 85.9 %copy-start.15 = (f32[384,1024]{1,0:T(8,128)S(1)}, f32[384,1024]{1,0:T(8,128)}, u32[]{:S(2)}) copy-start(f32[384,1024]{1,0:T(8,128)} %get-tuple-element.62.refs_5_) | copy-start | bytes 4718596
  192.9 3.6 copy-start.11
  192.9 4.3 slice-start
  193.4 3.8 slice-start.1
  197.2 3.4 copy-start.16
  200.7 9.9 %copy-start.29 = (f32[384,4096]{1,0:T(8,128)}, f32[384,4096]{1,0:T(8,128)S(1)}, u32[]{:S(2)}) copy-start(f32[384,4096]{1,0:T(8,128)S(1)} %fusion.32) | copy-start | bytes 18874372
  210.9 0.9 copy-start.25
  257.6 3.2 copy-start.14
  257.6 2.2 copy-start.17
  259.7 1.2 copy-start.23
  262.7 3.0 copy-start.24
  265.7 2.6 copy-start.30
  375.4 119.5 %copy-start.27 = (f32[2,2,1024]{2,1,0:T(2,128)S(1)}, f32[2,2,1024]{2,1,0:T(2,128)}, u32[]{:S(2)}) copy-start(f32[2,2,1024]{2,1,0:T(2,128)} %param.18) | copy-start | bytes 49156
  494.0 5.0 copy-start.26
  494.0 6.1 %copy-start.22 = (bf16[128,3072]{1,0:T(8,128)(2,1)S(1)}, bf16[128,3072]{1,0:T(8,128)(2,1)}, u32[]{:S(2)}) copy-start(bf16[128,3072]{1,0:T(8,128)(2,1)} %get-tuple-element.86) | copy-start | bytes 2359300
  496.9 4.5 copy-start.21
  499.0 3.9 copy-start.20
  502.9 3.8 copy-start.19
  504.5 3.4 copy-start.18
